TPU v7x, 256 devices: a whole 4x4x8 slice. The times are simulated.
256 devices in a mesh: section: 8 (over y, core), dp: 32 (over x, z).
Axes of the slice: x: 4, y: 4, z: 8, core: 2. Of those that a mesh axis runs over, the one named last changes fastest.
Arguments:
- hidden: bfloat16 [8192, 8192], P('dp'), may hold values from -100 to 100
- cluster: int32 [8192, 1], P('dp'), may hold values from 0 to 7; in each aligned block of 256 rows (0 to 255, 256 to 511, ...) at most 64 rows name the same one
- label: int32 [8192], P('dp'), may hold values from 0 to 16383
- proj: bfloat16 [8, 8192, 1024], P('section', 'dp'), may hold values from -0.0625 to 0.0625
- emb: bfloat16 [8, 1024, 16384], P('section', None, 'dp'), may hold values from -5 to 5
Outputs:
- loss: float32 [8192], P('dp')
Inputs may be any that keep to these rules, and one draw needn't show every extreme that they name: The tokens of one index of dp name each cluster at most 64 times, a bound that some block reaches.
All inputs are finite; a program needn't handle non-finite values.
Results may differ from a plain program's by a relative error of at most 0.0003.
Values may be sent and summed in bfloat16 or wider, within the bound.
No kernel may reach another device: no remote copies, remote signals or barrier semaphores. Data moves between devices by JAX's collectives and lax.ppermute only.
A program may use at most 64 MiB of HBM per device.

v0:
```python
import jax
import jax.numpy as jnp
from jax import lax
from jax.sharding import PartitionSpec as P

CAP = 64


def body(hidden, cluster, label, proj, emb):
    owner = lax.axis_index("section")
    ids = cluster[:, 0]
    mine = ids == owner
    within = jnp.cumsum(mine.astype(jnp.int32)) - 1
    slot_ids = jnp.arange(CAP, dtype=jnp.int32)
    select = (within[None, :] == slot_ids[:, None]) & mine[None, :]
    token_ids = jnp.arange(hidden.shape[0], dtype=jnp.int32)
    token_of = jnp.sum(jnp.where(select, token_ids[None, :], 0), axis=1)
    rows = jnp.take(hidden, token_of, axis=0)
    words = jnp.take(label, token_of, axis=0)
    weight = proj[0]
    table = emb[0]
    columns = rows
    projected = jnp.dot(
        columns,
        lax.all_gather(weight, "dp", axis=0, tiled=True),
        preferred_element_type=jnp.float32,
    )
    all_rows, all_words = (
        lax.all_gather(projected, "dp", axis=0, tiled=True),
        lax.all_gather(words, "dp", axis=0, tiled=True),
    )
    logits = jnp.dot(
        all_rows,
        table.astype(jnp.float32),
        precision=lax.Precision.HIGHEST,
        preferred_element_type=jnp.float32,
    )
    width = table.shape[1]
    local_word = all_words - lax.axis_index("dp") * width
    top = jnp.max(logits, axis=1)
    total = jnp.sum(jnp.exp(logits - top[:, None]), axis=1)
    columns = jnp.arange(width, dtype=jnp.int32)
    chosen = jnp.sum(jnp.where(columns[None, :] == local_word[:, None], logits, 0.0), axis=1)
    top_back, total_back, chosen_back = (
        lax.all_to_all(top, "dp", split_axis=0, concat_axis=0, tiled=True),
        lax.all_to_all(total, "dp", split_axis=0, concat_axis=0, tiled=True),
        lax.all_to_all(chosen, "dp", split_axis=0, concat_axis=0, tiled=True),
    )
    slices = lax.axis_size("dp")
    top_back = top_back.reshape(slices, CAP)
    total_back = total_back.reshape(slices, CAP)
    chosen_back = chosen_back.reshape(slices, CAP)
    highest = jnp.max(top_back, axis=0)
    summed = jnp.sum(total_back * jnp.exp(top_back - highest[None, :]), axis=0)
    slot_loss = highest + jnp.log(summed) - jnp.sum(chosen_back, axis=0)
    token_loss = jnp.sum(jnp.where(select, slot_loss[:, None], 0.0), axis=0)
    return lax.psum(token_loss, "section")


def solution(mesh):
    return jax.shard_map(
        body,
        mesh=mesh,
        in_specs=(
            P("dp", None),
            P("dp", None),
            P("dp"),
            P("section", "dp", None),
            P("section", None, "dp"),
        ),
        out_specs=P("dp"),
        check_vma=False,
    )
```

profile of v0, /device:TPU:1, one launch (start us, length us, event | category | flops | bytes accessed | tf_op | source)
XLA Modules:
  0.0 333.7 jit_solution(6206462634575633070)
XLA Ops:
  6.5 0.7 all-gather.6.cloned.1.call-update
  7.3 0.7 compare_reduce_fusion
  8.0 0.3 reduce-window.9
  8.4 0.1 slice_reduce_fusion
  8.8 4.9 %gather_fusion = bf16[64,8192]{1,0:T(8,128)(2,1)S(1)} fusion(bf16[256,8192]{1,0:T(8,128)(2,1)} %param.5, s32[1024]{0:T(1024)S(1)} %pad_clamp_fusion), kind=kCustom, calls=%fused_computation | custom fusion | bytes 2097408 | tf_op jit(solution)/shard_map/jit(_take)/gather | solution.py:18
  13.7 140.2 %all-gather.6.cloned.1.call-done = bf16[1,8192,1024]{2,1,0:T(8,128)(2,1)} async-done(((bf16[1,256,1024]{2,1,0:T(8,128)(2,1)}), bf16[1,8192,1024]{2,1,0:T(8,128)(2,1)}) %all-gather.6.cloned.1.call-update) | async-done | bytes 16777232 | tf_op jit(solution)/shard_map/all_gather | solution.py:25
  153.9 9.6 %fusion = f32[64,1024]{1,0:T(8,128)} fusion(bf16[1,8192,1024]{2,1,0:T(8,128)(2,1)} %all-gather.6.cloned.1.call-done, bf16[64,8192]{1,0:T(8,128)(2,1)S(1)} %gather_fusion, pred[64]{0:T(512)(128)(4,1)S(1)} %compare_and_fusion), kind=kOutput, calls=%fused_computation.2 | convolution fusion | flops 1074266112 | bytes 18088000 | tf_op jit(solution)/shard_map/dot_general | solution.py:23
  163.6 0.8 gather_fusion.1
  164.4 0.6 dynamic-slice
  165.6 0.1 select_dynamic-update-slice_fusion
  165.7 13.5 %all-reduce = s32[2048]{0:T(1024)S(1)} all-reduce(s32[2048]{0:T(1024)S(1)} %select_dynamic-update-slice_fusion), channel_id=1, replica_groups=mesh['section'=8,'dp'=32] {'dp'}, use_global_device_ids=true, to_apply=%add | all-reduce | flops 2048 | bytes 16384
  179.2 80.0 %all-gather.4.cloned.1.call-done = f32[2048,1024]{1,0:T(8,128)} async-done(((f32[64,1024]{1,0:T(8,128)}), f32[2048,1024]{1,0:T(8,128)}) %all-gather.4.cloned.1.call-update) | async-done | bytes 8388624 | tf_op jit(solution)/shard_map/all_gather | solution.py:29
  259.2 10.6 %fusion.10 = (f32[2048]{0:T(1024)S(1)}, f32[2048,512]{0,1:T(8,128)}) fusion(f32[2048,1024]{1,0:T(8,128)} %all-gather.4.cloned.1.call-done, bf16[1,1024,512]{2,1,0:T(8,128)(2,1)S(1)} %copy-done), kind=kOutput, calls=%fused_computation.30 | convolution fusion | flops 12885948416 | bytes 13639680 | tf_op jit(solution)/shard_map/dot_general | solution.py:32
  269.8 0.7 all_to_all.18
  270.5 5.4 %all-to-all-start = ((f32[32,64,1]{1,2,0:T(1,128)}), f32[32,64,1]{1,2,0:T(1,128)S(1)}, u32[]{:S(2)}, u32[]{:S(2)}) async-start(f32[32,64,1]{1,2,0:T(1,128)} %bitcast.6), calls=%async_computation | async-start | bytes 32768 | tf_op jit(solution)/shard_map/all_to_all | solution.py:45
  275.8 3.3 exponential_reduce_fusion
  279.1 0.7 all_to_all.20
  279.8 4.6 %all-to-all-done = f32[32,64,1]{1,2,0:T(1,128)S(1)} async-done(((f32[32,64,1]{1,2,0:T(1,128)}), f32[32,64,1]{1,2,0:T(1,128)S(1)}, u32[]{:S(2)}, u32[]{:S(2)}) %all-to-all-start) | async-done | bytes 8224 | tf_op jit(solution)/shard_map/all_to_all | solution.py:45
  284.5 4.6 %all-to-all-start.1 = ((f32[32,64,1]{1,2,0:T(1,128)}), f32[32,64,1]{1,2,0:T(1,128)S(1)}, u32[]{:S(2)}, u32[]{:S(2)}) async-start(f32[32,64,1]{1,2,0:T(1,128)} %all_to_all.20), calls=%async_computation.1 | async-start | bytes 32768 | tf_op jit(solution)/shard_map/all_to_all | solution.py:46
  289.1 0.7 all_to_all.22
  289.8 7.9 %all-to-all-done.1 = f32[32,64,1]{1,2,0:T(1,128)S(1)} async-done(((f32[32,64,1]{1,2,0:T(1,128)}), f32[32,64,1]{1,2,0:T(1,128)S(1)}, u32[]{:S(2)}, u32[]{:S(2)}) %all-to-all-start.1) | async-done | bytes 8224 | tf_op jit(solution)/shard_map/all_to_all | solution.py:46
  297.7 3.9 %all-to-all-start.2 = ((f32[32,64,1]{1,2,0:T(1,128)}), f32[32,64,1]{1,2,0:T(1,128)S(1)}, u32[]{:S(2)}, u32[]{:S(2)}) async-start(f32[32,64,1]{1,2,0:T(1,128)} %bitcast.10), calls=%async_computation.2 | async-start | bytes 32768 | tf_op jit(solution)/shard_map/all_to_all | solution.py:47
  301.6 8.6 %all-to-all-done.2 = f32[32,64,1]{1,2,0:T(1,128)S(1)} async-done(((f32[32,64,1]{1,2,0:T(1,128)}), f32[32,64,1]{1,2,0:T(1,128)S(1)}, u32[]{:S(2)}, u32[]{:S(2)}) %all-to-all-start.2) | async-done | bytes 8224 | tf_op jit(solution)/shard_map/all_to_all | solution.py:47
  310.3 16.6 %psum.7 = f32[256]{0:T(256)} all-reduce(f32[256]{0:T(256)S(1)} %select_reduce_fusion.1), channel_id=1, replica_groups=mesh['section'=8,'dp'=32] {'section'}, use_global_device_ids=true, to_apply=%region_10.11 | all-reduce | flops 256 | bytes 2048 | tf_op jit(solution)/shard_map/psum | solution.py:57
  (23 shorter events, 0.6 us)
Async XLA Ops:
  6.5 252.7 %copy-start = (bf16[1,1024,512]{2,1,0:T(8,128)(2,1)S(1)}, bf16[1,1024,512]{2,1,0:T(8,128)(2,1)}, u32[]{:S(2)}) copy-start(bf16[1,1024,512]{2,1,0:T(8,128)(2,1)} %param.9) | copy-start | bytes 3145732
  6.5 147.4 %all-gather.6.cloned.1.call-start = ((), (), s32[]{:S(2)}) async-start(), calls=%async_computation.4 | async-start | bytes 17301504 | tf_op jit(solution)/shard_map/all_gather | solution.py:25
  7.3 251.9 %all-gather.4.cloned.1.call-start = ((), (), s32[]{:S(2)}) async-start(), calls=%async_computation.3 | async-start | bytes 8650752 | tf_op jit(solution)/shard_map/all_gather | solution.py:29
  13.7 149.9 %copy-start.1 = (s32[256]{0:T(256)S(1)}, s32[256]{0:T(256)}, u32[]{:S(2)}) copy-start(s32[256]{0:T(256)} %param.7) | copy-start | bytes 3076
  13.7 150.7 %copy-start.2 = (u32[256]{0:T(256)S(1)}, u32[256]{0:T(256)}, u32[]{:S(2)}) copy-start(u32[256]{0:T(256)} %constant.55) | copy-start | bytes 3076
  270.5 14.0 %all-to-all-start = ((f32[32,64,1]{1,2,0:T(1,128)}), f32[32,64,1]{1,2,0:T(1,128)S(1)}, u32[]{:S(2)}, u32[]{:S(2)}) async-start(f32[32,64,1]{1,2,0:T(1,128)} %bitcast.6), calls=%async_computation | async-start | bytes 32768 | tf_op jit(solution)/shard_map/all_to_all | solution.py:45
  284.5 13.2 %all-to-all-start.1 = ((f32[32,64,1]{1,2,0:T(1,128)}), f32[32,64,1]{1,2,0:T(1,128)S(1)}, u32[]{:S(2)}, u32[]{:S(2)}) async-start(f32[32,64,1]{1,2,0:T(1,128)} %all_to_all.20), calls=%async_computation.1 | async-start | bytes 32768 | tf_op jit(solution)/shard_map/all_to_all | solution.py:46
  297.7 12.5 %all-to-all-start.2 = ((f32[32,64,1]{1,2,0:T(1,128)}), f32[32,64,1]{1,2,0:T(1,128)S(1)}, u32[]{:S(2)}, u32[]{:S(2)}) async-start(f32[32,64,1]{1,2,0:T(1,128)} %bitcast.10), calls=%async_computation.2 | async-start | bytes 32768 | tf_op jit(solution)/shard_map/all_to_all | solution.py:47
Sparse Core Ops, SparseCore 0:
  10.0 143.9 all-gather.5
  163.7 95.4 all-gather.3
where the time goes:
time: 334 us
  waiting for transfers between devices  242 us (72%)
  blocking collectives  30 us (9%)
  matrix products  20.2 us (6%)
  between operations  14.2 us (4%)
  starting transfers between devices  13.8 us (4%)
  local copies, waits for them, and re-layouts  8.48 us (3%)
  other arithmetic  4.91 us (1%)
    all_gather x1, waiting for transfers between devices, body(): lax.all_gather(weight, 'dp', axis=0, tiled=True)  140 us
    all_gather x1, waiting for transfers between devices, body(): lax.all_gather(projected, 'dp', axis=0, tiled=True)  80 us
    psum x1, blocking collectives, body(): return lax.psum(token_loss, 'section')  16.6 us
    unnamed x1, blocking collectives  13.5 us
    dot_general x1, matrix products, body(): jnp.dot(all_rows, table.astype(jnp.float32), precision=lax.Precision.HIGH...  10.6 us
    dot_general x1, matrix products, body(): jnp.dot(columns, lax.all_gather(weight, 'dp', axis=0, tiled=True), prefer...  9.59 us
    all_to_all x1, waiting for transfers between devices, body(): lax.all_to_all(chosen, 'dp', split_axis=0, concat_axis=0, tiled=True)  8.59 us
    all_to_all x1, waiting for transfers between devices, body(): lax.all_to_all(total, 'dp', split_axis=0, concat_axis=0, tiled=True)  7.91 us
  transfers between devices with their start and end apart: 5, of which 5 were waited for; matrix products, arithmetic and copies ran while one was open for 3% of the time, Pallas kernels for 0%

commit v1 on v0

v1 whole, which is shorter than its diff:
```python
import jax
import jax.numpy as jnp
from jax import lax
from jax.experimental import pallas as pl
from jax.experimental.pallas import tpu as pltpu
from jax.sharding import Mesh
from jax.sharding import PartitionSpec as P

CAP = 64
X = 4
Z = 8
BF16 = jnp.bfloat16
F16 = jnp.float16
F32 = jnp.float32
VMEM_LIMIT = 40 * 1024 * 1024


def ring(array, axis, size, step):
    return lax.ppermute(array, axis, [(i, (i + step) % size) for i in range(size)])


def params():
    return pltpu.CompilerParams(vmem_limit_bytes=VMEM_LIMIT)


def cost(flops, moved):
    return pl.CostEstimate(flops=flops, bytes_accessed=moved, transcendentals=0)


def slot_choice(ids, owner):
    tokens = ids.shape[1]
    mine = ids == owner
    ones = jnp.where(mine, 1.0, 0.0).astype(F32)
    earlier = lax.broadcasted_iota(jnp.int32, (tokens, tokens), 0)
    later = lax.broadcasted_iota(jnp.int32, (tokens, tokens), 1)
    upto = jnp.where(earlier <= later, 1.0, 0.0).astype(F32)
    within = jnp.dot(
        jnp.broadcast_to(ones, (8, tokens)), upto, preferred_element_type=F32
    )[0:1, :]
    place = lax.broadcasted_iota(jnp.int32, (CAP, tokens), 0)
    within = (within + 0.5).astype(jnp.int32) - 1
    return (within == place) & mine


def select_kernel(where_ref, ids_ref, label_ref, hidden_ref, *outs):
    pieces, words_ref, choice_ref = outs[:X], outs[X], outs[X + 1]
    owner, z = where_ref[0], where_ref[2]
    step = pl.program_id(0)

    @pl.when(step == 0)
    def _():
        choice = slot_choice(ids_ref[...], owner)
        choice_ref[...] = jnp.where(choice, 1.0, 0.0).astype(BF16)
        word = jnp.sum(jnp.where(choice, label_ref[...], 0), axis=1, keepdims=True)
        lane = lax.broadcasted_iota(jnp.int32, (CAP, 128), 1)
        parts = jnp.where(lane == 0, word >> 7, jnp.where(lane == 1, word & 127, 0))
        words_ref[...] = parts.astype(F32)

    depth = hidden_ref.shape[1] // Z
    for k in range(X):

        @pl.when(step == k)
        def _(k=k):
            for j in range(Z):
                at = pl.multiple_of(lax.rem(z + j, Z) * depth, depth)
                rows = jnp.dot(
                    choice_ref[...],
                    hidden_ref[:, pl.ds(at, depth)],
                    preferred_element_type=F32,
                )
                pieces[k][:, j * depth : (j + 1) * depth] = rows.astype(BF16)


def select_rows(where, ids, label, hidden):
    tokens, width = hidden.shape
    part = width // X
    whole = lambda shape: pl.BlockSpec(shape, lambda k, w: (0, 0))
    return pl.pallas_call(
        select_kernel,
        grid_spec=pltpu.PrefetchScalarGridSpec(
            num_scalar_prefetch=1,
            grid=(X,),
            in_specs=[
                whole((1, tokens)),
                whole((1, tokens)),
                pl.BlockSpec((tokens, part), lambda k, w: (0, lax.rem(w[1] + k, X))),
            ],
            out_specs=[whole((CAP, part))] * X + [whole((CAP, 128))],
            scratch_shapes=[pltpu.VMEM((CAP, tokens), BF16)],
        ),
        out_shape=[jax.ShapeDtypeStruct((CAP, part), BF16)] * X
        + [jax.ShapeDtypeStruct((CAP, 128), F32)],
        compiler_params=params(),
        cost_estimate=cost(2 * CAP * tokens * width, 2 * tokens * width),
    )(where, ids, label, hidden)


def project_first_kernel(offsets, *refs):
    rows, chunks, out = refs[:X], refs[X : X + len(offsets)], refs[-1]
    depth = chunks[0].shape[0]
    left = jnp.concatenate([r[...] for r in rows], axis=0)
    total = None
    for offset, chunk in zip(offsets, chunks):
        term = jnp.dot(
            left[:, offset * depth : (offset + 1) * depth],
            chunk[...],
            preferred_element_type=F32,
        )
        total = term if total is None else total + term
    out[...] = total


def project_first(rows, chunks, offsets):
    depth, wide = chunks[0].shape
    return pl.pallas_call(
        lambda *refs: project_first_kernel(offsets, *refs),
        out_shape=jax.ShapeDtypeStruct((X * CAP, wide), F32),
        compiler_params=params(),
        cost_estimate=cost(2 * X * CAP * depth * len(chunks) * wide, 6_000_000),
    )(*rows, *chunks)


def project_last_kernel(total_ref, *refs):
    rows, front, back, outs = refs[:X], refs[X], refs[X + 1], refs[X + 2 :]
    half = front.shape[0]
    left = jnp.concatenate([r[...] for r in rows], axis=0)
    total = total_ref[...]
    total += jnp.dot(left[:, :half], front[...], preferred_element_type=F32)
    total += jnp.dot(left[:, half:], back[...], preferred_element_type=F32)
    for k in range(X):
        outs[k][...] = total[k * CAP : (k + 1) * CAP, :].astype(outs[k].dtype)


def project_last(total, rows, front, back, held):
    half, wide = front.shape
    depth = 2 * half
    at = lambda *index: lambda i: index
    return pl.pallas_call(
        project_last_kernel,
        grid=(1,),
        in_specs=[pl.BlockSpec(total.shape, at(0, 0))]
        + [pl.BlockSpec((CAP, depth), at(0, Z // 2))] * X
        + [pl.BlockSpec((half, wide), at(0, 0))] * 2,
        out_specs=[pl.BlockSpec((CAP, wide), at(0, 0))] * X,
        out_shape=[jax.ShapeDtypeStruct((CAP, wide), held)] * X,
        compiler_params=params(),
        cost_estimate=cost(2 * X * CAP * depth * wide, 3_000_000),
    )(total, *rows, front, back)


def word_kernel(last, blocks, where_ref, high_ref, low_ref, word_ref, emb_ref, *refs):
    before = refs[0] if last else None
    out_ref, top_ref, sum_ref, hit_ref = refs[1:] if last else refs
    z = where_ref[2]
    part = pl.program_id(0)
    width = emb_ref.shape[2]

    @pl.when(part == 0)
    def _():
        top_ref[...] = jnp.full(top_ref.shape, -jnp.inf, F32)
        sum_ref[...] = jnp.zeros(sum_ref.shape, F32)
        hit_ref[...] = jnp.zeros(hit_ref.shape, F32)

    table = emb_ref[0]
    logits = jnp.dot(high_ref[...], table, preferred_element_type=F32)
    logits += jnp.dot(low_ref[...], table, preferred_element_type=F32)
    codes = word_ref[...]
    word = (codes[:, 0:1] * 128.0 + codes[:, 1:2]).astype(jnp.int32)
    local = word - (part * Z + z) * width
    column = lax.broadcasted_iota(jnp.int32, (logits.shape[0], 128), 1)
    tiles = [logits[:, i * 128 : (i + 1) * 128] for i in range(width // 128)]
    top = top_ref[...]
    best = top
    for tile in tiles:
        best = jnp.maximum(best, tile)
    total = sum_ref[...] * jnp.exp(top - best)
    hit = hit_ref[...]
    for i, tile in enumerate(tiles):
        total += jnp.exp(tile - best)
        hit += jnp.where(column + i * 128 == local, tile, 0.0)
    top_ref[...] = best
    sum_ref[...] = total
    hit_ref[...] = hit

    @pl.when(part == X - 1)
    def _():
        highest = jnp.max(best, axis=1, keepdims=True)
        summed = jnp.sum(total * jnp.exp(best - highest), axis=1, keepdims=True)
        chosen = jnp.sum(hit, axis=1, keepdims=True)
        stats = jnp.where(
            column == 0,
            highest,
            jnp.where(column == 1, summed, jnp.where(column == 2, chosen, 0.0)),
        )
        for i, back in enumerate(blocks):
            rows = stats[i * CAP : (i + 1) * CAP, :]
            turned = jnp.concatenate([rows, rows], axis=0).T[0:8, :]
            if last:
                out_ref[lax.rem(z - back + Z, Z)] = turned
            else:
                out_ref[i] = turned
        if last:
            done = refs[0].shape[0]
            for i, back in enumerate(FIRST[:done]):
                out_ref[lax.rem(z - back + Z, Z)] = before[i]


FIRST = (0, 1, 7, 2, 6)
SECOND = (3, 5, 4)


def word_stats(where, high, low, words, emb, before=None):
    last = before is not None
    blocks = SECOND if last else FIRST
    rows, depth = high.shape
    width = emb.shape[2]
    whole = lambda shape: pl.BlockSpec(shape, lambda k, w: (0,) * len(shape))
    count = Z if last else len(blocks)
    return pl.pallas_call(
        lambda *refs: word_kernel(last, blocks, *refs),
        grid_spec=pltpu.PrefetchScalarGridSpec(
            num_scalar_prefetch=1,
            grid=(X,),
            in_specs=[
                whole((rows, depth)),
                whole((rows, depth)),
                whole((rows, 128)),
                pl.BlockSpec((1, depth, width), lambda k, w: (k, 0, 0)),
            ]
            + ([whole(before.shape)] if last else []),
            out_specs=whole((count, 8, 128)),
            scratch_shapes=[pltpu.VMEM((rows, 128), F32)] * 3,
        ),
        out_shape=jax.ShapeDtypeStruct((count, 8, 128), F32),
        compiler_params=params(),
        cost_estimate=cost(4 * rows * depth * width * X, 2 * depth * width * X),
    )(where, high, low, words, emb, *((before,) if last else ()))


def combine_kernel(where_ref, ids_ref, stats_ref, out_ref):
    stats = stats_ref[...]
    top, total, chosen = stats[:, 0, :], stats[:, 1, :], stats[:, 2, :]
    highest = jnp.max(top, axis=0, keepdims=True)
    summed = jnp.sum(total * jnp.exp(top - highest), axis=0, keepdims=True)
    loss = highest + jnp.log(summed) - jnp.sum(chosen, axis=0, keepdims=True)
    column = jnp.broadcast_to(loss, (128, 128)).T[0:CAP, 0:1]
    choice = slot_choice(ids_ref[...], where_ref[0])
    out_ref[...] = jnp.sum(jnp.where(choice, column, 0.0), axis=0, keepdims=True)


def combine(where, ids, stats):
    tokens = ids.shape[1]
    return pl.pallas_call(
        combine_kernel,
        in_specs=[
            pl.BlockSpec(memory_space=pltpu.SMEM),
            pl.BlockSpec(memory_space=pltpu.VMEM),
            pl.BlockSpec(memory_space=pltpu.VMEM),
        ],
        out_shape=jax.ShapeDtypeStruct((1, tokens), F32),
        compiler_params=params(),
        cost_estimate=cost(2 * 8 * tokens * tokens, 50_000),
    )(where, ids, stats)


def split(blocks, width):
    held = jnp.concatenate(blocks, axis=0)
    wide = held[:, :width].astype(F32)
    high = lax.reduce_precision(wide, exponent_bits=8, mantissa_bits=7)
    return high.astype(BF16), (wide - high).astype(BF16), held[:, width:].astype(F32)


def body(hidden, cluster, label, proj, emb):
    x, z = lax.axis_index("x"), lax.axis_index("z")
    owner = lax.axis_index("y") * 2 + lax.axis_index("core")
    where = jnp.stack([owner, x, z]).astype(jnp.int32)
    ids = cluster.reshape(1, -1)
    weight = proj[0]
    half = weight.shape[0] // 2
    wide = weight.shape[1]

    table = lax.all_gather(emb[0], "x", axis=0)

    *pieces, words = select_rows(where, ids, label.reshape(1, -1), hidden)
    rows = [pieces[0]] + [ring(pieces[k], "x", X, k) for k in range(1, X)]

    chunks, offsets = [weight], [0]
    right = left = weight
    for s in range(1, Z // 2):
        right, left = ring(right, "z", Z, 1), ring(left, "z", Z, -1)
        chunks += [right, left]
        offsets += [Z - s, s]
    front = ring(right[:half], "z", Z, 1)
    back = ring(left[half:], "z", Z, -1)

    total = project_first(rows, chunks, offsets)
    parts = project_last(total, rows, front, back, F32)
    own = parts[0]
    for k in range(1, X):
        own = own + ring(parts[k], "x", X, -k)

    message = jnp.concatenate([own, words], axis=1).astype(F16)
    r1, l1 = ring(message, "z", Z, 1), ring(message, "z", Z, -1)
    r2, l2 = ring(message, "z", Z, 2), ring(message, "z", Z, -2)
    r3, l3 = ring(r2, "z", Z, 1), ring(l2, "z", Z, -1)
    r4 = ring(r2, "z", Z, 2)

    stats = word_stats(where, *split([message, r1, l1, r2, l2], wide), table)
    stats = word_stats(where, *split([r3, l3, r4], wide), table, stats)
    stats = lax.all_to_all(stats, "z", 0, 0, tiled=True)
    loss = combine(where, ids, stats)
    loss = loss + lax.ppermute(loss, "core", [(0, 1), (1, 0)])
    loss = loss + ring(loss, "y", 4, 1) + ring(loss, "y", 4, 2) + ring(loss, "y", 4, 3)
    return loss.reshape(-1)


def solution(mesh):
    fine = Mesh(mesh.devices.reshape(4, 2, X, Z), ("y", "core", "x", "z"))
    return jax.shard_map(
        body,
        mesh=fine,
        in_specs=(
            P(("x", "z"), None),
            P(("x", "z"), None),
            P(("x", "z")),
            P(("y", "core"), ("x", "z"), None),
            P(("y", "core"), None, ("x", "z")),
        ),
        out_specs=P(("x", "z")),
        check_vma=False,
    )
```

time: 334 us -> 152 us (0.46)
  waiting for transfers between devices: 242 us -> 65.8 us
  starting transfers between devices: 13.8 us -> 42.1 us
  matrix products: 20.2 us -> 0 us
  blocking collectives: 30 us -> 9.87 us
  Pallas kernels: 0 us -> 13 us
  other arithmetic: 4.91 us -> 1.17 us
    all_gather x2 -> x1, waiting for transfers between devices: 220 us -> 0.02 us  [body(): table = lax.all_gather(emb[0], 'x', axis=0)]
    ppermute x0 -> x25, waiting for transfers between devices: none -> 65.1 us  [the longest x24 64.3 us: ring(): lax.ppermute(array, axis, [(i, (i + step) % size) for i in range(size)])]
    ppermute x0 -> x25, starting transfers between devices: none -> 42.1 us  [the longest x24 38.1 us: ring(): lax.ppermute(array, axis, [(i, (i + step) % size) for i in range(size)])]
    all_to_all x3 -> x0, waiting for transfers between devices: 21.1 us -> none  [the longest x1 8.59 us: body(): lax.all_to_all(chosen, 'dp', split_axis=0, concat_axis=0, tiled=True)]
    dot_general x2 -> x0, matrix products: 20.2 us -> none  [the longest x1 10.6 us: body(): jnp.dot(all_rows, table.astype(jnp.float32), precision=lax.Precision.HIGH...]
    psum x1 -> x0, blocking collectives: 16.6 us -> none  [body(): return lax.psum(token_loss, 'section')]
    all_to_all x3 -> x0, starting transfers between devices: 13.8 us -> none  [the longest x1 5.36 us: body(): lax.all_to_all(top, 'dp', split_axis=0, concat_axis=0, tiled=True)]
    unnamed x1 -> x0, blocking collectives: 13.5 us -> none
  transfers between devices with their start and end apart: 5 -> 26, of which waited for: 5 -> 15; matrix products, arithmetic and copies ran while one was open for 3% -> 1% of each run, Pallas kernels for 0% -> 3%
where the time goes in v1:
time: 152 us
  waiting for transfers between devices  65.8 us (43%)
  starting transfers between devices  42.1 us (28%)
  between operations  13.6 us (9%)
  Pallas kernels  13 us (9%)
  blocking collectives  9.87 us (6%)
  local copies, waits for them, and re-layouts  6.09 us (4%)
    ppermute x24, waiting for transfers between devices, ring(): lax.ppermute(array, axis, [(i, (i + step) % size) for i in range(size)])  64.3 us
    ppermute x24, starting transfers between devices, ring(): lax.ppermute(array, axis, [(i, (i + step) % size) for i in range(size)])  38.1 us
    all_to_all x1, blocking collectives, body(): stats = lax.all_to_all(stats, 'z', 0, 0, tiled=True)  9.87 us
    pallas_call x2, Pallas kernels, word_stats(): pl.pallas_call(lambda *refs: word_kernel(last, blocks, *refs), grid_spec=...  8.32 us
    unnamed x17, local copies, waits for them, and re-layouts  5.98 us
    ppermute x1, starting transfers between devices, body(): loss = loss + lax.ppermute(loss, 'core', [(0, 1), (1, 0)])  3.95 us
  transfers between devices with their start and end apart: 26, of which 15 were waited for; matrix products, arithmetic and copies ran while one was open for 1% of the time, Pallas kernels for 3%

profile of v1, /device:TPU:1, one launch (start us, length us, event | category | flops | bytes accessed | tf_op | source)
XLA Modules:
  0.0 151.5 jit_solution(17628304786758784757)
XLA Ops:
  7.3 6.5 %collective-permute-start.4 = (bf16[256,1024]{1,0:T(8,128)(2,1)}, bf16[256,1024]{1,0:T(8,128)(2,1)S(1)}, u32[]{:S(2)}, u32[]{:S(2)}) collective-permute-start(bf16[256,1024]{1,0:T(8,128)(2,1)} %bitcast.7), channel_id=1, source_target_pairs={{0,7},{1,0},{2,1},{3,2},{4,3},{5,4},{6,5},{7,6},{8,15},{9,8},{10,9... | collective-permute-start | bytes 1572872 | tf_op jit(solution)/shard_map/ppermute | solution.py:19
  13.7 10.9 %collective-permute-done.4.refs_6_ = bf16[256,1024]{1,0:T(8,128)(2,1)S(1)} collective-permute-done((bf16[256,1024]{1,0:T(8,128)(2,1)}, bf16[256,1024]{1,0:T(8,128)(2,1)S(1)}, u32[]{:S(2)}, u32[]{:S(2)}) %collective-permute-start.4) | collective-permute-done | bytes 524320 | tf_op jit(solution)/shard_map/ppermute | solution.py:19
  24.6 3.3 %collective-permute-start.6 = (bf16[256,1024]{1,0:T(8,128)(2,1)S(1)}, bf16[256,1024]{1,0:T(8,128)(2,1)S(1)}, u32[]{:S(2)}, u32[]{:S(2)}) collective-permute-start(bf16[256,1024]{1,0:T(8,128)(2,1)S(1)} %collective-permute-done.4.refs_6_), channel_id=1, source_target_pairs={{0,7},{1,0},{2,1},{3,2},{4,3},{5,4},{6,5},{7,6},{8,15},{9,8},{10,9... | collective-permute-start | bytes 1572872 | tf_op jit(solution)/shard_map/ppermute | solution.py:19
  28.0 9.7 %collective-permute-done.6.refs_8_ = bf16[256,1024]{1,0:T(8,128)(2,1)S(1)} collective-permute-done((bf16[256,1024]{1,0:T(8,128)(2,1)S(1)}, bf16[256,1024]{1,0:T(8,128)(2,1)S(1)}, u32[]{:S(2)}, u32[]{:S(2)}) %collective-permute-start.6) | collective-permute-done | bytes 524320 | tf_op jit(solution)/shard_map/ppermute | solution.py:19
  37.6 3.5 %collective-permute-start.8 = (bf16[256,1024]{1,0:T(8,128)(2,1)S(1)}, bf16[256,1024]{1,0:T(8,128)(2,1)S(1)}, u32[]{:S(2)}, u32[]{:S(2)}) collective-permute-start(bf16[256,1024]{1,0:T(8,128)(2,1)S(1)} %collective-permute-done.6.refs_8_), channel_id=1, source_target_pairs={{0,7},{1,0},{2,1},{3,2},{4,3},{5,4},{6,5},{7,6},{8,15},{9,8},{10,9... | collective-permute-start | bytes 1572872 | tf_op jit(solution)/shard_map/ppermute | solution.py:19
  41.2 2.3 %copy-done = bf16[256,8192]{1,0:T(8,128)(2,1)S(1)} copy-done((bf16[256,8192]{1,0:T(8,128)(2,1)S(1)}, bf16[256,8192]{1,0:T(8,128)(2,1)}, u32[]{:S(2)}) %copy-start) | copy-done | bytes 4194328
  44.8 2.4 %shard_map.55 = (bf16[64,2048]{1,0:T(8,128)(2,1)S(1)}, bf16[64,2048]{1,0:T(8,128)(2,1)S(1)}, bf16[64,2048]{1,0:T(8,128)(2,1)S(1)}, bf16[64,2048]{1,0:T(8,128)(2,1)S(1)}, f32[64,128]{1,0:T(8,128)S(1)}) custom-call(s32[3]{0:T(128)S(1)} %pad_add_fusion.where_ref.refs_0_, s32[1,256]{1,0:T(1,128)S(1)} %bitcast.10, s32[1,256]{1,0:T(1,128)S(1)} %bitcast.12, ...), custom_call_target="tpu_custom_call" | custom-call | flops 268435456 | bytes 4194304 | tf_op jit(solution)/shard_map/pallas_call | solution.py:78
  48.4 2.5 %collective-permute-start.1 = (bf16[64,2048]{1,0:T(8,128)(2,1)S(1)}, bf16[64,2048]{1,0:T(8,128)(2,1)S(1)}, u32[]{:S(2)}, u32[]{:S(2)}) collective-permute-start(bf16[64,2048]{1,0:T(8,128)(2,1)S(1)} %get-tuple-element.16), channel_id=1, source_target_pairs={{0,16},{8,24},{16,0},{24,8},{1,17},{9,25},{17,1},{25,9},{2,18},{10... | collective-permute-start | bytes 786440 | tf_op jit(solution)/shard_map/ppermute | solution.py:19
  52.0 2.8 %collective-permute-start.10 = (bf16[128,1024]{1,0:T(8,128)(2,1)S(1)}, bf16[128,1024]{1,0:T(8,128)(2,1)S(1)}, u32[]{:S(2)}, u32[]{:S(2)}) collective-permute-start(bf16[128,1024]{1,0:T(8,128)(2,1)S(1)} %slice.25), channel_id=1, source_target_pairs={{0,7},{1,0},{2,1},{3,2},{4,3},{5,4},{6,5},{7,6},{8,15},{9,8},{10,9... | collective-permute-start | bytes 786440 | tf_op jit(solution)/shard_map/ppermute | solution.py:19
  54.9 6.6 %collective-permute-done.refs_1_ = bf16[64,2048]{1,0:T(8,128)(2,1)S(1)} collective-permute-done((bf16[64,2048]{1,0:T(8,128)(2,1)S(1)}, bf16[64,2048]{1,0:T(8,128)(2,1)S(1)}, u32[]{:S(2)}, u32[]{:S(2)}) %collective-permute-start) | collective-permute-done | bytes 262176 | tf_op jit(solution)/shard_map/ppermute | solution.py:19
  61.5 12.0 %collective-permute-done.1.refs_2_ = bf16[64,2048]{1,0:T(8,128)(2,1)S(1)} collective-permute-done((bf16[64,2048]{1,0:T(8,128)(2,1)S(1)}, bf16[64,2048]{1,0:T(8,128)(2,1)S(1)}, u32[]{:S(2)}, u32[]{:S(2)}) %collective-permute-start.1) | collective-permute-done | bytes 262176 | tf_op jit(solution)/shard_map/ppermute | solution.py:19
  75.2 2.1 %collective-permute-start.12 = (f32[64,1024]{1,0:T(8,128)S(1)}, f32[64,1024]{1,0:T(8,128)S(1)}, u32[]{:S(2)}, u32[]{:S(2)}) collective-permute-start(f32[64,1024]{1,0:T(8,128)S(1)} %get-tuple-element.20), channel_id=1, source_target_pairs={{0,16},{8,24},{16,0},{24,8},{1,17},{9,25},{17,1},{25,9},{2,18},{10... | collective-permute-start | bytes 786440 | tf_op jit(solution)/shard_map/ppermute | solution.py:19
  78.1 2.8 %collective-permute-done.11 = f32[64,1024]{1,0:T(8,128)S(1)} collective-permute-done((f32[64,1024]{1,0:T(8,128)S(1)}, f32[64,1024]{1,0:T(8,128)S(1)}, u32[]{:S(2)}, u32[]{:S(2)}) %collective-permute-start.11) | collective-permute-done | bytes 262176 | tf_op jit(solution)/shard_map/ppermute | solution.py:19
  82.6 7.6 %collective-permute-done.13 = f32[64,1024]{1,0:T(8,128)S(1)} collective-permute-done((f32[64,1024]{1,0:T(8,128)S(1)}, f32[64,1024]{1,0:T(8,128)S(1)}, u32[]{:S(2)}, u32[]{:S(2)}) %collective-permute-start.13) | collective-permute-done | bytes 262176 | tf_op jit(solution)/shard_map/ppermute | solution.py:19
  90.4 3.6 %collective-permute-start.16 = (f16[64,1152]{1,0:T(8,128)(2,1)S(1)}, f16[64,1152]{1,0:T(8,128)(2,1)S(1)}, u32[]{:S(2)}, u32[]{:S(2)}) collective-permute-start(f16[64,1152]{1,0:T(8,128)(2,1)S(1)} %get-tuple-element.28), channel_id=1, source_target_pairs={{0,6},{1,7},{2,0},{3,1},{4,2},{5,3},{6,4},{7,5},{8,14},{9,15},{10,... | collective-permute-start | bytes 442376 | tf_op jit(solution)/shard_map/ppermute | solution.py:19
  94.0 2.6 %collective-permute-start.20 = (f16[64,1152]{1,0:T(8,128)(2,1)S(1)}, f16[64,1152]{1,0:T(8,128)(2,1)S(1)}, u32[]{:S(2)}, u32[]{:S(2)}) collective-permute-start(f16[64,1152]{1,0:T(8,128)(2,1)S(1)} %get-tuple-element.28), channel_id=1, source_target_pairs={{0,7},{1,0},{2,1},{3,2},{4,3},{5,4},{6,5},{7,6},{8,15},{9,8},{10,9... | collective-permute-start | bytes 442376 | tf_op jit(solution)/shard_map/ppermute | solution.py:19
  96.7 3.1 %collective-permute-done.14 = f16[64,1152]{1,0:T(8,128)(2,1)S(1)} collective-permute-done((f16[64,1152]{1,0:T(8,128)(2,1)S(1)}, f16[64,1152]{1,0:T(8,128)(2,1)S(1)}, u32[]{:S(2)}, u32[]{:S(2)}) %collective-permute-start.14) | collective-permute-done | bytes 147488 | tf_op jit(solution)/shard_map/ppermute | solution.py:19
  105.4 5.9 %collective-permute-done.18 = f16[64,1152]{1,0:T(8,128)(2,1)S(1)} collective-permute-done((f16[64,1152]{1,0:T(8,128)(2,1)S(1)}, f16[64,1152]{1,0:T(8,128)(2,1)S(1)}, u32[]{:S(2)}, u32[]{:S(2)}) %collective-permute-start.18) | collective-permute-done | bytes 147488 | tf_op jit(solution)/shard_map/ppermute | solution.py:19
  111.5 2.2 %copy-done.5 = bf16[4,1024,512]{2,1,0:T(8,128)(2,1)S(1)} copy-done((bf16[4,1024,512]{2,1,0:T(8,128)(2,1)S(1)}, bf16[4,1024,512]{2,1,0:T(8,128)(2,1)}, u32[]{:S(2)}) %copy-start.5) | copy-done | bytes 4194328
  113.7 4.8 %shard_map.58.refs_5_ = f32[5,8,128]{2,1,0:T(8,128)S(1)} custom-call(s32[3]{0:T(128)S(1)} %pad_add_fusion.where_ref.refs_0_, bf16[320,1024]{1,0:T(8,128)(2,1)S(1)} %get-tuple-element.24.refs_1_, bf16[320,1024]{1,0:T(8,128)(2,1)S(1)} %get-tuple-element.23.refs_2_, f32[320,128]{1,0:T(8,128)S(1)} %slice_convert_fusion.refs_3_, bf16[4,1024,512]{2,1,0:T(8,128)(2,1)S(1)} %copy-done.5), custom_call_target="tpu_custom_call" | custom-call | flops 2684354560 | bytes 4194304 | tf_op jit(solution)/shard_map/pallas_call | solution.py:219
  118.5 3.5 %shard_map.59 = f32[8,8,128]{2,1,0:T(8,128)S(1)} custom-call(s32[3]{0:T(128)S(1)} %pad_add_fusion.where_ref.refs_0_, bf16[192,1024]{1,0:T(8,128)(2,1)S(1)} %get-tuple-element.26.refs_1_, bf16[192,1024]{1,0:T(8,128)(2,1)S(1)} %get-tuple-element.25.refs_2_, f32[192,128]{1,0:T(8,128)S(1)} %slice_convert_fusion.1.refs_3_, bf16[4,1024,512]{2,1,0:T(8,128)(2,1)S(1)} %copy-done.5, ...), custom_call_target="tpu_custom_call" | custom-call | flops 1610612736 | bytes 4194304 | tf_op jit(solution)/shard_map/pallas_call | solution.py:219
  122.1 9.9 %all_to_all.5.stats_ref = f32[8,8,128]{2,1,0:T(8,128)S(1)} all-to-all(f32[8,8,128]{2,1,0:T(8,128)S(1)} %shard_map.59), channel_id=1, replica_groups=mesh['y'=4,'core'=2,'x'=4,'z'=8] {'z'}, dimensions={0} | all-to-all | bytes 65536 | tf_op jit(solution)/shard_map/all_to_all | solution.py:310
  132.7 3.9 %collective-permute-start.21 = (f32[1,256]{1,0:T(1,128)S(1)}, f32[1,256]{1,0:T(1,128)S(1)}, u32[]{:S(2)}, u32[]{:S(2)}) collective-permute-start(f32[1,256]{1,0:T(1,128)S(1)} %shard_map.60), channel_id=1, source_target_pairs={{0,32},{32,0},{1,33},{33,1},{2,34},{34,2},{3,35},{35,3},{4,36},{36... | collective-permute-start | bytes 3080 | tf_op jit(solution)/shard_map/ppermute | solution.py:312
  138.8 2.9 %collective-permute-start.23 = (f32[1,256]{1,0:T(1,128)S(1)}, f32[1,256]{1,0:T(1,128)S(1)}, u32[]{:S(2)}, u32[]{:S(2)}) collective-permute-start(f32[1,256]{1,0:T(1,128)S(1)} %add.28), channel_id=1, source_target_pairs={{0,128},{64,192},{128,0},{192,64},{1,129},{65,193},{129,1},{193,65... | collective-permute-start | bytes 3080 | tf_op jit(solution)/shard_map/ppermute | solution.py:19
  (67 shorter events, 20.5 us)
Async XLA Ops:
  6.5 105.0 %all-gather.2.cloned.1.call-start = ((), (), s32[]{:S(2)}) async-start(), calls=%async_computation.1 | async-start | bytes 5242880 | tf_op jit(solution)/shard_map/all_gather | solution.py:282
  7.3 17.4 %collective-permute-start.4 = (bf16[256,1024]{1,0:T(8,128)(2,1)}, bf16[256,1024]{1,0:T(8,128)(2,1)S(1)}, u32[]{:S(2)}, u32[]{:S(2)}) collective-permute-start(bf16[256,1024]{1,0:T(8,128)(2,1)} %bitcast.7), channel_id=1, source_target_pairs={{0,7},{1,0},{2,1},{3,2},{4,3},{5,4},{6,5},{7,6},{8,15},{9,8},{10,9... | collective-permute-start | bytes 1572872 | tf_op jit(solution)/shard_map/ppermute | solution.py:19
  13.7 14.2 %collective-permute-start.3 = (bf16[256,1024]{1,0:T(8,128)(2,1)}, bf16[256,1024]{1,0:T(8,128)(2,1)S(1)}, u32[]{:S(2)}, u32[]{:S(2)}) collective-permute-start(bf16[256,1024]{1,0:T(8,128)(2,1)} %bitcast.8), channel_id=1, source_target_pairs={{0,1},{1,2},{2,3},{3,4},{4,5},{5,6},{6,7},{7,0},{8,9},{9,10},{10,1... | collective-permute-start | bytes 1572872 | tf_op jit(solution)/shard_map/ppermute | solution.py:19
  24.6 13.0 %collective-permute-start.6 = (bf16[256,1024]{1,0:T(8,128)(2,1)S(1)}, bf16[256,1024]{1,0:T(8,128)(2,1)S(1)}, u32[]{:S(2)}, u32[]{:S(2)}) collective-permute-start(bf16[256,1024]{1,0:T(8,128)(2,1)S(1)} %collective-permute-done.4.refs_6_), channel_id=1, source_target_pairs={{0,7},{1,0},{2,1},{3,2},{4,3},{5,4},{6,5},{7,6},{8,15},{9,8},{10,9... | collective-permute-start | bytes 1572872 | tf_op jit(solution)/shard_map/ppermute | solution.py:19
  28.0 13.2 %collective-permute-start.5 = (bf16[256,1024]{1,0:T(8,128)(2,1)S(1)}, bf16[256,1024]{1,0:T(8,128)(2,1)S(1)}, u32[]{:S(2)}, u32[]{:S(2)}) collective-permute-start(bf16[256,1024]{1,0:T(8,128)(2,1)S(1)} %collective-permute-done.3.refs_5_), channel_id=1, source_target_pairs={{0,1},{1,2},{2,3},{3,4},{4,5},{5,6},{6,7},{7,0},{8,9},{9,10},{10,1... | collective-permute-start | bytes 1572872 | tf_op jit(solution)/shard_map/ppermute | solution.py:19
  37.6 14.4 %collective-permute-start.8 = (bf16[256,1024]{1,0:T(8,128)(2,1)S(1)}, bf16[256,1024]{1,0:T(8,128)(2,1)S(1)}, u32[]{:S(2)}, u32[]{:S(2)}) collective-permute-start(bf16[256,1024]{1,0:T(8,128)(2,1)S(1)} %collective-permute-done.6.refs_8_), channel_id=1, source_target_pairs={{0,7},{1,0},{2,1},{3,2},{4,3},{5,4},{6,5},{7,6},{8,15},{9,8},{10,9... | collective-permute-start | bytes 1572872 | tf_op jit(solution)/shard_map/ppermute | solution.py:19
  41.1 13.6 %collective-permute-start.7 = (bf16[256,1024]{1,0:T(8,128)(2,1)S(1)}, bf16[256,1024]{1,0:T(8,128)(2,1)S(1)}, u32[]{:S(2)}, u32[]{:S(2)}) collective-permute-start(bf16[256,1024]{1,0:T(8,128)(2,1)S(1)} %collective-permute-done.5.refs_7_), channel_id=1, source_target_pairs={{0,1},{1,2},{2,3},{3,4},{4,5},{5,6},{6,7},{7,0},{8,9},{9,10},{10,1... | collective-permute-start | bytes 1572872 | tf_op jit(solution)/shard_map/ppermute | solution.py:19
  47.2 14.3 %collective-permute-start = (bf16[64,2048]{1,0:T(8,128)(2,1)S(1)}, bf16[64,2048]{1,0:T(8,128)(2,1)S(1)}, u32[]{:S(2)}, u32[]{:S(2)}) collective-permute-start(bf16[64,2048]{1,0:T(8,128)(2,1)S(1)} %get-tuple-element.15), channel_id=1, source_target_pairs={{0,8},{8,16},{16,24},{24,0},{1,9},{9,17},{17,25},{25,1},{2,10},{10... | collective-permute-start | bytes 786440 | tf_op jit(solution)/shard_map/ppermute | solution.py:19
  48.4 25.1 %collective-permute-start.1 = (bf16[64,2048]{1,0:T(8,128)(2,1)S(1)}, bf16[64,2048]{1,0:T(8,128)(2,1)S(1)}, u32[]{:S(2)}, u32[]{:S(2)}) collective-permute-start(bf16[64,2048]{1,0:T(8,128)(2,1)S(1)} %get-tuple-element.16), channel_id=1, source_target_pairs={{0,16},{8,24},{16,0},{24,8},{1,17},{9,25},{17,1},{25,9},{2,18},{10... | collective-permute-start | bytes 786440 | tf_op jit(solution)/shard_map/ppermute | solution.py:19
  50.9 22.6 %collective-permute-start.2 = (bf16[64,2048]{1,0:T(8,128)(2,1)S(1)}, bf16[64,2048]{1,0:T(8,128)(2,1)S(1)}, u32[]{:S(2)}, u32[]{:S(2)}) collective-permute-start(bf16[64,2048]{1,0:T(8,128)(2,1)S(1)} %get-tuple-element.17), channel_id=1, source_target_pairs={{0,24},{8,0},{16,8},{24,16},{1,25},{9,1},{17,9},{25,17},{2,26},{10... | collective-permute-start | bytes 786440 | tf_op jit(solution)/shard_map/ppermute | solution.py:19
  52.0 22.7 %collective-permute-start.10 = (bf16[128,1024]{1,0:T(8,128)(2,1)S(1)}, bf16[128,1024]{1,0:T(8,128)(2,1)S(1)}, u32[]{:S(2)}, u32[]{:S(2)}) collective-permute-start(bf16[128,1024]{1,0:T(8,128)(2,1)S(1)} %slice.25), channel_id=1, source_target_pairs={{0,7},{1,0},{2,1},{3,2},{4,3},{5,4},{6,5},{7,6},{8,15},{9,8},{10,9... | collective-permute-start | bytes 786440 | tf_op jit(solution)/shard_map/ppermute | solution.py:19
  54.8 19.9 %collective-permute-start.9 = (bf16[128,1024]{1,0:T(8,128)(2,1)S(1)}, bf16[128,1024]{1,0:T(8,128)(2,1)S(1)}, u32[]{:S(2)}, u32[]{:S(2)}) collective-permute-start(bf16[128,1024]{1,0:T(8,128)(2,1)S(1)} %slice.24), channel_id=1, source_target_pairs={{0,1},{1,2},{2,3},{3,4},{4,5},{5,6},{6,7},{7,0},{8,9},{9,10},{10,1... | collective-permute-start | bytes 786440 | tf_op jit(solution)/shard_map/ppermute | solution.py:19
  75.1 5.8 %collective-permute-start.11 = (f32[64,1024]{1,0:T(8,128)S(1)}, f32[64,1024]{1,0:T(8,128)S(1)}, u32[]{:S(2)}, u32[]{:S(2)}) collective-permute-start(f32[64,1024]{1,0:T(8,128)S(1)} %get-tuple-element.19), channel_id=1, source_target_pairs={{0,24},{8,0},{16,8},{24,16},{1,25},{9,1},{17,9},{25,17},{2,26},{10... | collective-permute-start | bytes 786440 | tf_op jit(solution)/shard_map/ppermute | solution.py:19
  75.2 7.3 %collective-permute-start.12 = (f32[64,1024]{1,0:T(8,128)S(1)}, f32[64,1024]{1,0:T(8,128)S(1)}, u32[]{:S(2)}, u32[]{:S(2)}) collective-permute-start(f32[64,1024]{1,0:T(8,128)S(1)} %get-tuple-element.20), channel_id=1, source_target_pairs={{0,16},{8,24},{16,0},{24,8},{1,17},{9,25},{17,1},{25,9},{2,18},{10... | collective-permute-start | bytes 786440 | tf_op jit(solution)/shard_map/ppermute | solution.py:19
  77.4 12.9 %collective-permute-start.13 = (f32[64,1024]{1,0:T(8,128)S(1)}, f32[64,1024]{1,0:T(8,128)S(1)}, u32[]{:S(2)}, u32[]{:S(2)}) collective-permute-start(f32[64,1024]{1,0:T(8,128)S(1)} %get-tuple-element.21), channel_id=1, source_target_pairs={{0,8},{8,16},{16,24},{24,0},{1,9},{9,17},{17,25},{25,1},{2,10},{10... | collective-permute-start | bytes 786440 | tf_op jit(solution)/shard_map/ppermute | solution.py:19
  90.3 9.4 %collective-permute-start.14 = (f16[64,1152]{1,0:T(8,128)(2,1)S(1)}, f16[64,1152]{1,0:T(8,128)(2,1)S(1)}, u32[]{:S(2)}, u32[]{:S(2)}) collective-permute-start(f16[64,1152]{1,0:T(8,128)(2,1)S(1)} %get-tuple-element.28), channel_id=1, source_target_pairs={{0,2},{1,3},{2,4},{3,5},{4,6},{5,7},{6,0},{7,1},{8,10},{9,11},{10,... | collective-permute-start | bytes 442376 | tf_op jit(solution)/shard_map/ppermute | solution.py:19
  90.4 10.2 %collective-permute-start.16 = (f16[64,1152]{1,0:T(8,128)(2,1)S(1)}, f16[64,1152]{1,0:T(8,128)(2,1)S(1)}, u32[]{:S(2)}, u32[]{:S(2)}) collective-permute-start(f16[64,1152]{1,0:T(8,128)(2,1)S(1)} %get-tuple-element.28), channel_id=1, source_target_pairs={{0,6},{1,7},{2,0},{3,1},{4,2},{5,3},{6,4},{7,5},{8,14},{9,15},{10,... | collective-permute-start | bytes 442376 | tf_op jit(solution)/shard_map/ppermute | solution.py:19
  94.0 8.9 %collective-permute-start.19 = (f16[64,1152]{1,0:T(8,128)(2,1)S(1)}, f16[64,1152]{1,0:T(8,128)(2,1)S(1)}, u32[]{:S(2)}, u32[]{:S(2)}) collective-permute-start(f16[64,1152]{1,0:T(8,128)(2,1)S(1)} %get-tuple-element.28), channel_id=1, source_target_pairs={{0,1},{1,2},{2,3},{3,4},{4,5},{5,6},{6,7},{7,0},{8,9},{9,10},{10,1... | collective-permute-start | bytes 442376 | tf_op jit(solution)/shard_map/ppermute | solution.py:19
  94.0 9.2 %collective-permute-start.20 = (f16[64,1152]{1,0:T(8,128)(2,1)S(1)}, f16[64,1152]{1,0:T(8,128)(2,1)S(1)}, u32[]{:S(2)}, u32[]{:S(2)}) collective-permute-start(f16[64,1152]{1,0:T(8,128)(2,1)S(1)} %get-tuple-element.28), channel_id=1, source_target_pairs={{0,7},{1,0},{2,1},{3,2},{4,3},{5,4},{6,5},{7,6},{8,15},{9,8},{10,9... | collective-permute-start | bytes 442376 | tf_op jit(solution)/shard_map/ppermute | solution.py:19
  99.7 5.2 %collective-permute-start.15 = (f16[64,1152]{1,0:T(8,128)(2,1)S(1)}, f16[64,1152]{1,0:T(8,128)(2,1)S(1)}, u32[]{:S(2)}, u32[]{:S(2)}) collective-permute-start(f16[64,1152]{1,0:T(8,128)(2,1)S(1)} %collective-permute-done.14), channel_id=1, source_target_pairs={{0,1},{1,2},{2,3},{3,4},{4,5},{5,6},{6,7},{7,0},{8,9},{9,10},{10,1... | collective-permute-start | bytes 442376 | tf_op jit(solution)/shard_map/ppermute | solution.py:19
  99.7 11.6 %collective-permute-start.18 = (f16[64,1152]{1,0:T(8,128)(2,1)S(1)}, f16[64,1152]{1,0:T(8,128)(2,1)S(1)}, u32[]{:S(2)}, u32[]{:S(2)}) collective-permute-start(f16[64,1152]{1,0:T(8,128)(2,1)S(1)} %collective-permute-done.14), channel_id=1, source_target_pairs={{0,2},{1,3},{2,4},{3,5},{4,6},{5,7},{6,0},{7,1},{8,10},{9,11},{10,... | collective-permute-start | bytes 442376 | tf_op jit(solution)/shard_map/ppermute | solution.py:19
  100.6 4.8 %collective-permute-start.17 = (f16[64,1152]{1,0:T(8,128)(2,1)S(1)}, f16[64,1152]{1,0:T(8,128)(2,1)S(1)}, u32[]{:S(2)}, u32[]{:S(2)}) collective-permute-start(f16[64,1152]{1,0:T(8,128)(2,1)S(1)} %collective-permute-done.16), channel_id=1, source_target_pairs={{0,7},{1,0},{2,1},{3,2},{4,3},{5,4},{6,5},{7,6},{8,15},{9,8},{10,9... | collective-permute-start | bytes 442376 | tf_op jit(solution)/shard_map/ppermute | solution.py:19
  132.7 4.8 %collective-permute-start.21 = (f32[1,256]{1,0:T(1,128)S(1)}, f32[1,256]{1,0:T(1,128)S(1)}, u32[]{:S(2)}, u32[]{:S(2)}) collective-permute-start(f32[1,256]{1,0:T(1,128)S(1)} %shard_map.60), channel_id=1, source_target_pairs={{0,32},{32,0},{1,33},{33,1},{2,34},{34,2},{3,35},{35,3},{4,36},{36... | collective-permute-start | bytes 3080 | tf_op jit(solution)/shard_map/ppermute | solution.py:312
  137.4 5.2 %collective-permute-start.22 = (f32[1,256]{1,0:T(1,128)S(1)}, f32[1,256]{1,0:T(1,128)S(1)}, u32[]{:S(2)}, u32[]{:S(2)}) collective-permute-start(f32[1,256]{1,0:T(1,128)S(1)} %add.28), channel_id=1, source_target_pairs={{0,64},{64,128},{128,192},{192,0},{1,65},{65,129},{129,193},{193,1... | collective-permute-start | bytes 3080 | tf_op jit(solution)/shard_map/ppermute | solution.py:19
  (8 other events, 51.9 us)
Sparse Core Ops, SparseCore 0:
  9.2 64.8 all-gather.1

commit v2 on v1

v2 whole, which is shorter than its diff:
```python
import jax
import jax.numpy as jnp
from jax import lax
from jax.experimental import pallas as pl
from jax.experimental.pallas import tpu as pltpu
from jax.sharding import Mesh
from jax.sharding import PartitionSpec as P

CAP = 64
X = 4
Z = 8
SECTIONS = 8
BF16 = jnp.bfloat16
F16 = jnp.float16
F32 = jnp.float32
VMEM_LIMIT = 40 * 1024 * 1024


def ring(array, axis, size, step):
    return lax.ppermute(array, axis, [(i, (i + step) % size) for i in range(size)])


def params():
    return pltpu.CompilerParams(vmem_limit_bytes=VMEM_LIMIT)


def cost(flops, moved):
    return pl.CostEstimate(flops=flops, bytes_accessed=moved, transcendentals=0)


def slot_choice(ids, owner):
    tokens = ids.shape[1]
    mine = ids == owner
    ones = jnp.where(mine, 1.0, 0.0).astype(F32)
    earlier = lax.broadcasted_iota(jnp.int32, (tokens, tokens), 0)
    later = lax.broadcasted_iota(jnp.int32, (tokens, tokens), 1)
    upto = jnp.where(earlier <= later, 1.0, 0.0).astype(F32)
    within = jnp.dot(
        jnp.broadcast_to(ones, (8, tokens)), upto, preferred_element_type=F32
    )[0:1, :]
    place = lax.broadcasted_iota(jnp.int32, (CAP, tokens), 0)
    within = (within + 0.5).astype(jnp.int32) - 1
    return (within == place) & mine


def select_kernel(
    where_ref, ids_ref, label_ref, hidden_ref, own_ref, up_ref, down_ref, words_ref, choice_ref
):
    owner, z = where_ref[0], where_ref[2]
    step = pl.program_id(0)

    @pl.when(step == 0)
    def _():
        choice = slot_choice(ids_ref[...], owner)
        choice_ref[...] = jnp.where(choice, 1.0, 0.0).astype(BF16)
        word = jnp.sum(jnp.where(choice, label_ref[...], 0), axis=1, keepdims=True)
        lane = lax.broadcasted_iota(jnp.int32, (CAP, 128), 1)
        parts = jnp.where(lane == 0, word >> 7, jnp.where(lane == 1, word & 127, 0))
        words_ref[...] = parts.astype(F32)

    part = hidden_ref.shape[1]
    depth, half = part // Z, part // 2

    def pick(j):
        at = pl.multiple_of(lax.rem(z + j, Z) * depth, depth)
        rows = jnp.dot(
            choice_ref[...], hidden_ref[:, pl.ds(at, depth)], preferred_element_type=F32
        )
        return rows.astype(BF16)

    for k, target in enumerate((own_ref, up_ref, None, down_ref)):

        @pl.when(step == k)
        def _(target=target):
            for j in range(Z):
                at = j * depth
                if target is not None:
                    target[:, at : at + depth] = pick(j)
                elif at < half:
                    up_ref[:, part + at : part + at + depth] = pick(j)
                else:
                    down_ref[:, half + at : half + at + depth] = pick(j)


def select_rows(where, ids, label, hidden):
    tokens, width = hidden.shape
    part = width // X
    whole = lambda shape: pl.BlockSpec(shape, lambda k, w: (0, 0))
    shapes = [(CAP, part), (CAP, part * 3 // 2), (CAP, part * 3 // 2)]
    return pl.pallas_call(
        select_kernel,
        grid_spec=pltpu.PrefetchScalarGridSpec(
            num_scalar_prefetch=1,
            grid=(X,),
            in_specs=[
                whole((1, tokens)),
                whole((1, tokens)),
                pl.BlockSpec((tokens, part), lambda k, w: (0, lax.rem(w[1] + k, X))),
            ],
            out_specs=[whole(shape) for shape in shapes] + [whole((CAP, 128))],
            scratch_shapes=[pltpu.VMEM((CAP, tokens), BF16)],
        ),
        out_shape=[jax.ShapeDtypeStruct(shape, BF16) for shape in shapes]
        + [jax.ShapeDtypeStruct((CAP, 128), F32)],
        compiler_params=params(),
        cost_estimate=cost(2 * CAP * tokens * width, 2 * tokens * width),
    )(where, ids, label, hidden)


def project_first_kernel(offsets, *refs):
    rows, chunks, out = refs[:X], refs[X : X + len(offsets)], refs[-1]
    depth = chunks[0].shape[0]
    part = depth * Z
    left = jnp.concatenate([r[:, :part] for r in rows], axis=0)
    total = None
    for offset, chunk in zip(offsets, chunks):
        term = jnp.dot(
            left[:, offset * depth : (offset + 1) * depth],
            chunk[...],
            preferred_element_type=F32,
        )
        total = term if total is None else total + term
    out[...] = total


def project_first(rows, chunks, offsets):
    depth, wide = chunks[0].shape
    return pl.pallas_call(
        lambda *refs: project_first_kernel(offsets, *refs),
        out_shape=jax.ShapeDtypeStruct((X * CAP, wide), F32),
        compiler_params=params(),
        cost_estimate=cost(2 * X * CAP * depth * len(chunks) * wide, 6_000_000),
    )(*rows, *chunks)


def project_last_kernel(total_ref, *refs):
    rows, front, back, outs = refs[:X], refs[X], refs[X + 1], refs[X + 2 :]
    half = front.shape[0]
    left = jnp.concatenate([r[...] for r in rows], axis=0)
    total = total_ref[...]
    total += jnp.dot(left[:, :half], front[...], preferred_element_type=F32)
    total += jnp.dot(left[:, half:], back[...], preferred_element_type=F32)
    for k in range(X):
        outs[k][...] = total[k * CAP : (k + 1) * CAP, :].astype(outs[k].dtype)


def project_last(total, rows, front, back, held):
    half, wide = front.shape
    depth = 2 * half
    at = lambda *index: lambda i: index
    return pl.pallas_call(
        project_last_kernel,
        grid=(1,),
        in_specs=[pl.BlockSpec(total.shape, at(0, 0))]
        + [pl.BlockSpec((CAP, depth), at(0, Z // 2))] * X
        + [pl.BlockSpec((half, wide), at(0, 0))] * 2,
        out_specs=[pl.BlockSpec((CAP, wide), at(0, 0))] * X,
        out_shape=[jax.ShapeDtypeStruct((CAP, wide), held)] * X,
        compiler_params=params(),
        cost_estimate=cost(2 * X * CAP * depth * wide, 3_000_000),
    )(total, *rows, front, back)


FIRST = (0, 1, 7, 2, 6)
SECOND = (3, 5, 4)


def word_kernel(last, blocks, where_ref, both_ref, word_ref, *refs):
    tables, refs = refs[: X + 1], refs[X + 1 :]
    before = refs[0] if last else None
    out_ref, held, arrived = refs[1:] if last else refs
    x, z = where_ref[1], where_ref[2]
    rows = word_ref.shape[0]
    width = held.shape[2]
    half = held.shape[1] // 2
    spots = [
        held.at[0],
        held.at[1],
        held.at[2],
        held.at[3, pl.ds(0, half)],
        held.at[3, pl.ds(half, half)],
    ]
    copies = [
        pltpu.make_async_copy(
            table.at[pl.ds(0, spot.shape[0])], spot, arrived.at[i]
        )
        for i, (table, spot) in enumerate(zip(tables, spots))
    ]
    for copy in copies:
        copy.start()

    codes = word_ref[...]
    word = (codes[:, 0:1] * 128.0 + codes[:, 1:2]).astype(jnp.int32)
    column = lax.broadcasted_iota(jnp.int32, (rows, 128), 1)
    best = total = hit = None
    for part, back in enumerate((0, 1, 3, 2)):
        copies[part].wait()
        if part == X - 1:
            copies[X].wait()
        products = jnp.dot(both_ref[...], held[part], preferred_element_type=F32)
        logits = products[:rows] + products[rows:]
        local = word - (lax.rem(x - back + X, X) * Z + z) * width
        tiles = [logits[:, i * 128 : (i + 1) * 128] for i in range(width // 128)]
        peak = tiles[0]
        for tile in tiles[1:]:
            peak = jnp.maximum(peak, tile)
        if best is None:
            best, total, hit = peak, jnp.zeros_like(peak), jnp.zeros_like(peak)
        else:
            peak = jnp.maximum(best, peak)
            best, total = peak, total * jnp.exp(best - peak)
        for i, tile in enumerate(tiles):
            total += jnp.exp(tile - best)
            hit += jnp.where(column + i * 128 == local, tile, 0.0)

    highest = jnp.max(best, axis=1, keepdims=True)
    summed = jnp.sum(total * jnp.exp(best - highest), axis=1, keepdims=True)
    chosen = jnp.sum(hit, axis=1, keepdims=True)
    stats = jnp.where(
        column == 0,
        highest,
        jnp.where(column == 1, summed, jnp.where(column == 2, chosen, 0.0)),
    )
    for i, back in enumerate(blocks):
        piece = stats[i * CAP : (i + 1) * CAP, :]
        turned = jnp.concatenate([piece, piece], axis=0).T
        top_sum = jnp.where(column[0:1] < CAP, turned[0:1], turned[1:2])
        pair = jnp.concatenate([top_sum, turned[2:3]], axis=0)
        if last:
            for s in range(SECTIONS):
                out_ref[s, lax.rem(z - back + Z, Z)] = pair
        else:
            out_ref[i] = pair
    if last:
        for i, back in enumerate(FIRST):
            for s in range(SECTIONS):
                out_ref[s, lax.rem(z - back + Z, Z)] = before[i]


def word_stats(where, both, words, tables, before=None):
    last = before is not None
    blocks = SECOND if last else FIRST
    rows, depth = words.shape[0], both.shape[1]
    width = tables[0].shape[1]
    inside = pl.BlockSpec(memory_space=pltpu.VMEM)
    return pl.pallas_call(
        lambda *refs: word_kernel(last, blocks, *refs),
        in_specs=[pl.BlockSpec(memory_space=pltpu.SMEM), inside, inside]
        + [pl.BlockSpec(memory_space=pl.ANY)] * (X + 1)
        + ([inside] if last else []),
        out_specs=inside,
        out_shape=jax.ShapeDtypeStruct(
            ((SECTIONS, Z) if last else (len(blocks),)) + (2, 128), F32
        ),
        scratch_shapes=[
            pltpu.VMEM((X, depth, width), BF16),
            pltpu.SemaphoreType.DMA((X + 1,)),
        ],
        compiler_params=params(),
        cost_estimate=cost(4 * rows * depth * width * X, 2 * depth * width * X),
    )(where, both, words, *tables, *((before,) if last else ()))


def combine_kernel(ids_ref, stats_ref, out_ref):
    stats = stats_ref[...]
    tokens = ids_ref.shape[1]
    top, total, chosen = stats[:, :, 0, :CAP], stats[:, :, 0, CAP:], stats[:, :, 1, :CAP]
    highest = jnp.max(top, axis=1, keepdims=True)
    summed = jnp.sum(total * jnp.exp(top - highest), axis=1)
    loss = highest[:, 0] + jnp.log(summed) - jnp.sum(chosen, axis=1)
    columns = jnp.concatenate(
        [
            jnp.concatenate([loss, jnp.zeros((SECTIONS, 128 - CAP), F32)], axis=1),
            jnp.zeros((128 - SECTIONS, 128), F32),
        ],
        axis=0,
    ).T
    ids = ids_ref[...]
    owner = lax.broadcasted_iota(jnp.int32, (SECTIONS, tokens), 0)
    mine = jnp.where(ids == owner, 1.0, 0.0).astype(F32)
    earlier = lax.broadcasted_iota(jnp.int32, (tokens, tokens), 0)
    later = lax.broadcasted_iota(jnp.int32, (tokens, tokens), 1)
    upto = jnp.where(earlier <= later, 1.0, 0.0).astype(F32)
    within = jnp.dot(mine, upto, preferred_element_type=F32)
    slot = jnp.sum(within * mine, axis=0, keepdims=True)
    slot = (slot + 0.5).astype(jnp.int32) - 1
    place = lax.broadcasted_iota(jnp.int32, (CAP, tokens), 0)
    found = jnp.zeros((CAP, tokens), F32)
    for s in range(SECTIONS):
        found = jnp.where(ids == s, columns[0:CAP, s : s + 1], found)
    out_ref[...] = jnp.sum(jnp.where(place == slot, found, 0.0), axis=0, keepdims=True)


def combine(ids, stats):
    tokens = ids.shape[1]
    return pl.pallas_call(
        combine_kernel,
        out_shape=jax.ShapeDtypeStruct((1, tokens), F32),
        compiler_params=params(),
        cost_estimate=cost(2 * 8 * tokens * tokens, 400_000),
    )(ids, stats)


def split(blocks, width):
    held = jnp.concatenate(blocks, axis=0)
    wide = held[:, :width].astype(F32)
    high = lax.reduce_precision(wide, exponent_bits=8, mantissa_bits=7)
    both = jnp.concatenate([high, wide - high], axis=0).astype(BF16)
    return both, held[:, width:].astype(F32)


def relay(table, message, part):
    width = table.shape[1]
    return jnp.concatenate(
        [table, message[:, part : part + width], message[:, part + width :]], axis=0
    )


def body(hidden, cluster, label, proj, emb):
    x, z = lax.axis_index("x"), lax.axis_index("z")
    owner = lax.axis_index("y") * 2 + lax.axis_index("core")
    where = jnp.stack([owner, x, z]).astype(jnp.int32)
    ids = cluster.reshape(1, -1)
    weight, table = proj[0], emb[0]
    half = weight.shape[0] // 2
    wide = weight.shape[1]
    middle = table.shape[0] // 2

    deep = table.shape[0]
    right1, left1 = ring(weight, "z", Z, 1), ring(weight, "z", Z, -1)
    own_rows, up, down, words = select_rows(where, ids, label.reshape(1, -1), hidden)
    part = own_rows.shape[1]
    up, down = ring(up, "x", X, 1), ring(down, "x", X, -1)
    right1, left1, words = lax.optimization_barrier((right1, left1, words))
    right2, left2 = ring(right1, "z", Z, 1), ring(left1, "z", Z, -1)
    up, down, _, _ = lax.optimization_barrier((up, down, right1, left1))
    after = ring(relay(table, up, part), "x", X, 1)
    ahead = ring(relay(table, down, part), "x", X, -1)
    right3, left3 = ring(right2, "z", Z, 1), ring(left2, "z", Z, -1)
    front = ring(right3[:half], "z", Z, 1)
    back = ring(left3[half:], "z", Z, -1)
    front, back, after, ahead = lax.optimization_barrier((front, back, after, ahead))
    far1 = ring(after[:middle], "x", X, 1)
    far2 = ring(ahead[middle:deep], "x", X, -1)
    tables = [table, after, ahead, far1, far2]
    across = jnp.concatenate(
        [side[deep + i : deep + i + CAP] for side in (after, ahead) for i in (0, CAP)],
        axis=1,
    )
    rows = [own_rows, up, across, down]

    chunks = [weight, right1, left1, right2, left2, right3, left3]
    total = project_first(rows, chunks, [0, 7, 1, 6, 2, 5, 3])
    parts = project_last(total, rows, front, back, F32)
    own = parts[0]
    for k in range(1, X):
        own = own + ring(parts[k].astype(F16), "x", X, -k).astype(F32)

    message = jnp.concatenate([own, words], axis=1).astype(F16)
    r1, l1 = ring(message, "z", Z, 1), ring(message, "z", Z, -1)
    r2, l2 = ring(message, "z", Z, 2), ring(message, "z", Z, -2)
    r3, l3 = ring(r2, "z", Z, 1), ring(l2, "z", Z, -1)
    r4 = ring(r2, "z", Z, 2)

    stats = word_stats(where, *split([message, r1, l1, r2, l2], wide), tables)
    stats, r3, l3, r4 = lax.optimization_barrier((stats, r3, l3, r4))
    stats = word_stats(where, *split([r3, l3, r4], wide), tables, stats)
    stats = stats.reshape(SECTIONS * Z, 2, 128)
    stats = lax.all_to_all(stats, ("y", "core", "z"), 0, 0, tiled=True)
    loss = combine(ids, stats.reshape(SECTIONS, Z, 2, 128))
    return loss.reshape(-1)


def solution(mesh):
    fine = Mesh(mesh.devices.reshape(4, 2, X, Z), ("y", "core", "x", "z"))
    return jax.shard_map(
        body,
        mesh=fine,
        in_specs=(
            P(("x", "z"), None),
            P(("x", "z"), None),
            P(("x", "z")),
            P(("y", "core"), ("x", "z"), None),
            P(("y", "core"), None, ("x", "z")),
        ),
        out_specs=P(("x", "z")),
        check_vma=False,
    )
```

time: 152 us -> 115 us (0.76)
  waiting for transfers between devices: 65.8 us -> 36.4 us
  blocking collectives: 9.87 us -> 27.1 us
  between operations: 13.6 us -> 0.31 us
  starting transfers between devices: 42.1 us -> 32.4 us
  local copies, waits for them, and re-layouts: 6.09 us -> 3.94 us
    ppermute x24, waiting for transfers between devices: 64.3 us -> 36.4 us  [ring(): lax.ppermute(array, axis, [(i, (i + step) % size) for i in range(size)])]
    all_to_all x1, blocking collectives: 9.87 us -> 27.1 us  [body(): stats = lax.all_to_all(stats, ('y', 'core', 'z'), 0, 0, tiled=True)]
    ppermute x24, starting transfers between devices: 38.1 us -> 32.4 us  [ring(): lax.ppermute(array, axis, [(i, (i + step) % size) for i in range(size)])]
    ppermute x1 -> x0, starting transfers between devices: 3.95 us -> none  [body(): loss = loss + lax.ppermute(loss, 'core', [(0, 1), (1, 0)])]
    unnamed x17, local copies, waits for them, and re-layouts: 5.98 us -> 3.73 us
  transfers between devices with their start and end apart: 26 -> 24, of which waited for: 15 -> 14; matrix products, arithmetic and copies ran while one was open for 1% -> 1% of each run, Pallas kernels for 3% -> 6%
where the time goes in v2:
time: 115 us
  waiting for transfers between devices  36.4 us (32%)
  starting transfers between devices  32.4 us (28%)
  blocking collectives  27.1 us (24%)
  Pallas kernels  13.6 us (12%)
  local copies, waits for them, and re-layouts  3.94 us (3%)
    ppermute x24, waiting for transfers between devices, ring(): lax.ppermute(array, axis, [(i, (i + step) % size) for i in range(size)])  36.4 us
    ppermute x24, starting transfers between devices, ring(): lax.ppermute(array, axis, [(i, (i + step) % size) for i in range(size)])  32.4 us
    all_to_all x1, blocking collectives, body(): stats = lax.all_to_all(stats, ('y', 'core', 'z'), 0, 0, tiled=True)  27.1 us
    pallas_call x2, Pallas kernels, word_stats(): pl.pallas_call(lambda *refs: word_kernel(last, blocks, *refs), in_specs=[...  8.77 us
    unnamed x17, local copies, waits for them, and re-layouts  3.73 us
    pallas_call x1, Pallas kernels, select_rows(): pl.pallas_call(select_kernel, grid_spec=pltpu.PrefetchScalarGridSpec(num_...  2.37 us
  transfers between devices with their start and end apart: 24, of which 14 were waited for; matrix products, arithmetic and copies ran while one was open for 1% of the time, Pallas kernels for 6%

profile of v2, /device:TPU:1, one launch (start us, length us, event | category | flops | bytes accessed | tf_op | source)
XLA Modules:
  0.0 114.7 jit_solution(14581790680037956536)
XLA Ops:
  0.0 6.4 %collective-permute-start.3 = (bf16[256,1024]{1,0:T(8,128)(2,1)}, bf16[256,1024]{1,0:T(8,128)(2,1)S(1)}, u32[]{:S(2)}, u32[]{:S(2)}) collective-permute-start(bf16[256,1024]{1,0:T(8,128)(2,1)} %bitcast.13), channel_id=1, source_target_pairs={{0,7},{1,0},{2,1},{3,2},{4,3},{5,4},{6,5},{7,6},{8,15},{9,8},{10,9... | collective-permute-start | bytes 1572872 | tf_op jit(solution)/shard_map/ppermute | solution.py:20
  6.5 2.2 %copy-done = bf16[256,8192]{1,0:T(8,128)(2,1)S(1)} copy-done((bf16[256,8192]{1,0:T(8,128)(2,1)S(1)}, bf16[256,8192]{1,0:T(8,128)(2,1)}, u32[]{:S(2)}) %copy-start) | copy-done | bytes 4194328
  10.0 2.4 %shard_map.55 = (bf16[64,2048]{1,0:T(8,128)(2,1)S(1)}, bf16[64,3072]{1,0:T(8,128)(2,1)S(1)}, bf16[64,3072]{1,0:T(8,128)(2,1)S(1)}, f32[64,128]{1,0:T(8,128)S(1)}) custom-call(s32[3]{0:T(128)S(1)} %pad_add_fusion.where_ref.refs_0_, s32[1,256]{1,0:T(1,128)S(1)} %bitcast.18, s32[1,256]{1,0:T(1,128)S(1)} %bitcast.20, bf16[256,8192]{1,0:T(8,128)(2,1)S(1)} %copy-done), custom_call_target="tpu_custom_call" | custom-call | flops 268435456 | bytes 4194304 | tf_op jit(solution)/shard_map/pallas_call | solution.py:90
  13.7 1.5 %collective-permute-start.1 = (bf16[64,3072]{1,0:T(8,128)(2,1)S(1)}, bf16[64,3072]{1,0:T(8,128)(2,1)S(1)}, u32[]{:S(2)}, u32[]{:S(2)}) collective-permute-start(bf16[64,3072]{1,0:T(8,128)(2,1)S(1)} %get-tuple-element.28), channel_id=1, source_target_pairs={{0,24},{8,0},{16,8},{24,16},{1,25},{9,1},{17,9},{25,17},{2,26},{10... | collective-permute-start | bytes 1179656 | tf_op jit(solution)/shard_map/ppermute | solution.py:20
  15.2 2.1 %collective-permute-done.3.refs_6_ = bf16[256,1024]{1,0:T(8,128)(2,1)S(1)} collective-permute-done((bf16[256,1024]{1,0:T(8,128)(2,1)}, bf16[256,1024]{1,0:T(8,128)(2,1)S(1)}, u32[]{:S(2)}, u32[]{:S(2)}) %collective-permute-start.3) | collective-permute-done | bytes 524320 | tf_op jit(solution)/shard_map/ppermute | solution.py:20
  17.3 3.0 %collective-permute-done.2.refs_5_ = bf16[256,1024]{1,0:T(8,128)(2,1)S(1)} collective-permute-done((bf16[256,1024]{1,0:T(8,128)(2,1)}, bf16[256,1024]{1,0:T(8,128)(2,1)S(1)}, u32[]{:S(2)}, u32[]{:S(2)}) %collective-permute-start.2) | collective-permute-done | bytes 524320 | tf_op jit(solution)/shard_map/ppermute | solution.py:20
  20.3 2.7 %collective-permute-start.7 = (bf16[256,1024]{1,0:T(8,128)(2,1)S(1)}, bf16[256,1024]{1,0:T(8,128)(2,1)S(1)}, u32[]{:S(2)}, u32[]{:S(2)}) collective-permute-start(bf16[256,1024]{1,0:T(8,128)(2,1)S(1)} %collective-permute-done.3.refs_6_), channel_id=1, source_target_pairs={{0,7},{1,0},{2,1},{3,2},{4,3},{5,4},{6,5},{7,6},{8,15},{9,8},{10,9... | collective-permute-start | bytes 1572872 | tf_op jit(solution)/shard_map/ppermute | solution.py:20
  23.6 2.5 %collective-permute-start.11 = (bf16[1152,512]{1,0:T(8,128)(2,1)S(1)}, bf16[1152,512]{1,0:T(8,128)(2,1)S(1)}, u32[]{:S(2)}, u32[]{:S(2)}) collective-permute-start(bf16[1152,512]{1,0:T(8,128)(2,1)S(1)} %get-tuple-element.51), channel_id=1, source_target_pairs={{0,24},{8,0},{16,8},{24,16},{1,25},{9,1},{17,9},{25,17},{2,26},{10... | collective-permute-start | bytes 3538952 | tf_op jit(solution)/shard_map/ppermute | solution.py:20
  26.1 7.0 %collective-permute-done.4.refs_7_ = bf16[256,1024]{1,0:T(8,128)(2,1)S(1)} collective-permute-done((bf16[256,1024]{1,0:T(8,128)(2,1)S(1)}, bf16[256,1024]{1,0:T(8,128)(2,1)S(1)}, u32[]{:S(2)}, u32[]{:S(2)}) %collective-permute-start.4) | collective-permute-done | bytes 524320 | tf_op jit(solution)/shard_map/ppermute | solution.py:20
  33.1 2.7 %collective-permute-start.8 = (bf16[256,1024]{1,0:T(8,128)(2,1)S(1)}, bf16[256,1024]{1,0:T(8,128)(2,1)S(1)}, u32[]{:S(2)}, u32[]{:S(2)}) collective-permute-start(bf16[256,1024]{1,0:T(8,128)(2,1)S(1)} %collective-permute-done.7.refs_8_), channel_id=1, source_target_pairs={{0,7},{1,0},{2,1},{3,2},{4,3},{5,4},{6,5},{7,6},{8,15},{9,8},{10,9... | collective-permute-start | bytes 1572872 | tf_op jit(solution)/shard_map/ppermute | solution.py:20
  35.7 9.2 %collective-permute-done.5.refs_9_ = bf16[256,1024]{1,0:T(8,128)(2,1)S(1)} collective-permute-done((bf16[256,1024]{1,0:T(8,128)(2,1)S(1)}, bf16[256,1024]{1,0:T(8,128)(2,1)S(1)}, u32[]{:S(2)}, u32[]{:S(2)}) %collective-permute-start.5) | collective-permute-done | bytes 524320 | tf_op jit(solution)/shard_map/ppermute | solution.py:20
  45.1 2.7 %collective-permute-start.9 = (bf16[128,1024]{1,0:T(8,128)(2,1)S(1)}, bf16[128,1024]{1,0:T(8,128)(2,1)S(1)}, u32[]{:S(2)}, u32[]{:S(2)}) collective-permute-start(bf16[128,1024]{1,0:T(8,128)(2,1)S(1)} %slice.65), channel_id=1, source_target_pairs={{0,7},{1,0},{2,1},{3,2},{4,3},{5,4},{6,5},{7,6},{8,15},{9,8},{10,9... | collective-permute-start | bytes 786440 | tf_op jit(solution)/shard_map/ppermute | solution.py:20
  47.8 1.4 %collective-permute-done.11.refs_5_ = bf16[1152,512]{1,0:T(8,128)(2,1)S(1)} collective-permute-done((bf16[1152,512]{1,0:T(8,128)(2,1)S(1)}, bf16[1152,512]{1,0:T(8,128)(2,1)S(1)}, u32[]{:S(2)}, u32[]{:S(2)}) %collective-permute-start.11) | collective-permute-done | bytes 1179680 | tf_op jit(solution)/shard_map/ppermute | solution.py:20
  49.1 3.1 %collective-permute-done.10.refs_4_ = bf16[1152,512]{1,0:T(8,128)(2,1)S(1)} collective-permute-done((bf16[1152,512]{1,0:T(8,128)(2,1)S(1)}, bf16[1152,512]{1,0:T(8,128)(2,1)S(1)}, u32[]{:S(2)}, u32[]{:S(2)}) %collective-permute-start.10) | collective-permute-done | bytes 1179680 | tf_op jit(solution)/shard_map/ppermute | solution.py:20
  54.6 2.8 %collective-permute-start.13 = (f16[64,1024]{1,0:T(8,128)(2,1)S(1)}, f16[64,1024]{1,0:T(8,128)(2,1)S(1)}, u32[]{:S(2)}, u32[]{:S(2)}) collective-permute-start(f16[64,1024]{1,0:T(8,128)(2,1)S(1)} %convert_element_type.35), channel_id=1, source_target_pairs={{0,16},{8,24},{16,0},{24,8},{1,17},{9,25},{17,1},{25,9},{2,18},{10... | collective-permute-start | bytes 393224 | tf_op jit(solution)/shard_map/ppermute | solution.py:20
  59.3 1.8 %collective-permute-done.13 = f16[64,1024]{1,0:T(8,128)(2,1)S(1)} collective-permute-done((f16[64,1024]{1,0:T(8,128)(2,1)S(1)}, f16[64,1024]{1,0:T(8,128)(2,1)S(1)}, u32[]{:S(2)}, u32[]{:S(2)}) %collective-permute-start.13) | collective-permute-done | bytes 131104 | tf_op jit(solution)/shard_map/ppermute | solution.py:20
  61.5 2.5 %collective-permute-start.15 = (f16[64,1152]{1,0:T(8,128)(2,1)S(1)}, f16[64,1152]{1,0:T(8,128)(2,1)S(1)}, u32[]{:S(2)}, u32[]{:S(2)}) collective-permute-start(f16[64,1152]{1,0:T(8,128)(2,1)S(1)} %get-tuple-element.61), channel_id=1, source_target_pairs={{0,1},{1,2},{2,3},{3,4},{4,5},{5,6},{6,7},{7,0},{8,9},{9,10},{10,1... | collective-permute-start | bytes 442376 | tf_op jit(solution)/shard_map/ppermute | solution.py:20
  64.0 2.1 %collective-permute-start.20 = (bf16[512,512]{1,0:T(8,128)(2,1)S(1)}, bf16[512,512]{1,0:T(8,128)(2,1)S(1)}, u32[]{:S(2)}, u32[]{:S(2)}) collective-permute-start(bf16[512,512]{1,0:T(8,128)(2,1)S(1)} %slice.61), channel_id=1, source_target_pairs={{0,24},{8,0},{16,8},{24,16},{1,25},{9,1},{17,9},{25,17},{2,26},{10... | collective-permute-start | bytes 1572872 | tf_op jit(solution)/shard_map/ppermute | solution.py:20
  66.8 2.5 %collective-permute-done.17 = f16[64,1152]{1,0:T(8,128)(2,1)S(1)} collective-permute-done((f16[64,1152]{1,0:T(8,128)(2,1)S(1)}, f16[64,1152]{1,0:T(8,128)(2,1)S(1)}, u32[]{:S(2)}, u32[]{:S(2)}) %collective-permute-start.17) | collective-permute-done | bytes 147488 | tf_op jit(solution)/shard_map/ppermute | solution.py:20
  69.8 1.8 %collective-permute-start.23 = (f16[64,1152]{1,0:T(8,128)(2,1)S(1)}, f16[64,1152]{1,0:T(8,128)(2,1)S(1)}, u32[]{:S(2)}, u32[]{:S(2)}) collective-permute-start(f16[64,1152]{1,0:T(8,128)(2,1)S(1)} %collective-permute-done.17), channel_id=1, source_target_pairs={{0,2},{1,3},{2,4},{3,5},{4,6},{5,7},{6,0},{7,1},{8,10},{9,11},{10,... | collective-permute-start | bytes 442376 | tf_op jit(solution)/shard_map/ppermute | solution.py:20
  72.0 3.6 %collective-permute-done.18 = f16[64,1152]{1,0:T(8,128)(2,1)S(1)} collective-permute-done((f16[64,1152]{1,0:T(8,128)(2,1)S(1)}, f16[64,1152]{1,0:T(8,128)(2,1)S(1)}, u32[]{:S(2)}, u32[]{:S(2)}) %collective-permute-start.18) | collective-permute-done | bytes 147488 | tf_op jit(solution)/shard_map/ppermute | solution.py:20
  77.1 5.0 %shard_map.58.refs_8_ = f32[5,2,128]{2,1,0:T(2,128)S(1)} custom-call(s32[3]{0:T(128)S(1)} %pad_add_fusion.where_ref.refs_0_, bf16[640,1024]{1,0:T(8,128)(2,1)S(1)} %pad_maximum_fusion.refs_1_, f32[320,128]{1,0:T(8,128)S(1)} %slice_convert_fusion.refs_2_, bf16[1024,512]{1,0:T(8,128)(2,1)S(1)} %bitcast.11, ...), custom_call_target="tpu_custom_call" | custom-call | flops 2684354560 | bytes 4194304 | tf_op jit(solution)/shard_map/pallas_call | solution.py:246
  82.9 3.7 %shard_map.59 = f32[8,8,2,128]{3,2,1,0:T(2,128)S(1)} custom-call(s32[3]{0:T(128)S(1)} %pad_add_fusion.where_ref.refs_0_, bf16[384,1024]{1,0:T(8,128)(2,1)S(1)} %pad_maximum_fusion.3.refs_1_, f32[192,128]{1,0:T(8,128)S(1)} %slice_convert_fusion.1.refs_2_, bf16[1024,512]{1,0:T(8,128)(2,1)S(1)} %bitcast.12, ...), custom_call_target="tpu_custom_call" | custom-call | flops 1610612736 | bytes 4194304 | tf_op jit(solution)/shard_map/pallas_call | solution.py:246
  86.7 27.1 %all_to_all.5 = f32[64,2,128]{2,1,0:T(2,128)S(1)} all-to-all(f32[64,2,128]{2,1,0:T(2,128)S(1)} %bitcast.17), channel_id=1, replica_groups=mesh['y'=4,'core'=2,'x'=4,'z'=8] {'y','core','z'}, dimensions={0} | all-to-all | bytes 131072 | tf_op jit(solution)/shard_map/all_to_all | solution.py:369
  (72 shorter events, 12.6 us)
Async XLA Ops:
  0.0 17.3 %collective-permute-start.3 = (bf16[256,1024]{1,0:T(8,128)(2,1)}, bf16[256,1024]{1,0:T(8,128)(2,1)S(1)}, u32[]{:S(2)}, u32[]{:S(2)}) collective-permute-start(bf16[256,1024]{1,0:T(8,128)(2,1)} %bitcast.13), channel_id=1, source_target_pairs={{0,7},{1,0},{2,1},{3,2},{4,3},{5,4},{6,5},{7,6},{8,15},{9,8},{10,9... | collective-permute-start | bytes 1572872 | tf_op jit(solution)/shard_map/ppermute | solution.py:20
  6.4 13.9 %collective-permute-start.2 = (bf16[256,1024]{1,0:T(8,128)(2,1)}, bf16[256,1024]{1,0:T(8,128)(2,1)S(1)}, u32[]{:S(2)}, u32[]{:S(2)}) collective-permute-start(bf16[256,1024]{1,0:T(8,128)(2,1)} %bitcast.14), channel_id=1, source_target_pairs={{0,1},{1,2},{2,3},{3,4},{4,5},{5,6},{6,7},{7,0},{8,9},{9,10},{10,1... | collective-permute-start | bytes 1572872 | tf_op jit(solution)/shard_map/ppermute | solution.py:20
  12.4 10.9 %collective-permute-start = (bf16[64,3072]{1,0:T(8,128)(2,1)S(1)}, bf16[64,3072]{1,0:T(8,128)(2,1)S(1)}, u32[]{:S(2)}, u32[]{:S(2)}) collective-permute-start(bf16[64,3072]{1,0:T(8,128)(2,1)S(1)} %get-tuple-element.27), channel_id=1, source_target_pairs={{0,8},{8,16},{16,24},{24,0},{1,9},{9,17},{17,25},{25,1},{2,10},{10... | collective-permute-start | bytes 1179656 | tf_op jit(solution)/shard_map/ppermute | solution.py:20
  13.7 9.7 %collective-permute-start.1 = (bf16[64,3072]{1,0:T(8,128)(2,1)S(1)}, bf16[64,3072]{1,0:T(8,128)(2,1)S(1)}, u32[]{:S(2)}, u32[]{:S(2)}) collective-permute-start(bf16[64,3072]{1,0:T(8,128)(2,1)S(1)} %get-tuple-element.28), channel_id=1, source_target_pairs={{0,24},{8,0},{16,8},{24,16},{1,25},{9,1},{17,9},{25,17},{2,26},{10... | collective-permute-start | bytes 1179656 | tf_op jit(solution)/shard_map/ppermute | solution.py:20
  20.3 12.8 %collective-permute-start.4 = (bf16[256,1024]{1,0:T(8,128)(2,1)S(1)}, bf16[256,1024]{1,0:T(8,128)(2,1)S(1)}, u32[]{:S(2)}, u32[]{:S(2)}) collective-permute-start(bf16[256,1024]{1,0:T(8,128)(2,1)S(1)} %collective-permute-done.2.refs_5_), channel_id=1, source_target_pairs={{0,1},{1,2},{2,3},{3,4},{4,5},{5,6},{6,7},{7,0},{8,9},{9,10},{10,1... | collective-permute-start | bytes 1572872 | tf_op jit(solution)/shard_map/ppermute | solution.py:20
  20.3 12.8 %collective-permute-start.7 = (bf16[256,1024]{1,0:T(8,128)(2,1)S(1)}, bf16[256,1024]{1,0:T(8,128)(2,1)S(1)}, u32[]{:S(2)}, u32[]{:S(2)}) collective-permute-start(bf16[256,1024]{1,0:T(8,128)(2,1)S(1)} %collective-permute-done.3.refs_6_), channel_id=1, source_target_pairs={{0,7},{1,0},{2,1},{3,2},{4,3},{5,4},{6,5},{7,6},{8,15},{9,8},{10,9... | collective-permute-start | bytes 1572872 | tf_op jit(solution)/shard_map/ppermute | solution.py:20
  23.6 25.6 %collective-permute-start.11 = (bf16[1152,512]{1,0:T(8,128)(2,1)S(1)}, bf16[1152,512]{1,0:T(8,128)(2,1)S(1)}, u32[]{:S(2)}, u32[]{:S(2)}) collective-permute-start(bf16[1152,512]{1,0:T(8,128)(2,1)S(1)} %get-tuple-element.51), channel_id=1, source_target_pairs={{0,24},{8,0},{16,8},{24,16},{1,25},{9,1},{17,9},{25,17},{2,26},{10... | collective-permute-start | bytes 3538952 | tf_op jit(solution)/shard_map/ppermute | solution.py:20
  26.0 26.2 %collective-permute-start.10 = (bf16[1152,512]{1,0:T(8,128)(2,1)S(1)}, bf16[1152,512]{1,0:T(8,128)(2,1)S(1)}, u32[]{:S(2)}, u32[]{:S(2)}) collective-permute-start(bf16[1152,512]{1,0:T(8,128)(2,1)S(1)} %get-tuple-element.52), channel_id=1, source_target_pairs={{0,8},{8,16},{16,24},{24,0},{1,9},{9,17},{17,25},{25,1},{2,10},{10... | collective-permute-start | bytes 3538952 | tf_op jit(solution)/shard_map/ppermute | solution.py:20
  33.1 11.8 %collective-permute-start.5 = (bf16[256,1024]{1,0:T(8,128)(2,1)S(1)}, bf16[256,1024]{1,0:T(8,128)(2,1)S(1)}, u32[]{:S(2)}, u32[]{:S(2)}) collective-permute-start(bf16[256,1024]{1,0:T(8,128)(2,1)S(1)} %collective-permute-done.4.refs_7_), channel_id=1, source_target_pairs={{0,1},{1,2},{2,3},{3,4},{4,5},{5,6},{6,7},{7,0},{8,9},{9,10},{10,1... | collective-permute-start | bytes 1572872 | tf_op jit(solution)/shard_map/ppermute | solution.py:20
  33.1 12.0 %collective-permute-start.8 = (bf16[256,1024]{1,0:T(8,128)(2,1)S(1)}, bf16[256,1024]{1,0:T(8,128)(2,1)S(1)}, u32[]{:S(2)}, u32[]{:S(2)}) collective-permute-start(bf16[256,1024]{1,0:T(8,128)(2,1)S(1)} %collective-permute-done.7.refs_8_), channel_id=1, source_target_pairs={{0,7},{1,0},{2,1},{3,2},{4,3},{5,4},{6,5},{7,6},{8,15},{9,8},{10,9... | collective-permute-start | bytes 1572872 | tf_op jit(solution)/shard_map/ppermute | solution.py:20
  44.9 7.4 %collective-permute-start.6 = (bf16[128,1024]{1,0:T(8,128)(2,1)S(1)}, bf16[128,1024]{1,0:T(8,128)(2,1)S(1)}, u32[]{:S(2)}, u32[]{:S(2)}) collective-permute-start(bf16[128,1024]{1,0:T(8,128)(2,1)S(1)} %slice.64), channel_id=1, source_target_pairs={{0,1},{1,2},{2,3},{3,4},{4,5},{5,6},{6,7},{7,0},{8,9},{9,10},{10,1... | collective-permute-start | bytes 786440 | tf_op jit(solution)/shard_map/ppermute | solution.py:20
  45.1 7.2 %collective-permute-start.9 = (bf16[128,1024]{1,0:T(8,128)(2,1)S(1)}, bf16[128,1024]{1,0:T(8,128)(2,1)S(1)}, u32[]{:S(2)}, u32[]{:S(2)}) collective-permute-start(bf16[128,1024]{1,0:T(8,128)(2,1)S(1)} %slice.65), channel_id=1, source_target_pairs={{0,7},{1,0},{2,1},{3,2},{4,3},{5,4},{6,5},{7,6},{8,15},{9,8},{10,9... | collective-permute-start | bytes 786440 | tf_op jit(solution)/shard_map/ppermute | solution.py:20
  54.0 5.3 %collective-permute-start.14 = (f16[64,1024]{1,0:T(8,128)(2,1)S(1)}, f16[64,1024]{1,0:T(8,128)(2,1)S(1)}, u32[]{:S(2)}, u32[]{:S(2)}) collective-permute-start(f16[64,1024]{1,0:T(8,128)(2,1)S(1)} %convert_element_type.37), channel_id=1, source_target_pairs={{0,8},{8,16},{16,24},{24,0},{1,9},{9,17},{17,25},{25,1},{2,10},{10... | collective-permute-start | bytes 393224 | tf_op jit(solution)/shard_map/ppermute | solution.py:20
  54.6 6.5 %collective-permute-start.13 = (f16[64,1024]{1,0:T(8,128)(2,1)S(1)}, f16[64,1024]{1,0:T(8,128)(2,1)S(1)}, u32[]{:S(2)}, u32[]{:S(2)}) collective-permute-start(f16[64,1024]{1,0:T(8,128)(2,1)S(1)} %convert_element_type.35), channel_id=1, source_target_pairs={{0,16},{8,24},{16,0},{24,8},{1,17},{9,25},{17,1},{25,9},{2,18},{10... | collective-permute-start | bytes 393224 | tf_op jit(solution)/shard_map/ppermute | solution.py:20
  57.3 3.9 %collective-permute-start.12 = (f16[64,1024]{1,0:T(8,128)(2,1)S(1)}, f16[64,1024]{1,0:T(8,128)(2,1)S(1)}, u32[]{:S(2)}, u32[]{:S(2)}) collective-permute-start(f16[64,1024]{1,0:T(8,128)(2,1)S(1)} %convert_element_type.33), channel_id=1, source_target_pairs={{0,24},{8,0},{16,8},{24,16},{1,25},{9,1},{17,9},{25,17},{2,26},{10... | collective-permute-start | bytes 393224 | tf_op jit(solution)/shard_map/ppermute | solution.py:20
  61.4 7.9 %collective-permute-start.17 = (f16[64,1152]{1,0:T(8,128)(2,1)S(1)}, f16[64,1152]{1,0:T(8,128)(2,1)S(1)}, u32[]{:S(2)}, u32[]{:S(2)}) collective-permute-start(f16[64,1152]{1,0:T(8,128)(2,1)S(1)} %get-tuple-element.61), channel_id=1, source_target_pairs={{0,2},{1,3},{2,4},{3,5},{4,6},{5,7},{6,0},{7,1},{8,10},{9,11},{10,... | collective-permute-start | bytes 442376 | tf_op jit(solution)/shard_map/ppermute | solution.py:20
  61.5 8.4 %collective-permute-start.15 = (f16[64,1152]{1,0:T(8,128)(2,1)S(1)}, f16[64,1152]{1,0:T(8,128)(2,1)S(1)}, u32[]{:S(2)}, u32[]{:S(2)}) collective-permute-start(f16[64,1152]{1,0:T(8,128)(2,1)S(1)} %get-tuple-element.61), channel_id=1, source_target_pairs={{0,1},{1,2},{2,3},{3,4},{4,5},{5,6},{6,7},{7,0},{8,9},{9,10},{10,1... | collective-permute-start | bytes 442376 | tf_op jit(solution)/shard_map/ppermute | solution.py:20
  64.0 13.0 %collective-permute-start.20 = (bf16[512,512]{1,0:T(8,128)(2,1)S(1)}, bf16[512,512]{1,0:T(8,128)(2,1)S(1)}, u32[]{:S(2)}, u32[]{:S(2)}) collective-permute-start(bf16[512,512]{1,0:T(8,128)(2,1)S(1)} %slice.61), channel_id=1, source_target_pairs={{0,24},{8,0},{16,8},{24,16},{1,25},{9,1},{17,9},{25,17},{2,26},{10... | collective-permute-start | bytes 1572872 | tf_op jit(solution)/shard_map/ppermute | solution.py:20
  66.2 10.9 %collective-permute-start.19 = (bf16[512,512]{1,0:T(8,128)(2,1)S(1)}, bf16[512,512]{1,0:T(8,128)(2,1)S(1)}, u32[]{:S(2)}, u32[]{:S(2)}) collective-permute-start(bf16[512,512]{1,0:T(8,128)(2,1)S(1)} %slice.60), channel_id=1, source_target_pairs={{0,8},{8,16},{16,24},{24,0},{1,9},{9,17},{17,25},{25,1},{2,10},{10... | collective-permute-start | bytes 1572872 | tf_op jit(solution)/shard_map/ppermute | solution.py:20
  66.2 5.5 %collective-permute-start.16 = (f16[64,1152]{1,0:T(8,128)(2,1)S(1)}, f16[64,1152]{1,0:T(8,128)(2,1)S(1)}, u32[]{:S(2)}, u32[]{:S(2)}) collective-permute-start(f16[64,1152]{1,0:T(8,128)(2,1)S(1)} %get-tuple-element.61), channel_id=1, source_target_pairs={{0,7},{1,0},{2,1},{3,2},{4,3},{5,4},{6,5},{7,6},{8,15},{9,8},{10,9... | collective-permute-start | bytes 442376 | tf_op jit(solution)/shard_map/ppermute | solution.py:20
  69.3 6.3 %collective-permute-start.18 = (f16[64,1152]{1,0:T(8,128)(2,1)S(1)}, f16[64,1152]{1,0:T(8,128)(2,1)S(1)}, u32[]{:S(2)}, u32[]{:S(2)}) collective-permute-start(f16[64,1152]{1,0:T(8,128)(2,1)S(1)} %get-tuple-element.61), channel_id=1, source_target_pairs={{0,6},{1,7},{2,0},{3,1},{4,2},{5,3},{6,4},{7,5},{8,14},{9,15},{10,... | collective-permute-start | bytes 442376 | tf_op jit(solution)/shard_map/ppermute | solution.py:20
  69.8 12.3 %collective-permute-start.23 = (f16[64,1152]{1,0:T(8,128)(2,1)S(1)}, f16[64,1152]{1,0:T(8,128)(2,1)S(1)}, u32[]{:S(2)}, u32[]{:S(2)}) collective-permute-start(f16[64,1152]{1,0:T(8,128)(2,1)S(1)} %collective-permute-done.17), channel_id=1, source_target_pairs={{0,2},{1,3},{2,4},{3,5},{4,6},{5,7},{6,0},{7,1},{8,10},{9,11},{10,... | collective-permute-start | bytes 442376 | tf_op jit(solution)/shard_map/ppermute | solution.py:20
  71.7 10.9 %collective-permute-start.21 = (f16[64,1152]{1,0:T(8,128)(2,1)S(1)}, f16[64,1152]{1,0:T(8,128)(2,1)S(1)}, u32[]{:S(2)}, u32[]{:S(2)}) collective-permute-start(f16[64,1152]{1,0:T(8,128)(2,1)S(1)} %collective-permute-done.17), channel_id=1, source_target_pairs={{0,1},{1,2},{2,3},{3,4},{4,5},{5,6},{6,7},{7,0},{8,9},{9,10},{10,1... | collective-permute-start | bytes 442376 | tf_op jit(solution)/shard_map/ppermute | solution.py:20
  75.6 7.0 %collective-permute-start.22 = (f16[64,1152]{1,0:T(8,128)(2,1)S(1)}, f16[64,1152]{1,0:T(8,128)(2,1)S(1)}, u32[]{:S(2)}, u32[]{:S(2)}) collective-permute-start(f16[64,1152]{1,0:T(8,128)(2,1)S(1)} %collective-permute-done.18), channel_id=1, source_target_pairs={{0,7},{1,0},{2,1},{3,2},{4,3},{5,4},{6,5},{7,6},{8,15},{9,8},{10,9... | collective-permute-start | bytes 442376 | tf_op jit(solution)/shard_map/ppermute | solution.py:20
  (6 other events, 76.5 us)

commit v3 on v2

--- a/solution.py
+++ b/solution.py
@@ -168,36 +168,28 @@
 def word_kernel(last, blocks, where_ref, both_ref, word_ref, *refs):
     tables, refs = refs[: X + 1], refs[X + 1 :]
     before = refs[0] if last else None
-    out_ref, held, arrived = refs[1:] if last else refs
+    out_ref = refs[-1]
     x, z = where_ref[1], where_ref[2]
     rows = word_ref.shape[0]
-    width = held.shape[2]
-    half = held.shape[1] // 2
-    spots = [
-        held.at[0],
-        held.at[1],
-        held.at[2],
-        held.at[3, pl.ds(0, half)],
-        held.at[3, pl.ds(half, half)],
-    ]
-    copies = [
-        pltpu.make_async_copy(
-            table.at[pl.ds(0, spot.shape[0])], spot, arrived.at[i]
-        )
-        for i, (table, spot) in enumerate(zip(tables, spots))
-    ]
-    for copy in copies:
-        copy.start()
+    deep, width = tables[0].shape
+    half = deep // 2
 
     codes = word_ref[...]
     word = (codes[:, 0:1] * 128.0 + codes[:, 1:2]).astype(jnp.int32)
     column = lax.broadcasted_iota(jnp.int32, (rows, 128), 1)
     best = total = hit = None
     for part, back in enumerate((0, 1, 3, 2)):
-        copies[part].wait()
-        if part == X - 1:
-            copies[X].wait()
-        products = jnp.dot(both_ref[...], held[part], preferred_element_type=F32)
+        if part < X - 1:
+            products = jnp.dot(
+                both_ref[...], tables[part][:deep, :], preferred_element_type=F32
+            )
+        else:
+            products = jnp.dot(
+                both_ref[:, :half], tables[part][...], preferred_element_type=F32
+            )
+            products += jnp.dot(
+                both_ref[:, half:], tables[part + 1][...], preferred_element_type=F32
+            )
         logits = products[:rows] + products[rows:]
         local = word - (lax.rem(x - back + X, X) * Z + z) * width
         tiles = [logits[:, i * 128 : (i + 1) * 128] for i in range(width // 128)]
@@ -246,16 +238,12 @@
     return pl.pallas_call(
         lambda *refs: word_kernel(last, blocks, *refs),
         in_specs=[pl.BlockSpec(memory_space=pltpu.SMEM), inside, inside]
-        + [pl.BlockSpec(memory_space=pl.ANY)] * (X + 1)
+        + [inside] * (X + 1)
         + ([inside] if last else []),
         out_specs=inside,
         out_shape=jax.ShapeDtypeStruct(
             ((SECTIONS, Z) if last else (len(blocks),)) + (2, 128), F32
         ),
-        scratch_shapes=[
-            pltpu.VMEM((X, depth, width), BF16),
-            pltpu.SemaphoreType.DMA((X + 1,)),
-        ],
         compiler_params=params(),
         cost_estimate=cost(4 * rows * depth * width * X, 2 * depth * width * X),
     )(where, both, words, *tables, *((before,) if last else ()))

time: 115 us -> 113 us (0.983)
  Pallas kernels: 13.6 us -> 11.4 us
  blocking collectives: 27.1 us -> 25.9 us
  waiting for transfers between devices: 36.4 us -> 37.6 us
    pallas_call x2, Pallas kernels: 8.77 us -> 6.51 us  [word_stats(): pl.pallas_call(lambda *refs: word_kernel(last, blocks, *refs), in_specs=[...]
    ppermute x24, waiting for transfers between devices: 36.4 us -> 37.6 us  [ring(): lax.ppermute(array, axis, [(i, (i + step) % size) for i in range(size)])]
    all_to_all x1, blocking collectives: 27.1 us -> 25.9 us  [body(): stats = lax.all_to_all(stats, ('y', 'core', 'z'), 0, 0, tiled=True)]
where the time goes in v3:
time: 113 us; the launch traced here: 112 us
  waiting for transfers between devices  37.6 us (33%)
  starting transfers between devices  32.4 us (29%)
  blocking collectives  25.9 us (23%)
  Pallas kernels  11.4 us (10%)
  local copies, waits for them, and re-layouts  3.94 us (3%)
    ppermute x24, waiting for transfers between devices, ring(): lax.ppermute(array, axis, [(i, (i + step) % size) for i in range(size)])  37.6 us
    ppermute x24, starting transfers between devices, ring(): lax.ppermute(array, axis, [(i, (i + step) % size) for i in range(size)])  32.4 us
    all_to_all x1, blocking collectives, body(): stats = lax.all_to_all(stats, ('y', 'core', 'z'), 0, 0, tiled=True)  25.9 us
    pallas_call x2, Pallas kernels, word_stats(): pl.pallas_call(lambda *refs: word_kernel(last, blocks, *refs), in_specs=[...  6.51 us
    unnamed x17, local copies, waits for them, and re-layouts  3.73 us
    pallas_call x1, Pallas kernels, select_rows(): pl.pallas_call(select_kernel, grid_spec=pltpu.PrefetchScalarGridSpec(num_...  2.37 us
  transfers between devices with their start and end apart: 24, of which 14 were waited for; matrix products, arithmetic and copies ran while one was open for 1% of the time, Pallas kernels for 6%

profile of v3, /device:TPU:1, one launch (start us, length us, event | category | flops | bytes accessed | tf_op | source)
XLA Modules:
  0.0 112.5 jit_solution(6734522190778206587)
XLA Ops:
  0.0 6.4 %collective-permute-start.3 = (bf16[256,1024]{1,0:T(8,128)(2,1)}, bf16[256,1024]{1,0:T(8,128)(2,1)S(1)}, u32[]{:S(2)}, u32[]{:S(2)}) collective-permute-start(bf16[256,1024]{1,0:T(8,128)(2,1)} %bitcast.13), channel_id=1, source_target_pairs={{0,7},{1,0},{2,1},{3,2},{4,3},{5,4},{6,5},{7,6},{8,15},{9,8},{10,9... | collective-permute-start | bytes 1572872 | tf_op jit(solution)/shard_map/ppermute | solution.py:20
  6.5 2.2 %copy-done = bf16[256,8192]{1,0:T(8,128)(2,1)S(1)} copy-done((bf16[256,8192]{1,0:T(8,128)(2,1)S(1)}, bf16[256,8192]{1,0:T(8,128)(2,1)}, u32[]{:S(2)}) %copy-start) | copy-done | bytes 4194328
  10.0 2.4 %shard_map.55 = (bf16[64,2048]{1,0:T(8,128)(2,1)S(1)}, bf16[64,3072]{1,0:T(8,128)(2,1)S(1)}, bf16[64,3072]{1,0:T(8,128)(2,1)S(1)}, f32[64,128]{1,0:T(8,128)S(1)}) custom-call(s32[3]{0:T(128)S(1)} %pad_add_fusion.where_ref.refs_0_, s32[1,256]{1,0:T(1,128)S(1)} %bitcast.18, s32[1,256]{1,0:T(1,128)S(1)} %bitcast.20, bf16[256,8192]{1,0:T(8,128)(2,1)S(1)} %copy-done), custom_call_target="tpu_custom_call" | custom-call | flops 268435456 | bytes 4194304 | tf_op jit(solution)/shard_map/pallas_call | solution.py:90
  13.7 1.5 %collective-permute-start.1 = (bf16[64,3072]{1,0:T(8,128)(2,1)S(1)}, bf16[64,3072]{1,0:T(8,128)(2,1)S(1)}, u32[]{:S(2)}, u32[]{:S(2)}) collective-permute-start(bf16[64,3072]{1,0:T(8,128)(2,1)S(1)} %get-tuple-element.28), channel_id=1, source_target_pairs={{0,24},{8,0},{16,8},{24,16},{1,25},{9,1},{17,9},{25,17},{2,26},{10... | collective-permute-start | bytes 1179656 | tf_op jit(solution)/shard_map/ppermute | solution.py:20
  15.2 2.1 %collective-permute-done.3.refs_6_ = bf16[256,1024]{1,0:T(8,128)(2,1)S(1)} collective-permute-done((bf16[256,1024]{1,0:T(8,128)(2,1)}, bf16[256,1024]{1,0:T(8,128)(2,1)S(1)}, u32[]{:S(2)}, u32[]{:S(2)}) %collective-permute-start.3) | collective-permute-done | bytes 524320 | tf_op jit(solution)/shard_map/ppermute | solution.py:20
  17.3 3.0 %collective-permute-done.2.refs_5_ = bf16[256,1024]{1,0:T(8,128)(2,1)S(1)} collective-permute-done((bf16[256,1024]{1,0:T(8,128)(2,1)}, bf16[256,1024]{1,0:T(8,128)(2,1)S(1)}, u32[]{:S(2)}, u32[]{:S(2)}) %collective-permute-start.2) | collective-permute-done | bytes 524320 | tf_op jit(solution)/shard_map/ppermute | solution.py:20
  20.3 2.7 %collective-permute-start.7 = (bf16[256,1024]{1,0:T(8,128)(2,1)S(1)}, bf16[256,1024]{1,0:T(8,128)(2,1)S(1)}, u32[]{:S(2)}, u32[]{:S(2)}) collective-permute-start(bf16[256,1024]{1,0:T(8,128)(2,1)S(1)} %collective-permute-done.3.refs_6_), channel_id=1, source_target_pairs={{0,7},{1,0},{2,1},{3,2},{4,3},{5,4},{6,5},{7,6},{8,15},{9,8},{10,9... | collective-permute-start | bytes 1572872 | tf_op jit(solution)/shard_map/ppermute | solution.py:20
  23.6 2.5 %collective-permute-start.11 = (bf16[1152,512]{1,0:T(8,128)(2,1)S(1)}, bf16[1152,512]{1,0:T(8,128)(2,1)S(1)}, u32[]{:S(2)}, u32[]{:S(2)}) collective-permute-start(bf16[1152,512]{1,0:T(8,128)(2,1)S(1)} %get-tuple-element.51), channel_id=1, source_target_pairs={{0,24},{8,0},{16,8},{24,16},{1,25},{9,1},{17,9},{25,17},{2,26},{10... | collective-permute-start | bytes 3538952 | tf_op jit(solution)/shard_map/ppermute | solution.py:20
  26.1 7.0 %collective-permute-done.4.refs_7_ = bf16[256,1024]{1,0:T(8,128)(2,1)S(1)} collective-permute-done((bf16[256,1024]{1,0:T(8,128)(2,1)S(1)}, bf16[256,1024]{1,0:T(8,128)(2,1)S(1)}, u32[]{:S(2)}, u32[]{:S(2)}) %collective-permute-start.4) | collective-permute-done | bytes 524320 | tf_op jit(solution)/shard_map/ppermute | solution.py:20
  33.1 2.7 %collective-permute-start.8 = (bf16[256,1024]{1,0:T(8,128)(2,1)S(1)}, bf16[256,1024]{1,0:T(8,128)(2,1)S(1)}, u32[]{:S(2)}, u32[]{:S(2)}) collective-permute-start(bf16[256,1024]{1,0:T(8,128)(2,1)S(1)} %collective-permute-done.7.refs_8_), channel_id=1, source_target_pairs={{0,7},{1,0},{2,1},{3,2},{4,3},{5,4},{6,5},{7,6},{8,15},{9,8},{10,9... | collective-permute-start | bytes 1572872 | tf_op jit(solution)/shard_map/ppermute | solution.py:20
  35.7 9.2 %collective-permute-done.5.refs_9_ = bf16[256,1024]{1,0:T(8,128)(2,1)S(1)} collective-permute-done((bf16[256,1024]{1,0:T(8,128)(2,1)S(1)}, bf16[256,1024]{1,0:T(8,128)(2,1)S(1)}, u32[]{:S(2)}, u32[]{:S(2)}) %collective-permute-start.5) | collective-permute-done | bytes 524320 | tf_op jit(solution)/shard_map/ppermute | solution.py:20
  45.1 2.7 %collective-permute-start.9 = (bf16[128,1024]{1,0:T(8,128)(2,1)S(1)}, bf16[128,1024]{1,0:T(8,128)(2,1)S(1)}, u32[]{:S(2)}, u32[]{:S(2)}) collective-permute-start(bf16[128,1024]{1,0:T(8,128)(2,1)S(1)} %slice.65), channel_id=1, source_target_pairs={{0,7},{1,0},{2,1},{3,2},{4,3},{5,4},{6,5},{7,6},{8,15},{9,8},{10,9... | collective-permute-start | bytes 786440 | tf_op jit(solution)/shard_map/ppermute | solution.py:20
  49.1 3.1 %collective-permute-done.10.refs_4_ = bf16[1152,512]{1,0:T(8,128)(2,1)S(1)} collective-permute-done((bf16[1152,512]{1,0:T(8,128)(2,1)S(1)}, bf16[1152,512]{1,0:T(8,128)(2,1)S(1)}, u32[]{:S(2)}, u32[]{:S(2)}) %collective-permute-start.10) | collective-permute-done | bytes 1179680 | tf_op jit(solution)/shard_map/ppermute | solution.py:20
  54.6 2.8 %collective-permute-start.13 = (f16[64,1024]{1,0:T(8,128)(2,1)S(1)}, f16[64,1024]{1,0:T(8,128)(2,1)S(1)}, u32[]{:S(2)}, u32[]{:S(2)}) collective-permute-start(f16[64,1024]{1,0:T(8,128)(2,1)S(1)} %convert_element_type.35), channel_id=1, source_target_pairs={{0,16},{8,24},{16,0},{24,8},{1,17},{9,25},{17,1},{25,9},{2,18},{10... | collective-permute-start | bytes 393224 | tf_op jit(solution)/shard_map/ppermute | solution.py:20
  59.3 1.8 %collective-permute-done.13 = f16[64,1024]{1,0:T(8,128)(2,1)S(1)} collective-permute-done((f16[64,1024]{1,0:T(8,128)(2,1)S(1)}, f16[64,1024]{1,0:T(8,128)(2,1)S(1)}, u32[]{:S(2)}, u32[]{:S(2)}) %collective-permute-start.13) | collective-permute-done | bytes 131104 | tf_op jit(solution)/shard_map/ppermute | solution.py:20
  61.5 2.5 %collective-permute-start.15 = (f16[64,1152]{1,0:T(8,128)(2,1)S(1)}, f16[64,1152]{1,0:T(8,128)(2,1)S(1)}, u32[]{:S(2)}, u32[]{:S(2)}) collective-permute-start(f16[64,1152]{1,0:T(8,128)(2,1)S(1)} %get-tuple-element.61), channel_id=1, source_target_pairs={{0,1},{1,2},{2,3},{3,4},{4,5},{5,6},{6,7},{7,0},{8,9},{9,10},{10,1... | collective-permute-start | bytes 442376 | tf_op jit(solution)/shard_map/ppermute | solution.py:20
  64.0 2.1 %collective-permute-start.20 = (bf16[512,512]{1,0:T(8,128)(2,1)S(1)}, bf16[512,512]{1,0:T(8,128)(2,1)S(1)}, u32[]{:S(2)}, u32[]{:S(2)}) collective-permute-start(bf16[512,512]{1,0:T(8,128)(2,1)S(1)} %slice.61), channel_id=1, source_target_pairs={{0,24},{8,0},{16,8},{24,16},{1,25},{9,1},{17,9},{25,17},{2,26},{10... | collective-permute-start | bytes 1572872 | tf_op jit(solution)/shard_map/ppermute | solution.py:20
  66.8 2.5 %collective-permute-done.17 = f16[64,1152]{1,0:T(8,128)(2,1)S(1)} collective-permute-done((f16[64,1152]{1,0:T(8,128)(2,1)S(1)}, f16[64,1152]{1,0:T(8,128)(2,1)S(1)}, u32[]{:S(2)}, u32[]{:S(2)}) %collective-permute-start.17) | collective-permute-done | bytes 147488 | tf_op jit(solution)/shard_map/ppermute | solution.py:20
  69.8 1.8 %collective-permute-start.23 = (f16[64,1152]{1,0:T(8,128)(2,1)S(1)}, f16[64,1152]{1,0:T(8,128)(2,1)S(1)}, u32[]{:S(2)}, u32[]{:S(2)}) collective-permute-start(f16[64,1152]{1,0:T(8,128)(2,1)S(1)} %collective-permute-done.17), channel_id=1, source_target_pairs={{0,2},{1,3},{2,4},{3,5},{4,6},{5,7},{6,0},{7,1},{8,10},{9,11},{10,... | collective-permute-start | bytes 442376 | tf_op jit(solution)/shard_map/ppermute | solution.py:20
  72.0 3.6 %collective-permute-done.18 = f16[64,1152]{1,0:T(8,128)(2,1)S(1)} collective-permute-done((f16[64,1152]{1,0:T(8,128)(2,1)S(1)}, f16[64,1152]{1,0:T(8,128)(2,1)S(1)}, u32[]{:S(2)}, u32[]{:S(2)}) %collective-permute-start.18) | collective-permute-done | bytes 147488 | tf_op jit(solution)/shard_map/ppermute | solution.py:20
  77.1 3.8 %shard_map.58.refs_8_ = f32[5,2,128]{2,1,0:T(2,128)S(1)} custom-call(s32[3]{0:T(128)S(1)} %pad_add_fusion.where_ref.refs_0_, bf16[640,1024]{1,0:T(8,128)(2,1)S(1)} %pad_maximum_fusion.refs_1_, f32[320,128]{1,0:T(8,128)S(1)} %slice_convert_fusion.refs_2_, bf16[1024,512]{1,0:T(8,128)(2,1)S(1)} %bitcast.11, ...), custom_call_target="tpu_custom_call" | custom-call | flops 2684354560 | bytes 4194304 | tf_op jit(solution)/shard_map/pallas_call | solution.py:238
  80.9 1.7 %collective-permute-done.21 = f16[64,1152]{1,0:T(8,128)(2,1)S(1)} collective-permute-done((f16[64,1152]{1,0:T(8,128)(2,1)S(1)}, f16[64,1152]{1,0:T(8,128)(2,1)S(1)}, u32[]{:S(2)}, u32[]{:S(2)}) %collective-permute-start.21) | collective-permute-done | bytes 147488 | tf_op jit(solution)/shard_map/ppermute | solution.py:20
  82.9 2.7 %shard_map.59 = f32[8,8,2,128]{3,2,1,0:T(2,128)S(1)} custom-call(s32[3]{0:T(128)S(1)} %pad_add_fusion.where_ref.refs_0_, bf16[384,1024]{1,0:T(8,128)(2,1)S(1)} %pad_maximum_fusion.3.refs_1_, f32[192,128]{1,0:T(8,128)S(1)} %slice_convert_fusion.1.refs_2_, bf16[1024,512]{1,0:T(8,128)(2,1)S(1)} %bitcast.12, ...), custom_call_target="tpu_custom_call" | custom-call | flops 1610612736 | bytes 4194304 | tf_op jit(solution)/shard_map/pallas_call | solution.py:238
  85.6 25.9 %all_to_all.5 = f32[64,2,128]{2,1,0:T(2,128)S(1)} all-to-all(f32[64,2,128]{2,1,0:T(2,128)S(1)} %bitcast.17), channel_id=1, replica_groups=mesh['y'=4,'core'=2,'x'=4,'z'=8] {'y','core','z'}, dimensions={0} | all-to-all | bytes 131072 | tf_op jit(solution)/shard_map/all_to_all | solution.py:357
  (72 shorter events, 13.5 us)
Async XLA Ops:
  0.0 17.3 %collective-permute-start.3 = (bf16[256,1024]{1,0:T(8,128)(2,1)}, bf16[256,1024]{1,0:T(8,128)(2,1)S(1)}, u32[]{:S(2)}, u32[]{:S(2)}) collective-permute-start(bf16[256,1024]{1,0:T(8,128)(2,1)} %bitcast.13), channel_id=1, source_target_pairs={{0,7},{1,0},{2,1},{3,2},{4,3},{5,4},{6,5},{7,6},{8,15},{9,8},{10,9... | collective-permute-start | bytes 1572872 | tf_op jit(solution)/shard_map/ppermute | solution.py:20
  6.4 13.9 %collective-permute-start.2 = (bf16[256,1024]{1,0:T(8,128)(2,1)}, bf16[256,1024]{1,0:T(8,128)(2,1)S(1)}, u32[]{:S(2)}, u32[]{:S(2)}) collective-permute-start(bf16[256,1024]{1,0:T(8,128)(2,1)} %bitcast.14), channel_id=1, source_target_pairs={{0,1},{1,2},{2,3},{3,4},{4,5},{5,6},{6,7},{7,0},{8,9},{9,10},{10,1... | collective-permute-start | bytes 1572872 | tf_op jit(solution)/shard_map/ppermute | solution.py:20
  12.4 10.9 %collective-permute-start = (bf16[64,3072]{1,0:T(8,128)(2,1)S(1)}, bf16[64,3072]{1,0:T(8,128)(2,1)S(1)}, u32[]{:S(2)}, u32[]{:S(2)}) collective-permute-start(bf16[64,3072]{1,0:T(8,128)(2,1)S(1)} %get-tuple-element.27), channel_id=1, source_target_pairs={{0,8},{8,16},{16,24},{24,0},{1,9},{9,17},{17,25},{25,1},{2,10},{10... | collective-permute-start | bytes 1179656 | tf_op jit(solution)/shard_map/ppermute | solution.py:20
  13.7 9.7 %collective-permute-start.1 = (bf16[64,3072]{1,0:T(8,128)(2,1)S(1)}, bf16[64,3072]{1,0:T(8,128)(2,1)S(1)}, u32[]{:S(2)}, u32[]{:S(2)}) collective-permute-start(bf16[64,3072]{1,0:T(8,128)(2,1)S(1)} %get-tuple-element.28), channel_id=1, source_target_pairs={{0,24},{8,0},{16,8},{24,16},{1,25},{9,1},{17,9},{25,17},{2,26},{10... | collective-permute-start | bytes 1179656 | tf_op jit(solution)/shard_map/ppermute | solution.py:20
  20.3 12.8 %collective-permute-start.4 = (bf16[256,1024]{1,0:T(8,128)(2,1)S(1)}, bf16[256,1024]{1,0:T(8,128)(2,1)S(1)}, u32[]{:S(2)}, u32[]{:S(2)}) collective-permute-start(bf16[256,1024]{1,0:T(8,128)(2,1)S(1)} %collective-permute-done.2.refs_5_), channel_id=1, source_target_pairs={{0,1},{1,2},{2,3},{3,4},{4,5},{5,6},{6,7},{7,0},{8,9},{9,10},{10,1... | collective-permute-start | bytes 1572872 | tf_op jit(solution)/shard_map/ppermute | solution.py:20
  20.3 12.8 %collective-permute-start.7 = (bf16[256,1024]{1,0:T(8,128)(2,1)S(1)}, bf16[256,1024]{1,0:T(8,128)(2,1)S(1)}, u32[]{:S(2)}, u32[]{:S(2)}) collective-permute-start(bf16[256,1024]{1,0:T(8,128)(2,1)S(1)} %collective-permute-done.3.refs_6_), channel_id=1, source_target_pairs={{0,7},{1,0},{2,1},{3,2},{4,3},{5,4},{6,5},{7,6},{8,15},{9,8},{10,9... | collective-permute-start | bytes 1572872 | tf_op jit(solution)/shard_map/ppermute | solution.py:20
  23.6 25.6 %collective-permute-start.11 = (bf16[1152,512]{1,0:T(8,128)(2,1)S(1)}, bf16[1152,512]{1,0:T(8,128)(2,1)S(1)}, u32[]{:S(2)}, u32[]{:S(2)}) collective-permute-start(bf16[1152,512]{1,0:T(8,128)(2,1)S(1)} %get-tuple-element.51), channel_id=1, source_target_pairs={{0,24},{8,0},{16,8},{24,16},{1,25},{9,1},{17,9},{25,17},{2,26},{10... | collective-permute-start | bytes 3538952 | tf_op jit(solution)/shard_map/ppermute | solution.py:20
  26.0 26.2 %collective-permute-start.10 = (bf16[1152,512]{1,0:T(8,128)(2,1)S(1)}, bf16[1152,512]{1,0:T(8,128)(2,1)S(1)}, u32[]{:S(2)}, u32[]{:S(2)}) collective-permute-start(bf16[1152,512]{1,0:T(8,128)(2,1)S(1)} %get-tuple-element.52), channel_id=1, source_target_pairs={{0,8},{8,16},{16,24},{24,0},{1,9},{9,17},{17,25},{25,1},{2,10},{10... | collective-permute-start | bytes 3538952 | tf_op jit(solution)/shard_map/ppermute | solution.py:20
  33.1 11.8 %collective-permute-start.5 = (bf16[256,1024]{1,0:T(8,128)(2,1)S(1)}, bf16[256,1024]{1,0:T(8,128)(2,1)S(1)}, u32[]{:S(2)}, u32[]{:S(2)}) collective-permute-start(bf16[256,1024]{1,0:T(8,128)(2,1)S(1)} %collective-permute-done.4.refs_7_), channel_id=1, source_target_pairs={{0,1},{1,2},{2,3},{3,4},{4,5},{5,6},{6,7},{7,0},{8,9},{9,10},{10,1... | collective-permute-start | bytes 1572872 | tf_op jit(solution)/shard_map/ppermute | solution.py:20
  33.1 12.0 %collective-permute-start.8 = (bf16[256,1024]{1,0:T(8,128)(2,1)S(1)}, bf16[256,1024]{1,0:T(8,128)(2,1)S(1)}, u32[]{:S(2)}, u32[]{:S(2)}) collective-permute-start(bf16[256,1024]{1,0:T(8,128)(2,1)S(1)} %collective-permute-done.7.refs_8_), channel_id=1, source_target_pairs={{0,7},{1,0},{2,1},{3,2},{4,3},{5,4},{6,5},{7,6},{8,15},{9,8},{10,9... | collective-permute-start | bytes 1572872 | tf_op jit(solution)/shard_map/ppermute | solution.py:20
  44.9 7.4 %collective-permute-start.6 = (bf16[128,1024]{1,0:T(8,128)(2,1)S(1)}, bf16[128,1024]{1,0:T(8,128)(2,1)S(1)}, u32[]{:S(2)}, u32[]{:S(2)}) collective-permute-start(bf16[128,1024]{1,0:T(8,128)(2,1)S(1)} %slice.64), channel_id=1, source_target_pairs={{0,1},{1,2},{2,3},{3,4},{4,5},{5,6},{6,7},{7,0},{8,9},{9,10},{10,1... | collective-permute-start | bytes 786440 | tf_op jit(solution)/shard_map/ppermute | solution.py:20
  45.1 7.2 %collective-permute-start.9 = (bf16[128,1024]{1,0:T(8,128)(2,1)S(1)}, bf16[128,1024]{1,0:T(8,128)(2,1)S(1)}, u32[]{:S(2)}, u32[]{:S(2)}) collective-permute-start(bf16[128,1024]{1,0:T(8,128)(2,1)S(1)} %slice.65), channel_id=1, source_target_pairs={{0,7},{1,0},{2,1},{3,2},{4,3},{5,4},{6,5},{7,6},{8,15},{9,8},{10,9... | collective-permute-start | bytes 786440 | tf_op jit(solution)/shard_map/ppermute | solution.py:20
  54.0 5.3 %collective-permute-start.14 = (f16[64,1024]{1,0:T(8,128)(2,1)S(1)}, f16[64,1024]{1,0:T(8,128)(2,1)S(1)}, u32[]{:S(2)}, u32[]{:S(2)}) collective-permute-start(f16[64,1024]{1,0:T(8,128)(2,1)S(1)} %convert_element_type.37), channel_id=1, source_target_pairs={{0,8},{8,16},{16,24},{24,0},{1,9},{9,17},{17,25},{25,1},{2,10},{10... | collective-permute-start | bytes 393224 | tf_op jit(solution)/shard_map/ppermute | solution.py:20
  54.6 6.5 %collective-permute-start.13 = (f16[64,1024]{1,0:T(8,128)(2,1)S(1)}, f16[64,1024]{1,0:T(8,128)(2,1)S(1)}, u32[]{:S(2)}, u32[]{:S(2)}) collective-permute-start(f16[64,1024]{1,0:T(8,128)(2,1)S(1)} %convert_element_type.35), channel_id=1, source_target_pairs={{0,16},{8,24},{16,0},{24,8},{1,17},{9,25},{17,1},{25,9},{2,18},{10... | collective-permute-start | bytes 393224 | tf_op jit(solution)/shard_map/ppermute | solution.py:20
  57.3 3.9 %collective-permute-start.12 = (f16[64,1024]{1,0:T(8,128)(2,1)S(1)}, f16[64,1024]{1,0:T(8,128)(2,1)S(1)}, u32[]{:S(2)}, u32[]{:S(2)}) collective-permute-start(f16[64,1024]{1,0:T(8,128)(2,1)S(1)} %convert_element_type.33), channel_id=1, source_target_pairs={{0,24},{8,0},{16,8},{24,16},{1,25},{9,1},{17,9},{25,17},{2,26},{10... | collective-permute-start | bytes 393224 | tf_op jit(solution)/shard_map/ppermute | solution.py:20
  61.4 7.9 %collective-permute-start.17 = (f16[64,1152]{1,0:T(8,128)(2,1)S(1)}, f16[64,1152]{1,0:T(8,128)(2,1)S(1)}, u32[]{:S(2)}, u32[]{:S(2)}) collective-permute-start(f16[64,1152]{1,0:T(8,128)(2,1)S(1)} %get-tuple-element.61), channel_id=1, source_target_pairs={{0,2},{1,3},{2,4},{3,5},{4,6},{5,7},{6,0},{7,1},{8,10},{9,11},{10,... | collective-permute-start | bytes 442376 | tf_op jit(solution)/shard_map/ppermute | solution.py:20
  61.5 8.4 %collective-permute-start.15 = (f16[64,1152]{1,0:T(8,128)(2,1)S(1)}, f16[64,1152]{1,0:T(8,128)(2,1)S(1)}, u32[]{:S(2)}, u32[]{:S(2)}) collective-permute-start(f16[64,1152]{1,0:T(8,128)(2,1)S(1)} %get-tuple-element.61), channel_id=1, source_target_pairs={{0,1},{1,2},{2,3},{3,4},{4,5},{5,6},{6,7},{7,0},{8,9},{9,10},{10,1... | collective-permute-start | bytes 442376 | tf_op jit(solution)/shard_map/ppermute | solution.py:20
  64.0 13.0 %collective-permute-start.20 = (bf16[512,512]{1,0:T(8,128)(2,1)S(1)}, bf16[512,512]{1,0:T(8,128)(2,1)S(1)}, u32[]{:S(2)}, u32[]{:S(2)}) collective-permute-start(bf16[512,512]{1,0:T(8,128)(2,1)S(1)} %slice.61), channel_id=1, source_target_pairs={{0,24},{8,0},{16,8},{24,16},{1,25},{9,1},{17,9},{25,17},{2,26},{10... | collective-permute-start | bytes 1572872 | tf_op jit(solution)/shard_map/ppermute | solution.py:20
  66.2 10.9 %collective-permute-start.19 = (bf16[512,512]{1,0:T(8,128)(2,1)S(1)}, bf16[512,512]{1,0:T(8,128)(2,1)S(1)}, u32[]{:S(2)}, u32[]{:S(2)}) collective-permute-start(bf16[512,512]{1,0:T(8,128)(2,1)S(1)} %slice.60), channel_id=1, source_target_pairs={{0,8},{8,16},{16,24},{24,0},{1,9},{9,17},{17,25},{25,1},{2,10},{10... | collective-permute-start | bytes 1572872 | tf_op jit(solution)/shard_map/ppermute | solution.py:20
  66.2 5.5 %collective-permute-start.16 = (f16[64,1152]{1,0:T(8,128)(2,1)S(1)}, f16[64,1152]{1,0:T(8,128)(2,1)S(1)}, u32[]{:S(2)}, u32[]{:S(2)}) collective-permute-start(f16[64,1152]{1,0:T(8,128)(2,1)S(1)} %get-tuple-element.61), channel_id=1, source_target_pairs={{0,7},{1,0},{2,1},{3,2},{4,3},{5,4},{6,5},{7,6},{8,15},{9,8},{10,9... | collective-permute-start | bytes 442376 | tf_op jit(solution)/shard_map/ppermute | solution.py:20
  69.3 6.3 %collective-permute-start.18 = (f16[64,1152]{1,0:T(8,128)(2,1)S(1)}, f16[64,1152]{1,0:T(8,128)(2,1)S(1)}, u32[]{:S(2)}, u32[]{:S(2)}) collective-permute-start(f16[64,1152]{1,0:T(8,128)(2,1)S(1)} %get-tuple-element.61), channel_id=1, source_target_pairs={{0,6},{1,7},{2,0},{3,1},{4,2},{5,3},{6,4},{7,5},{8,14},{9,15},{10,... | collective-permute-start | bytes 442376 | tf_op jit(solution)/shard_map/ppermute | solution.py:20
  69.8 11.1 %collective-permute-start.23 = (f16[64,1152]{1,0:T(8,128)(2,1)S(1)}, f16[64,1152]{1,0:T(8,128)(2,1)S(1)}, u32[]{:S(2)}, u32[]{:S(2)}) collective-permute-start(f16[64,1152]{1,0:T(8,128)(2,1)S(1)} %collective-permute-done.17), channel_id=1, source_target_pairs={{0,2},{1,3},{2,4},{3,5},{4,6},{5,7},{6,0},{7,1},{8,10},{9,11},{10,... | collective-permute-start | bytes 442376 | tf_op jit(solution)/shard_map/ppermute | solution.py:20
  71.7 10.9 %collective-permute-start.21 = (f16[64,1152]{1,0:T(8,128)(2,1)S(1)}, f16[64,1152]{1,0:T(8,128)(2,1)S(1)}, u32[]{:S(2)}, u32[]{:S(2)}) collective-permute-start(f16[64,1152]{1,0:T(8,128)(2,1)S(1)} %collective-permute-done.17), channel_id=1, source_target_pairs={{0,1},{1,2},{2,3},{3,4},{4,5},{5,6},{6,7},{7,0},{8,9},{9,10},{10,1... | collective-permute-start | bytes 442376 | tf_op jit(solution)/shard_map/ppermute | solution.py:20
  75.6 7.0 %collective-permute-start.22 = (f16[64,1152]{1,0:T(8,128)(2,1)S(1)}, f16[64,1152]{1,0:T(8,128)(2,1)S(1)}, u32[]{:S(2)}, u32[]{:S(2)}) collective-permute-start(f16[64,1152]{1,0:T(8,128)(2,1)S(1)} %collective-permute-done.18), channel_id=1, source_target_pairs={{0,7},{1,0},{2,1},{3,2},{4,3},{5,4},{6,5},{7,6},{8,15},{9,8},{10,9... | collective-permute-start | bytes 442376 | tf_op jit(solution)/shard_map/ppermute | solution.py:20
  (6 other events, 74.3 us)

commit v4 on v3

--- a/solution.py
+++ b/solution.py
@@ -348,11 +348,12 @@
     r1, l1 = ring(message, "z", Z, 1), ring(message, "z", Z, -1)
     r2, l2 = ring(message, "z", Z, 2), ring(message, "z", Z, -2)
     r3, l3 = ring(r2, "z", Z, 1), ring(l2, "z", Z, -1)
-    r4 = ring(r2, "z", Z, 2)
+    edge = CAP // 2
+    r4, l4 = ring(r2[:edge], "z", Z, 2), ring(l2[edge:], "z", Z, -2)
 
     stats = word_stats(where, *split([message, r1, l1, r2, l2], wide), tables)
-    stats, r3, l3, r4 = lax.optimization_barrier((stats, r3, l3, r4))
-    stats = word_stats(where, *split([r3, l3, r4], wide), tables, stats)
+    stats, r3, l3, r4, l4 = lax.optimization_barrier((stats, r3, l3, r4, l4))
+    stats = word_stats(where, *split([r3, l3, r4, l4], wide), tables, stats)
     stats = stats.reshape(SECTIONS * Z, 2, 128)
     stats = lax.all_to_all(stats, ("y", "core", "z"), 0, 0, tiled=True)
     loss = combine(ids, stats.reshape(SECTIONS, Z, 2, 128))

time: 113 us -> 112 us (level)
  starting transfers between devices: 32.4 us -> 37.9 us
  waiting for transfers between devices: 37.6 us -> 32.4 us
  blocking collectives: 25.9 us -> 24.7 us
    ppermute x24 -> x25, starting transfers between devices: 32.4 us -> 37.9 us  [ring(): lax.ppermute(array, axis, [(i, (i + step) % size) for i in range(size)])]
    ppermute x24 -> x25, waiting for transfers between devices: 37.6 us -> 32.4 us  [ring(): lax.ppermute(array, axis, [(i, (i + step) % size) for i in range(size)])]
    all_to_all x1, blocking collectives: 25.9 us -> 24.7 us  [body(): stats = lax.all_to_all(stats, ('y', 'core', 'z'), 0, 0, tiled=True)]
    unnamed x17 -> x18, local copies, waits for them, and re-layouts: 3.73 us -> 3.75 us
  transfers between devices with their start and end apart: 24 -> 25, of which waited for: 14 -> 12; matrix products, arithmetic and copies ran while one was open for 1% -> 1% of each run, Pallas kernels for 6% -> 6%
where the time goes in v4:
time: 112 us
  starting transfers between devices  37.9 us (34%)
  waiting for transfers between devices  32.4 us (29%)
  blocking collectives  24.7 us (22%)
  Pallas kernels  11.4 us (10%)
  local copies, waits for them, and re-layouts  3.99 us (4%)
    ppermute x25, starting transfers between devices, ring(): lax.ppermute(array, axis, [(i, (i + step) % size) for i in range(size)])  37.9 us
    ppermute x25, waiting for transfers between devices, ring(): lax.ppermute(array, axis, [(i, (i + step) % size) for i in range(size)])  32.4 us
    all_to_all x1, blocking collectives, body(): stats = lax.all_to_all(stats, ('y', 'core', 'z'), 0, 0, tiled=True)  24.7 us
    pallas_call x2, Pallas kernels, word_stats(): pl.pallas_call(lambda *refs: word_kernel(last, blocks, *refs), in_specs=[...  6.5 us
    unnamed x18, local copies, waits for them, and re-layouts  3.75 us
    pallas_call x1, Pallas kernels, select_rows(): pl.pallas_call(select_kernel, grid_spec=pltpu.PrefetchScalarGridSpec(num_...  2.37 us
  transfers between devices with their start and end apart: 25, of which 12 were waited for; matrix products, arithmetic and copies ran while one was open for 1% of the time, Pallas kernels for 6%

profile of v4, /device:TPU:1, one launch (start us, length us, event | category | flops | bytes accessed | tf_op | source)
XLA Modules:
  0.0 111.6 jit_solution(11599944647544432804)
XLA Ops:
  0.0 6.4 %collective-permute-start.3 = (bf16[256,1024]{1,0:T(8,128)(2,1)}, bf16[256,1024]{1,0:T(8,128)(2,1)S(1)}, u32[]{:S(2)}, u32[]{:S(2)}) collective-permute-start(bf16[256,1024]{1,0:T(8,128)(2,1)} %bitcast.13), channel_id=1, source_target_pairs={{0,7},{1,0},{2,1},{3,2},{4,3},{5,4},{6,5},{7,6},{8,15},{9,8},{10,9... | collective-permute-start | bytes 1572872 | tf_op jit(solution)/shard_map/ppermute | solution.py:20
  6.5 2.2 %copy-done = bf16[256,8192]{1,0:T(8,128)(2,1)S(1)} copy-done((bf16[256,8192]{1,0:T(8,128)(2,1)S(1)}, bf16[256,8192]{1,0:T(8,128)(2,1)}, u32[]{:S(2)}) %copy-start) | copy-done | bytes 4194328
  10.0 2.4 %shard_map.55 = (bf16[64,2048]{1,0:T(8,128)(2,1)S(1)}, bf16[64,3072]{1,0:T(8,128)(2,1)S(1)}, bf16[64,3072]{1,0:T(8,128)(2,1)S(1)}, f32[64,128]{1,0:T(8,128)S(1)}) custom-call(s32[3]{0:T(128)S(1)} %pad_add_fusion.where_ref.refs_0_, s32[1,256]{1,0:T(1,128)S(1)} %bitcast.18, s32[1,256]{1,0:T(1,128)S(1)} %bitcast.20, bf16[256,8192]{1,0:T(8,128)(2,1)S(1)} %copy-done), custom_call_target="tpu_custom_call" | custom-call | flops 268435456 | bytes 4194304 | tf_op jit(solution)/shard_map/pallas_call | solution.py:90
  15.2 2.1 %collective-permute-done.3.refs_6_ = bf16[256,1024]{1,0:T(8,128)(2,1)S(1)} collective-permute-done((bf16[256,1024]{1,0:T(8,128)(2,1)}, bf16[256,1024]{1,0:T(8,128)(2,1)S(1)}, u32[]{:S(2)}, u32[]{:S(2)}) %collective-permute-start.3) | collective-permute-done | bytes 524320 | tf_op jit(solution)/shard_map/ppermute | solution.py:20
  17.3 3.0 %collective-permute-done.2.refs_5_ = bf16[256,1024]{1,0:T(8,128)(2,1)S(1)} collective-permute-done((bf16[256,1024]{1,0:T(8,128)(2,1)}, bf16[256,1024]{1,0:T(8,128)(2,1)S(1)}, u32[]{:S(2)}, u32[]{:S(2)}) %collective-permute-start.2) | collective-permute-done | bytes 524320 | tf_op jit(solution)/shard_map/ppermute | solution.py:20
  20.3 2.7 %collective-permute-start.7 = (bf16[256,1024]{1,0:T(8,128)(2,1)S(1)}, bf16[256,1024]{1,0:T(8,128)(2,1)S(1)}, u32[]{:S(2)}, u32[]{:S(2)}) collective-permute-start(bf16[256,1024]{1,0:T(8,128)(2,1)S(1)} %collective-permute-done.3.refs_6_), channel_id=1, source_target_pairs={{0,7},{1,0},{2,1},{3,2},{4,3},{5,4},{6,5},{7,6},{8,15},{9,8},{10,9... | collective-permute-start | bytes 1572872 | tf_op jit(solution)/shard_map/ppermute | solution.py:20
  23.6 2.5 %collective-permute-start.11 = (bf16[1152,512]{1,0:T(8,128)(2,1)S(1)}, bf16[1152,512]{1,0:T(8,128)(2,1)S(1)}, u32[]{:S(2)}, u32[]{:S(2)}) collective-permute-start(bf16[1152,512]{1,0:T(8,128)(2,1)S(1)} %get-tuple-element.53), channel_id=1, source_target_pairs={{0,24},{8,0},{16,8},{24,16},{1,25},{9,1},{17,9},{25,17},{2,26},{10... | collective-permute-start | bytes 3538952 | tf_op jit(solution)/shard_map/ppermute | solution.py:20
  26.1 7.0 %collective-permute-done.4.refs_7_ = bf16[256,1024]{1,0:T(8,128)(2,1)S(1)} collective-permute-done((bf16[256,1024]{1,0:T(8,128)(2,1)S(1)}, bf16[256,1024]{1,0:T(8,128)(2,1)S(1)}, u32[]{:S(2)}, u32[]{:S(2)}) %collective-permute-start.4) | collective-permute-done | bytes 524320 | tf_op jit(solution)/shard_map/ppermute | solution.py:20
  33.1 2.7 %collective-permute-start.8 = (bf16[256,1024]{1,0:T(8,128)(2,1)S(1)}, bf16[256,1024]{1,0:T(8,128)(2,1)S(1)}, u32[]{:S(2)}, u32[]{:S(2)}) collective-permute-start(bf16[256,1024]{1,0:T(8,128)(2,1)S(1)} %collective-permute-done.7.refs_8_), channel_id=1, source_target_pairs={{0,7},{1,0},{2,1},{3,2},{4,3},{5,4},{6,5},{7,6},{8,15},{9,8},{10,9... | collective-permute-start | bytes 1572872 | tf_op jit(solution)/shard_map/ppermute | solution.py:20
  35.7 9.2 %collective-permute-done.5.refs_9_ = bf16[256,1024]{1,0:T(8,128)(2,1)S(1)} collective-permute-done((bf16[256,1024]{1,0:T(8,128)(2,1)S(1)}, bf16[256,1024]{1,0:T(8,128)(2,1)S(1)}, u32[]{:S(2)}, u32[]{:S(2)}) %collective-permute-start.5) | collective-permute-done | bytes 524320 | tf_op jit(solution)/shard_map/ppermute | solution.py:20
  45.1 2.7 %collective-permute-start.9 = (bf16[128,1024]{1,0:T(8,128)(2,1)S(1)}, bf16[128,1024]{1,0:T(8,128)(2,1)S(1)}, u32[]{:S(2)}, u32[]{:S(2)}) collective-permute-start(bf16[128,1024]{1,0:T(8,128)(2,1)S(1)} %slice.73), channel_id=1, source_target_pairs={{0,7},{1,0},{2,1},{3,2},{4,3},{5,4},{6,5},{7,6},{8,15},{9,8},{10,9... | collective-permute-start | bytes 786440 | tf_op jit(solution)/shard_map/ppermute | solution.py:20
  49.1 3.1 %collective-permute-done.10.refs_4_ = bf16[1152,512]{1,0:T(8,128)(2,1)S(1)} collective-permute-done((bf16[1152,512]{1,0:T(8,128)(2,1)S(1)}, bf16[1152,512]{1,0:T(8,128)(2,1)S(1)}, u32[]{:S(2)}, u32[]{:S(2)}) %collective-permute-start.10) | collective-permute-done | bytes 1179680 | tf_op jit(solution)/shard_map/ppermute | solution.py:20
  54.6 2.8 %collective-permute-start.13 = (f16[64,1024]{1,0:T(8,128)(2,1)S(1)}, f16[64,1024]{1,0:T(8,128)(2,1)S(1)}, u32[]{:S(2)}, u32[]{:S(2)}) collective-permute-start(f16[64,1024]{1,0:T(8,128)(2,1)S(1)} %convert_element_type.35), channel_id=1, source_target_pairs={{0,16},{8,24},{16,0},{24,8},{1,17},{9,25},{17,1},{25,9},{2,18},{10... | collective-permute-start | bytes 393224 | tf_op jit(solution)/shard_map/ppermute | solution.py:20
  59.3 1.8 %collective-permute-done.13 = f16[64,1024]{1,0:T(8,128)(2,1)S(1)} collective-permute-done((f16[64,1024]{1,0:T(8,128)(2,1)S(1)}, f16[64,1024]{1,0:T(8,128)(2,1)S(1)}, u32[]{:S(2)}, u32[]{:S(2)}) %collective-permute-start.13) | collective-permute-done | bytes 131104 | tf_op jit(solution)/shard_map/ppermute | solution.py:20
  61.5 3.6 %collective-permute-start.18 = (f16[64,1152]{1,0:T(8,128)(2,1)S(1)}, f16[64,1152]{1,0:T(8,128)(2,1)S(1)}, u32[]{:S(2)}, u32[]{:S(2)}) collective-permute-start(f16[64,1152]{1,0:T(8,128)(2,1)S(1)} %get-tuple-element.63), channel_id=1, source_target_pairs={{0,6},{1,7},{2,0},{3,1},{4,2},{5,3},{6,4},{7,5},{8,14},{9,15},{10,... | collective-permute-start | bytes 442376 | tf_op jit(solution)/shard_map/ppermute | solution.py:20
  65.5 2.1 %collective-permute-start.20 = (bf16[512,512]{1,0:T(8,128)(2,1)S(1)}, bf16[512,512]{1,0:T(8,128)(2,1)S(1)}, u32[]{:S(2)}, u32[]{:S(2)}) collective-permute-start(bf16[512,512]{1,0:T(8,128)(2,1)S(1)} %slice.67), channel_id=1, source_target_pairs={{0,24},{8,0},{16,8},{24,16},{1,25},{9,1},{17,9},{25,17},{2,26},{10... | collective-permute-start | bytes 1572872 | tf_op jit(solution)/shard_map/ppermute | solution.py:20
  67.6 1.6 %collective-permute-done.17 = f16[64,1152]{1,0:T(8,128)(2,1)S(1)} collective-permute-done((f16[64,1152]{1,0:T(8,128)(2,1)S(1)}, f16[64,1152]{1,0:T(8,128)(2,1)S(1)}, u32[]{:S(2)}, u32[]{:S(2)}) %collective-permute-start.17) | collective-permute-done | bytes 147488 | tf_op jit(solution)/shard_map/ppermute | solution.py:20
  70.3 1.5 %collective-permute-start.23 = (f16[32,1152]{1,0:T(8,128)(2,1)S(1)}, f16[32,1152]{1,0:T(8,128)(2,1)S(1)}, u32[]{:S(2)}, u32[]{:S(2)}) collective-permute-start(f16[32,1152]{1,0:T(8,128)(2,1)S(1)} %slice.76), channel_id=1, source_target_pairs={{0,2},{1,3},{2,4},{3,5},{4,6},{5,7},{6,0},{7,1},{8,10},{9,11},{10,... | collective-permute-start | bytes 221192 | tf_op jit(solution)/shard_map/ppermute | solution.py:20
  71.8 2.3 %collective-permute-start.24 = (f16[32,1152]{1,0:T(8,128)(2,1)S(1)}, f16[32,1152]{1,0:T(8,128)(2,1)S(1)}, u32[]{:S(2)}, u32[]{:S(2)}) collective-permute-start(f16[32,1152]{1,0:T(8,128)(2,1)S(1)} %slice.77), channel_id=1, source_target_pairs={{0,6},{1,7},{2,0},{3,1},{4,2},{5,3},{6,4},{7,5},{8,14},{9,15},{10,... | collective-permute-start | bytes 221192 | tf_op jit(solution)/shard_map/ppermute | solution.py:20
  74.1 1.5 %collective-permute-done.16 = f16[64,1152]{1,0:T(8,128)(2,1)S(1)} collective-permute-done((f16[64,1152]{1,0:T(8,128)(2,1)S(1)}, f16[64,1152]{1,0:T(8,128)(2,1)S(1)}, u32[]{:S(2)}, u32[]{:S(2)}) %collective-permute-start.16) | collective-permute-done | bytes 147488 | tf_op jit(solution)/shard_map/ppermute | solution.py:20
  76.9 2.2 %collective-permute-start.22 = (f16[64,1152]{1,0:T(8,128)(2,1)S(1)}, f16[64,1152]{1,0:T(8,128)(2,1)S(1)}, u32[]{:S(2)}, u32[]{:S(2)}) collective-permute-start(f16[64,1152]{1,0:T(8,128)(2,1)S(1)} %collective-permute-done.18), channel_id=1, source_target_pairs={{0,7},{1,0},{2,1},{3,2},{4,3},{5,4},{6,5},{7,6},{8,15},{9,8},{10,9... | collective-permute-start | bytes 442376 | tf_op jit(solution)/shard_map/ppermute | solution.py:20
  79.1 3.8 %shard_map.58.refs_8_ = f32[5,2,128]{2,1,0:T(2,128)S(1)} custom-call(s32[3]{0:T(128)S(1)} %pad_add_fusion.where_ref.refs_0_, bf16[640,1024]{1,0:T(8,128)(2,1)S(1)} %pad_maximum_fusion.refs_1_, f32[320,128]{1,0:T(8,128)S(1)} %slice_convert_fusion.refs_2_, bf16[1024,512]{1,0:T(8,128)(2,1)S(1)} %bitcast.11, ...), custom_call_target="tpu_custom_call" | custom-call | flops 2684354560 | bytes 4194304 | tf_op jit(solution)/shard_map/pallas_call | solution.py:238
  83.3 2.7 %shard_map.59 = f32[8,8,2,128]{3,2,1,0:T(2,128)S(1)} custom-call(s32[3]{0:T(128)S(1)} %pad_add_fusion.where_ref.refs_0_, bf16[384,1024]{1,0:T(8,128)(2,1)S(1)} %pad_maximum_fusion.3.refs_1_, f32[192,128]{1,0:T(8,128)S(1)} %slice_convert_fusion.1.refs_2_, bf16[1024,512]{1,0:T(8,128)(2,1)S(1)} %bitcast.12, ...), custom_call_target="tpu_custom_call" | custom-call | flops 1610612736 | bytes 4194304 | tf_op jit(solution)/shard_map/pallas_call | solution.py:238
  86.0 24.7 %all_to_all.5 = f32[64,2,128]{2,1,0:T(2,128)S(1)} all-to-all(f32[64,2,128]{2,1,0:T(2,128)S(1)} %bitcast.17), channel_id=1, replica_groups=mesh['y'=4,'core'=2,'x'=4,'z'=8] {'y','core','z'}, dimensions={0} | all-to-all | bytes 131072 | tf_op jit(solution)/shard_map/all_to_all | solution.py:358
  (77 shorter events, 14.8 us)
Async XLA Ops:
  0.0 17.3 %collective-permute-start.3 = (bf16[256,1024]{1,0:T(8,128)(2,1)}, bf16[256,1024]{1,0:T(8,128)(2,1)S(1)}, u32[]{:S(2)}, u32[]{:S(2)}) collective-permute-start(bf16[256,1024]{1,0:T(8,128)(2,1)} %bitcast.13), channel_id=1, source_target_pairs={{0,7},{1,0},{2,1},{3,2},{4,3},{5,4},{6,5},{7,6},{8,15},{9,8},{10,9... | collective-permute-start | bytes 1572872 | tf_op jit(solution)/shard_map/ppermute | solution.py:20
  6.4 13.9 %collective-permute-start.2 = (bf16[256,1024]{1,0:T(8,128)(2,1)}, bf16[256,1024]{1,0:T(8,128)(2,1)S(1)}, u32[]{:S(2)}, u32[]{:S(2)}) collective-permute-start(bf16[256,1024]{1,0:T(8,128)(2,1)} %bitcast.14), channel_id=1, source_target_pairs={{0,1},{1,2},{2,3},{3,4},{4,5},{5,6},{6,7},{7,0},{8,9},{9,10},{10,1... | collective-permute-start | bytes 1572872 | tf_op jit(solution)/shard_map/ppermute | solution.py:20
  12.4 10.9 %collective-permute-start = (bf16[64,3072]{1,0:T(8,128)(2,1)S(1)}, bf16[64,3072]{1,0:T(8,128)(2,1)S(1)}, u32[]{:S(2)}, u32[]{:S(2)}) collective-permute-start(bf16[64,3072]{1,0:T(8,128)(2,1)S(1)} %get-tuple-element.28), channel_id=1, source_target_pairs={{0,8},{8,16},{16,24},{24,0},{1,9},{9,17},{17,25},{25,1},{2,10},{10... | collective-permute-start | bytes 1179656 | tf_op jit(solution)/shard_map/ppermute | solution.py:20
  13.7 9.7 %collective-permute-start.1 = (bf16[64,3072]{1,0:T(8,128)(2,1)S(1)}, bf16[64,3072]{1,0:T(8,128)(2,1)S(1)}, u32[]{:S(2)}, u32[]{:S(2)}) collective-permute-start(bf16[64,3072]{1,0:T(8,128)(2,1)S(1)} %get-tuple-element.29), channel_id=1, source_target_pairs={{0,24},{8,0},{16,8},{24,16},{1,25},{9,1},{17,9},{25,17},{2,26},{10... | collective-permute-start | bytes 1179656 | tf_op jit(solution)/shard_map/ppermute | solution.py:20
  20.3 12.8 %collective-permute-start.4 = (bf16[256,1024]{1,0:T(8,128)(2,1)S(1)}, bf16[256,1024]{1,0:T(8,128)(2,1)S(1)}, u32[]{:S(2)}, u32[]{:S(2)}) collective-permute-start(bf16[256,1024]{1,0:T(8,128)(2,1)S(1)} %collective-permute-done.2.refs_5_), channel_id=1, source_target_pairs={{0,1},{1,2},{2,3},{3,4},{4,5},{5,6},{6,7},{7,0},{8,9},{9,10},{10,1... | collective-permute-start | bytes 1572872 | tf_op jit(solution)/shard_map/ppermute | solution.py:20
  20.3 12.8 %collective-permute-start.7 = (bf16[256,1024]{1,0:T(8,128)(2,1)S(1)}, bf16[256,1024]{1,0:T(8,128)(2,1)S(1)}, u32[]{:S(2)}, u32[]{:S(2)}) collective-permute-start(bf16[256,1024]{1,0:T(8,128)(2,1)S(1)} %collective-permute-done.3.refs_6_), channel_id=1, source_target_pairs={{0,7},{1,0},{2,1},{3,2},{4,3},{5,4},{6,5},{7,6},{8,15},{9,8},{10,9... | collective-permute-start | bytes 1572872 | tf_op jit(solution)/shard_map/ppermute | solution.py:20
  23.6 25.6 %collective-permute-start.11 = (bf16[1152,512]{1,0:T(8,128)(2,1)S(1)}, bf16[1152,512]{1,0:T(8,128)(2,1)S(1)}, u32[]{:S(2)}, u32[]{:S(2)}) collective-permute-start(bf16[1152,512]{1,0:T(8,128)(2,1)S(1)} %get-tuple-element.53), channel_id=1, source_target_pairs={{0,24},{8,0},{16,8},{24,16},{1,25},{9,1},{17,9},{25,17},{2,26},{10... | collective-permute-start | bytes 3538952 | tf_op jit(solution)/shard_map/ppermute | solution.py:20
  26.0 26.2 %collective-permute-start.10 = (bf16[1152,512]{1,0:T(8,128)(2,1)S(1)}, bf16[1152,512]{1,0:T(8,128)(2,1)S(1)}, u32[]{:S(2)}, u32[]{:S(2)}) collective-permute-start(bf16[1152,512]{1,0:T(8,128)(2,1)S(1)} %get-tuple-element.54), channel_id=1, source_target_pairs={{0,8},{8,16},{16,24},{24,0},{1,9},{9,17},{17,25},{25,1},{2,10},{10... | collective-permute-start | bytes 3538952 | tf_op jit(solution)/shard_map/ppermute | solution.py:20
  33.1 11.8 %collective-permute-start.5 = (bf16[256,1024]{1,0:T(8,128)(2,1)S(1)}, bf16[256,1024]{1,0:T(8,128)(2,1)S(1)}, u32[]{:S(2)}, u32[]{:S(2)}) collective-permute-start(bf16[256,1024]{1,0:T(8,128)(2,1)S(1)} %collective-permute-done.4.refs_7_), channel_id=1, source_target_pairs={{0,1},{1,2},{2,3},{3,4},{4,5},{5,6},{6,7},{7,0},{8,9},{9,10},{10,1... | collective-permute-start | bytes 1572872 | tf_op jit(solution)/shard_map/ppermute | solution.py:20
  33.1 12.0 %collective-permute-start.8 = (bf16[256,1024]{1,0:T(8,128)(2,1)S(1)}, bf16[256,1024]{1,0:T(8,128)(2,1)S(1)}, u32[]{:S(2)}, u32[]{:S(2)}) collective-permute-start(bf16[256,1024]{1,0:T(8,128)(2,1)S(1)} %collective-permute-done.7.refs_8_), channel_id=1, source_target_pairs={{0,7},{1,0},{2,1},{3,2},{4,3},{5,4},{6,5},{7,6},{8,15},{9,8},{10,9... | collective-permute-start | bytes 1572872 | tf_op jit(solution)/shard_map/ppermute | solution.py:20
  44.9 7.4 %collective-permute-start.6 = (bf16[128,1024]{1,0:T(8,128)(2,1)S(1)}, bf16[128,1024]{1,0:T(8,128)(2,1)S(1)}, u32[]{:S(2)}, u32[]{:S(2)}) collective-permute-start(bf16[128,1024]{1,0:T(8,128)(2,1)S(1)} %slice.72), channel_id=1, source_target_pairs={{0,1},{1,2},{2,3},{3,4},{4,5},{5,6},{6,7},{7,0},{8,9},{9,10},{10,1... | collective-permute-start | bytes 786440 | tf_op jit(solution)/shard_map/ppermute | solution.py:20
  45.1 7.2 %collective-permute-start.9 = (bf16[128,1024]{1,0:T(8,128)(2,1)S(1)}, bf16[128,1024]{1,0:T(8,128)(2,1)S(1)}, u32[]{:S(2)}, u32[]{:S(2)}) collective-permute-start(bf16[128,1024]{1,0:T(8,128)(2,1)S(1)} %slice.73), channel_id=1, source_target_pairs={{0,7},{1,0},{2,1},{3,2},{4,3},{5,4},{6,5},{7,6},{8,15},{9,8},{10,9... | collective-permute-start | bytes 786440 | tf_op jit(solution)/shard_map/ppermute | solution.py:20
  54.0 5.3 %collective-permute-start.14 = (f16[64,1024]{1,0:T(8,128)(2,1)S(1)}, f16[64,1024]{1,0:T(8,128)(2,1)S(1)}, u32[]{:S(2)}, u32[]{:S(2)}) collective-permute-start(f16[64,1024]{1,0:T(8,128)(2,1)S(1)} %convert_element_type.37), channel_id=1, source_target_pairs={{0,8},{8,16},{16,24},{24,0},{1,9},{9,17},{17,25},{25,1},{2,10},{10... | collective-permute-start | bytes 393224 | tf_op jit(solution)/shard_map/ppermute | solution.py:20
  54.6 6.5 %collective-permute-start.13 = (f16[64,1024]{1,0:T(8,128)(2,1)S(1)}, f16[64,1024]{1,0:T(8,128)(2,1)S(1)}, u32[]{:S(2)}, u32[]{:S(2)}) collective-permute-start(f16[64,1024]{1,0:T(8,128)(2,1)S(1)} %convert_element_type.35), channel_id=1, source_target_pairs={{0,16},{8,24},{16,0},{24,8},{1,17},{9,25},{17,1},{25,9},{2,18},{10... | collective-permute-start | bytes 393224 | tf_op jit(solution)/shard_map/ppermute | solution.py:20
  61.4 7.9 %collective-permute-start.17 = (f16[64,1152]{1,0:T(8,128)(2,1)S(1)}, f16[64,1152]{1,0:T(8,128)(2,1)S(1)}, u32[]{:S(2)}, u32[]{:S(2)}) collective-permute-start(f16[64,1152]{1,0:T(8,128)(2,1)S(1)} %get-tuple-element.63), channel_id=1, source_target_pairs={{0,2},{1,3},{2,4},{3,5},{4,6},{5,7},{6,0},{7,1},{8,10},{9,11},{10,... | collective-permute-start | bytes 442376 | tf_op jit(solution)/shard_map/ppermute | solution.py:20
  61.5 8.8 %collective-permute-start.18 = (f16[64,1152]{1,0:T(8,128)(2,1)S(1)}, f16[64,1152]{1,0:T(8,128)(2,1)S(1)}, u32[]{:S(2)}, u32[]{:S(2)}) collective-permute-start(f16[64,1152]{1,0:T(8,128)(2,1)S(1)} %get-tuple-element.63), channel_id=1, source_target_pairs={{0,6},{1,7},{2,0},{3,1},{4,2},{5,3},{6,4},{7,5},{8,14},{9,15},{10,... | collective-permute-start | bytes 442376 | tf_op jit(solution)/shard_map/ppermute | solution.py:20
  65.0 6.8 %collective-permute-start.15 = (f16[64,1152]{1,0:T(8,128)(2,1)S(1)}, f16[64,1152]{1,0:T(8,128)(2,1)S(1)}, u32[]{:S(2)}, u32[]{:S(2)}) collective-permute-start(f16[64,1152]{1,0:T(8,128)(2,1)S(1)} %get-tuple-element.63), channel_id=1, source_target_pairs={{0,1},{1,2},{2,3},{3,4},{4,5},{5,6},{6,7},{7,0},{8,9},{9,10},{10,1... | collective-permute-start | bytes 442376 | tf_op jit(solution)/shard_map/ppermute | solution.py:20
  65.5 11.4 %collective-permute-start.20 = (bf16[512,512]{1,0:T(8,128)(2,1)S(1)}, bf16[512,512]{1,0:T(8,128)(2,1)S(1)}, u32[]{:S(2)}, u32[]{:S(2)}) collective-permute-start(bf16[512,512]{1,0:T(8,128)(2,1)S(1)} %slice.67), channel_id=1, source_target_pairs={{0,24},{8,0},{16,8},{24,16},{1,25},{9,1},{17,9},{25,17},{2,26},{10... | collective-permute-start | bytes 1572872 | tf_op jit(solution)/shard_map/ppermute | solution.py:20
  67.6 11.4 %collective-permute-start.19 = (bf16[512,512]{1,0:T(8,128)(2,1)S(1)}, bf16[512,512]{1,0:T(8,128)(2,1)S(1)}, u32[]{:S(2)}, u32[]{:S(2)}) collective-permute-start(bf16[512,512]{1,0:T(8,128)(2,1)S(1)} %slice.66), channel_id=1, source_target_pairs={{0,8},{8,16},{16,24},{24,0},{1,9},{9,17},{17,25},{25,1},{2,10},{10... | collective-permute-start | bytes 1572872 | tf_op jit(solution)/shard_map/ppermute | solution.py:20
  69.3 6.3 %collective-permute-start.16 = (f16[64,1152]{1,0:T(8,128)(2,1)S(1)}, f16[64,1152]{1,0:T(8,128)(2,1)S(1)}, u32[]{:S(2)}, u32[]{:S(2)}) collective-permute-start(f16[64,1152]{1,0:T(8,128)(2,1)S(1)} %get-tuple-element.63), channel_id=1, source_target_pairs={{0,7},{1,0},{2,1},{3,2},{4,3},{5,4},{6,5},{7,6},{8,15},{9,8},{10,9... | collective-permute-start | bytes 442376 | tf_op jit(solution)/shard_map/ppermute | solution.py:20
  70.3 12.6 %collective-permute-start.23 = (f16[32,1152]{1,0:T(8,128)(2,1)S(1)}, f16[32,1152]{1,0:T(8,128)(2,1)S(1)}, u32[]{:S(2)}, u32[]{:S(2)}) collective-permute-start(f16[32,1152]{1,0:T(8,128)(2,1)S(1)} %slice.76), channel_id=1, source_target_pairs={{0,2},{1,3},{2,4},{3,5},{4,6},{5,7},{6,0},{7,1},{8,10},{9,11},{10,... | collective-permute-start | bytes 221192 | tf_op jit(solution)/shard_map/ppermute | solution.py:20
  71.8 11.1 %collective-permute-start.24 = (f16[32,1152]{1,0:T(8,128)(2,1)S(1)}, f16[32,1152]{1,0:T(8,128)(2,1)S(1)}, u32[]{:S(2)}, u32[]{:S(2)}) collective-permute-start(f16[32,1152]{1,0:T(8,128)(2,1)S(1)} %slice.77), channel_id=1, source_target_pairs={{0,6},{1,7},{2,0},{3,1},{4,2},{5,3},{6,4},{7,5},{8,14},{9,15},{10,... | collective-permute-start | bytes 221192 | tf_op jit(solution)/shard_map/ppermute | solution.py:20
  75.6 7.3 %collective-permute-start.21 = (f16[64,1152]{1,0:T(8,128)(2,1)S(1)}, f16[64,1152]{1,0:T(8,128)(2,1)S(1)}, u32[]{:S(2)}, u32[]{:S(2)}) collective-permute-start(f16[64,1152]{1,0:T(8,128)(2,1)S(1)} %collective-permute-done.17), channel_id=1, source_target_pairs={{0,1},{1,2},{2,3},{3,4},{4,5},{5,6},{6,7},{7,0},{8,9},{9,10},{10,1... | collective-permute-start | bytes 442376 | tf_op jit(solution)/shard_map/ppermute | solution.py:20
  76.9 6.1 %collective-permute-start.22 = (f16[64,1152]{1,0:T(8,128)(2,1)S(1)}, f16[64,1152]{1,0:T(8,128)(2,1)S(1)}, u32[]{:S(2)}, u32[]{:S(2)}) collective-permute-start(f16[64,1152]{1,0:T(8,128)(2,1)S(1)} %collective-permute-done.18), channel_id=1, source_target_pairs={{0,7},{1,0},{2,1},{3,2},{4,3},{5,4},{6,5},{7,6},{8,15},{9,8},{10,9... | collective-permute-start | bytes 442376 | tf_op jit(solution)/shard_map/ppermute | solution.py:20
  (7 other events, 77.0 us)

commit v5 on v4

--- a/solution.py
+++ b/solution.py
@@ -341,7 +341,7 @@
     total = project_first(rows, chunks, [0, 7, 1, 6, 2, 5, 3])
     parts = project_last(total, rows, front, back, F32)
     own = parts[0]
-    for k in range(1, X):
+    for k in (1, 3, 2):
         own = own + ring(parts[k].astype(F16), "x", X, -k).astype(F32)
 
     message = jnp.concatenate([own, words], axis=1).astype(F16)

time: 112 us -> 111 us (level)
  waiting for transfers between devices: 32.4 us -> 29.1 us
  starting transfers between devices: 37.9 us -> 40.5 us
    ppermute x25, waiting for transfers between devices: 32.4 us -> 29.1 us  [ring(): lax.ppermute(array, axis, [(i, (i + step) % size) for i in range(size)])]
    ppermute x25, starting transfers between devices: 37.9 us -> 40.5 us  [ring(): lax.ppermute(array, axis, [(i, (i + step) % size) for i in range(size)])]
  transfers between devices with their start and end apart: 25 -> 25, of which waited for: 12 -> 10; matrix products, arithmetic and copies ran while one was open for 1% -> 1% of each run, Pallas kernels for 6% -> 6%
where the time goes in v5:
time: 111 us
  starting transfers between devices  40.5 us (36%)
  waiting for transfers between devices  29.1 us (26%)
  blocking collectives  24.7 us (22%)
  Pallas kernels  11.4 us (10%)
  local copies, waits for them, and re-layouts  3.99 us (4%)
    ppermute x25, starting transfers between devices, ring(): lax.ppermute(array, axis, [(i, (i + step) % size) for i in range(size)])  40.5 us
    ppermute x25, waiting for transfers between devices, ring(): lax.ppermute(array, axis, [(i, (i + step) % size) for i in range(size)])  29.1 us
    all_to_all x1, blocking collectives, body(): stats = lax.all_to_all(stats, ('y', 'core', 'z'), 0, 0, tiled=True)  24.7 us
    pallas_call x2, Pallas kernels, word_stats(): pl.pallas_call(lambda *refs: word_kernel(last, blocks, *refs), in_specs=[...  6.51 us
    unnamed x18, local copies, waits for them, and re-layouts  3.75 us
    pallas_call x1, Pallas kernels, select_rows(): pl.pallas_call(select_kernel, grid_spec=pltpu.PrefetchScalarGridSpec(num_...  2.37 us
  transfers between devices with their start and end apart: 25, of which 10 were waited for; matrix products, arithmetic and copies ran while one was open for 1% of the time, Pallas kernels for 6%

profile of v5, /device:TPU:1, one launch (start us, length us, event | category | flops | bytes accessed | tf_op | source)
XLA Modules:
  0.0 111.0 jit_solution(12836909712880042036)
XLA Ops:
  0.0 6.4 %collective-permute-start.3 = (bf16[256,1024]{1,0:T(8,128)(2,1)}, bf16[256,1024]{1,0:T(8,128)(2,1)S(1)}, u32[]{:S(2)}, u32[]{:S(2)}) collective-permute-start(bf16[256,1024]{1,0:T(8,128)(2,1)} %bitcast.13), channel_id=1, source_target_pairs={{0,7},{1,0},{2,1},{3,2},{4,3},{5,4},{6,5},{7,6},{8,15},{9,8},{10,9... | collective-permute-start | bytes 1572872 | tf_op jit(solution)/shard_map/ppermute | solution.py:20
  6.5 2.2 %copy-done = bf16[256,8192]{1,0:T(8,128)(2,1)S(1)} copy-done((bf16[256,8192]{1,0:T(8,128)(2,1)S(1)}, bf16[256,8192]{1,0:T(8,128)(2,1)}, u32[]{:S(2)}) %copy-start) | copy-done | bytes 4194328
  10.0 2.4 %shard_map.55 = (bf16[64,2048]{1,0:T(8,128)(2,1)S(1)}, bf16[64,3072]{1,0:T(8,128)(2,1)S(1)}, bf16[64,3072]{1,0:T(8,128)(2,1)S(1)}, f32[64,128]{1,0:T(8,128)S(1)}) custom-call(s32[3]{0:T(128)S(1)} %pad_add_fusion.where_ref.refs_0_, s32[1,256]{1,0:T(1,128)S(1)} %bitcast.18, s32[1,256]{1,0:T(1,128)S(1)} %bitcast.20, bf16[256,8192]{1,0:T(8,128)(2,1)S(1)} %copy-done), custom_call_target="tpu_custom_call" | custom-call | flops 268435456 | bytes 4194304 | tf_op jit(solution)/shard_map/pallas_call | solution.py:90
  13.7 1.5 %collective-permute-start.1 = (bf16[64,3072]{1,0:T(8,128)(2,1)S(1)}, bf16[64,3072]{1,0:T(8,128)(2,1)S(1)}, u32[]{:S(2)}, u32[]{:S(2)}) collective-permute-start(bf16[64,3072]{1,0:T(8,128)(2,1)S(1)} %get-tuple-element.29), channel_id=1, source_target_pairs={{0,24},{8,0},{16,8},{24,16},{1,25},{9,1},{17,9},{25,17},{2,26},{10... | collective-permute-start | bytes 1179656 | tf_op jit(solution)/shard_map/ppermute | solution.py:20
  15.2 2.1 %collective-permute-done.3.refs_6_ = bf16[256,1024]{1,0:T(8,128)(2,1)S(1)} collective-permute-done((bf16[256,1024]{1,0:T(8,128)(2,1)}, bf16[256,1024]{1,0:T(8,128)(2,1)S(1)}, u32[]{:S(2)}, u32[]{:S(2)}) %collective-permute-start.3) | collective-permute-done | bytes 524320 | tf_op jit(solution)/shard_map/ppermute | solution.py:20
  17.3 3.0 %collective-permute-done.2.refs_5_ = bf16[256,1024]{1,0:T(8,128)(2,1)S(1)} collective-permute-done((bf16[256,1024]{1,0:T(8,128)(2,1)}, bf16[256,1024]{1,0:T(8,128)(2,1)S(1)}, u32[]{:S(2)}, u32[]{:S(2)}) %collective-permute-start.2) | collective-permute-done | bytes 524320 | tf_op jit(solution)/shard_map/ppermute | solution.py:20
  20.3 2.7 %collective-permute-start.7 = (bf16[256,1024]{1,0:T(8,128)(2,1)S(1)}, bf16[256,1024]{1,0:T(8,128)(2,1)S(1)}, u32[]{:S(2)}, u32[]{:S(2)}) collective-permute-start(bf16[256,1024]{1,0:T(8,128)(2,1)S(1)} %collective-permute-done.3.refs_6_), channel_id=1, source_target_pairs={{0,7},{1,0},{2,1},{3,2},{4,3},{5,4},{6,5},{7,6},{8,15},{9,8},{10,9... | collective-permute-start | bytes 1572872 | tf_op jit(solution)/shard_map/ppermute | solution.py:20
  23.6 2.5 %collective-permute-start.11 = (bf16[1152,512]{1,0:T(8,128)(2,1)S(1)}, bf16[1152,512]{1,0:T(8,128)(2,1)S(1)}, u32[]{:S(2)}, u32[]{:S(2)}) collective-permute-start(bf16[1152,512]{1,0:T(8,128)(2,1)S(1)} %get-tuple-element.53), channel_id=1, source_target_pairs={{0,24},{8,0},{16,8},{24,16},{1,25},{9,1},{17,9},{25,17},{2,26},{10... | collective-permute-start | bytes 3538952 | tf_op jit(solution)/shard_map/ppermute | solution.py:20
  26.1 7.0 %collective-permute-done.4.refs_7_ = bf16[256,1024]{1,0:T(8,128)(2,1)S(1)} collective-permute-done((bf16[256,1024]{1,0:T(8,128)(2,1)S(1)}, bf16[256,1024]{1,0:T(8,128)(2,1)S(1)}, u32[]{:S(2)}, u32[]{:S(2)}) %collective-permute-start.4) | collective-permute-done | bytes 524320 | tf_op jit(solution)/shard_map/ppermute | solution.py:20
  33.1 2.7 %collective-permute-start.8 = (bf16[256,1024]{1,0:T(8,128)(2,1)S(1)}, bf16[256,1024]{1,0:T(8,128)(2,1)S(1)}, u32[]{:S(2)}, u32[]{:S(2)}) collective-permute-start(bf16[256,1024]{1,0:T(8,128)(2,1)S(1)} %collective-permute-done.7.refs_8_), channel_id=1, source_target_pairs={{0,7},{1,0},{2,1},{3,2},{4,3},{5,4},{6,5},{7,6},{8,15},{9,8},{10,9... | collective-permute-start | bytes 1572872 | tf_op jit(solution)/shard_map/ppermute | solution.py:20
  35.7 9.2 %collective-permute-done.5.refs_9_ = bf16[256,1024]{1,0:T(8,128)(2,1)S(1)} collective-permute-done((bf16[256,1024]{1,0:T(8,128)(2,1)S(1)}, bf16[256,1024]{1,0:T(8,128)(2,1)S(1)}, u32[]{:S(2)}, u32[]{:S(2)}) %collective-permute-start.5) | collective-permute-done | bytes 524320 | tf_op jit(solution)/shard_map/ppermute | solution.py:20
  45.1 2.7 %collective-permute-start.9 = (bf16[128,1024]{1,0:T(8,128)(2,1)S(1)}, bf16[128,1024]{1,0:T(8,128)(2,1)S(1)}, u32[]{:S(2)}, u32[]{:S(2)}) collective-permute-start(bf16[128,1024]{1,0:T(8,128)(2,1)S(1)} %slice.73), channel_id=1, source_target_pairs={{0,7},{1,0},{2,1},{3,2},{4,3},{5,4},{6,5},{7,6},{8,15},{9,8},{10,9... | collective-permute-start | bytes 786440 | tf_op jit(solution)/shard_map/ppermute | solution.py:20
  49.1 3.1 %collective-permute-done.10.refs_4_ = bf16[1152,512]{1,0:T(8,128)(2,1)S(1)} collective-permute-done((bf16[1152,512]{1,0:T(8,128)(2,1)S(1)}, bf16[1152,512]{1,0:T(8,128)(2,1)S(1)}, u32[]{:S(2)}, u32[]{:S(2)}) %collective-permute-start.10) | collective-permute-done | bytes 1179680 | tf_op jit(solution)/shard_map/ppermute | solution.py:20
  54.0 2.2 %collective-permute-start.14 = (f16[64,1024]{1,0:T(8,128)(2,1)S(1)}, f16[64,1024]{1,0:T(8,128)(2,1)S(1)}, u32[]{:S(2)}, u32[]{:S(2)}) collective-permute-start(f16[64,1024]{1,0:T(8,128)(2,1)S(1)} %convert_element_type.37), channel_id=1, source_target_pairs={{0,16},{8,24},{16,0},{24,8},{1,17},{9,25},{17,1},{25,9},{2,18},{10... | collective-permute-start | bytes 393224 | tf_op jit(solution)/shard_map/ppermute | solution.py:20
  56.8 2.1 %collective-permute-start.12 = (f16[64,1024]{1,0:T(8,128)(2,1)S(1)}, f16[64,1024]{1,0:T(8,128)(2,1)S(1)}, u32[]{:S(2)}, u32[]{:S(2)}) collective-permute-start(f16[64,1024]{1,0:T(8,128)(2,1)S(1)} %convert_element_type.33), channel_id=1, source_target_pairs={{0,24},{8,0},{16,8},{24,16},{1,25},{9,1},{17,9},{25,17},{2,26},{10... | collective-permute-start | bytes 393224 | tf_op jit(solution)/shard_map/ppermute | solution.py:20
  59.6 1.6 %collective-permute-done.13 = f16[64,1024]{1,0:T(8,128)(2,1)S(1)} collective-permute-done((f16[64,1024]{1,0:T(8,128)(2,1)S(1)}, f16[64,1024]{1,0:T(8,128)(2,1)S(1)}, u32[]{:S(2)}, u32[]{:S(2)}) %collective-permute-start.13) | collective-permute-done | bytes 131104 | tf_op jit(solution)/shard_map/ppermute | solution.py:20
  61.6 3.4 %collective-permute-start.18 = (f16[64,1152]{1,0:T(8,128)(2,1)S(1)}, f16[64,1152]{1,0:T(8,128)(2,1)S(1)}, u32[]{:S(2)}, u32[]{:S(2)}) collective-permute-start(f16[64,1152]{1,0:T(8,128)(2,1)S(1)} %get-tuple-element.63), channel_id=1, source_target_pairs={{0,6},{1,7},{2,0},{3,1},{4,2},{5,3},{6,4},{7,5},{8,14},{9,15},{10,... | collective-permute-start | bytes 442376 | tf_op jit(solution)/shard_map/ppermute | solution.py:20
  65.5 2.8 %collective-permute-start.20 = (bf16[512,512]{1,0:T(8,128)(2,1)S(1)}, bf16[512,512]{1,0:T(8,128)(2,1)S(1)}, u32[]{:S(2)}, u32[]{:S(2)}) collective-permute-start(bf16[512,512]{1,0:T(8,128)(2,1)S(1)} %slice.67), channel_id=1, source_target_pairs={{0,24},{8,0},{16,8},{24,16},{1,25},{9,1},{17,9},{25,17},{2,26},{10... | collective-permute-start | bytes 1572872 | tf_op jit(solution)/shard_map/ppermute | solution.py:20
  68.3 2.2 %collective-permute-start.16 = (f16[64,1152]{1,0:T(8,128)(2,1)S(1)}, f16[64,1152]{1,0:T(8,128)(2,1)S(1)}, u32[]{:S(2)}, u32[]{:S(2)}) collective-permute-start(f16[64,1152]{1,0:T(8,128)(2,1)S(1)} %get-tuple-element.63), channel_id=1, source_target_pairs={{0,7},{1,0},{2,1},{3,2},{4,3},{5,4},{6,5},{7,6},{8,15},{9,8},{10,9... | collective-permute-start | bytes 442376 | tf_op jit(solution)/shard_map/ppermute | solution.py:20
  70.6 3.6 %collective-permute-start.24 = (f16[32,1152]{1,0:T(8,128)(2,1)S(1)}, f16[32,1152]{1,0:T(8,128)(2,1)S(1)}, u32[]{:S(2)}, u32[]{:S(2)}) collective-permute-start(f16[32,1152]{1,0:T(8,128)(2,1)S(1)} %slice.77), channel_id=1, source_target_pairs={{0,6},{1,7},{2,0},{3,1},{4,2},{5,3},{6,4},{7,5},{8,14},{9,15},{10,... | collective-permute-start | bytes 221192 | tf_op jit(solution)/shard_map/ppermute | solution.py:20
  74.3 1.9 %collective-permute-start.21 = (f16[64,1152]{1,0:T(8,128)(2,1)S(1)}, f16[64,1152]{1,0:T(8,128)(2,1)S(1)}, u32[]{:S(2)}, u32[]{:S(2)}) collective-permute-start(f16[64,1152]{1,0:T(8,128)(2,1)S(1)} %collective-permute-done.17), channel_id=1, source_target_pairs={{0,1},{1,2},{2,3},{3,4},{4,5},{5,6},{6,7},{7,0},{8,9},{9,10},{10,1... | collective-permute-start | bytes 442376 | tf_op jit(solution)/shard_map/ppermute | solution.py:20
  77.9 3.8 %shard_map.58.refs_8_ = f32[5,2,128]{2,1,0:T(2,128)S(1)} custom-call(s32[3]{0:T(128)S(1)} %pad_add_fusion.where_ref.refs_0_, bf16[640,1024]{1,0:T(8,128)(2,1)S(1)} %pad_maximum_fusion.refs_1_, f32[320,128]{1,0:T(8,128)S(1)} %slice_convert_fusion.refs_2_, bf16[1024,512]{1,0:T(8,128)(2,1)S(1)} %bitcast.11, ...), custom_call_target="tpu_custom_call" | custom-call | flops 2684354560 | bytes 4194304 | tf_op jit(solution)/shard_map/pallas_call | solution.py:238
  82.6 2.7 %shard_map.59 = f32[8,8,2,128]{3,2,1,0:T(2,128)S(1)} custom-call(s32[3]{0:T(128)S(1)} %pad_add_fusion.where_ref.refs_0_, bf16[384,1024]{1,0:T(8,128)(2,1)S(1)} %pad_maximum_fusion.3.refs_1_, f32[192,128]{1,0:T(8,128)S(1)} %slice_convert_fusion.1.refs_2_, bf16[1024,512]{1,0:T(8,128)(2,1)S(1)} %bitcast.12, ...), custom_call_target="tpu_custom_call" | custom-call | flops 1610612736 | bytes 4194304 | tf_op jit(solution)/shard_map/pallas_call | solution.py:238
  85.3 24.7 %all_to_all.5 = f32[64,2,128]{2,1,0:T(2,128)S(1)} all-to-all(f32[64,2,128]{2,1,0:T(2,128)S(1)} %bitcast.17), channel_id=1, replica_groups=mesh['y'=4,'core'=2,'x'=4,'z'=8] {'y','core','z'}, dimensions={0} | all-to-all | bytes 131072 | tf_op jit(solution)/shard_map/all_to_all | solution.py:358
  (77 shorter events, 12.4 us)
Async XLA Ops:
  0.0 17.3 %collective-permute-start.3 = (bf16[256,1024]{1,0:T(8,128)(2,1)}, bf16[256,1024]{1,0:T(8,128)(2,1)S(1)}, u32[]{:S(2)}, u32[]{:S(2)}) collective-permute-start(bf16[256,1024]{1,0:T(8,128)(2,1)} %bitcast.13), channel_id=1, source_target_pairs={{0,7},{1,0},{2,1},{3,2},{4,3},{5,4},{6,5},{7,6},{8,15},{9,8},{10,9... | collective-permute-start | bytes 1572872 | tf_op jit(solution)/shard_map/ppermute | solution.py:20
  6.4 13.9 %collective-permute-start.2 = (bf16[256,1024]{1,0:T(8,128)(2,1)}, bf16[256,1024]{1,0:T(8,128)(2,1)S(1)}, u32[]{:S(2)}, u32[]{:S(2)}) collective-permute-start(bf16[256,1024]{1,0:T(8,128)(2,1)} %bitcast.14), channel_id=1, source_target_pairs={{0,1},{1,2},{2,3},{3,4},{4,5},{5,6},{6,7},{7,0},{8,9},{9,10},{10,1... | collective-permute-start | bytes 1572872 | tf_op jit(solution)/shard_map/ppermute | solution.py:20
  12.4 10.9 %collective-permute-start = (bf16[64,3072]{1,0:T(8,128)(2,1)S(1)}, bf16[64,3072]{1,0:T(8,128)(2,1)S(1)}, u32[]{:S(2)}, u32[]{:S(2)}) collective-permute-start(bf16[64,3072]{1,0:T(8,128)(2,1)S(1)} %get-tuple-element.28), channel_id=1, source_target_pairs={{0,8},{8,16},{16,24},{24,0},{1,9},{9,17},{17,25},{25,1},{2,10},{10... | collective-permute-start | bytes 1179656 | tf_op jit(solution)/shard_map/ppermute | solution.py:20
  13.7 9.7 %collective-permute-start.1 = (bf16[64,3072]{1,0:T(8,128)(2,1)S(1)}, bf16[64,3072]{1,0:T(8,128)(2,1)S(1)}, u32[]{:S(2)}, u32[]{:S(2)}) collective-permute-start(bf16[64,3072]{1,0:T(8,128)(2,1)S(1)} %get-tuple-element.29), channel_id=1, source_target_pairs={{0,24},{8,0},{16,8},{24,16},{1,25},{9,1},{17,9},{25,17},{2,26},{10... | collective-permute-start | bytes 1179656 | tf_op jit(solution)/shard_map/ppermute | solution.py:20
  20.3 12.8 %collective-permute-start.4 = (bf16[256,1024]{1,0:T(8,128)(2,1)S(1)}, bf16[256,1024]{1,0:T(8,128)(2,1)S(1)}, u32[]{:S(2)}, u32[]{:S(2)}) collective-permute-start(bf16[256,1024]{1,0:T(8,128)(2,1)S(1)} %collective-permute-done.2.refs_5_), channel_id=1, source_target_pairs={{0,1},{1,2},{2,3},{3,4},{4,5},{5,6},{6,7},{7,0},{8,9},{9,10},{10,1... | collective-permute-start | bytes 1572872 | tf_op jit(solution)/shard_map/ppermute | solution.py:20
  20.3 12.8 %collective-permute-start.7 = (bf16[256,1024]{1,0:T(8,128)(2,1)S(1)}, bf16[256,1024]{1,0:T(8,128)(2,1)S(1)}, u32[]{:S(2)}, u32[]{:S(2)}) collective-permute-start(bf16[256,1024]{1,0:T(8,128)(2,1)S(1)} %collective-permute-done.3.refs_6_), channel_id=1, source_target_pairs={{0,7},{1,0},{2,1},{3,2},{4,3},{5,4},{6,5},{7,6},{8,15},{9,8},{10,9... | collective-permute-start | bytes 1572872 | tf_op jit(solution)/shard_map/ppermute | solution.py:20
  23.6 25.6 %collective-permute-start.11 = (bf16[1152,512]{1,0:T(8,128)(2,1)S(1)}, bf16[1152,512]{1,0:T(8,128)(2,1)S(1)}, u32[]{:S(2)}, u32[]{:S(2)}) collective-permute-start(bf16[1152,512]{1,0:T(8,128)(2,1)S(1)} %get-tuple-element.53), channel_id=1, source_target_pairs={{0,24},{8,0},{16,8},{24,16},{1,25},{9,1},{17,9},{25,17},{2,26},{10... | collective-permute-start | bytes 3538952 | tf_op jit(solution)/shard_map/ppermute | solution.py:20
  26.0 26.2 %collective-permute-start.10 = (bf16[1152,512]{1,0:T(8,128)(2,1)S(1)}, bf16[1152,512]{1,0:T(8,128)(2,1)S(1)}, u32[]{:S(2)}, u32[]{:S(2)}) collective-permute-start(bf16[1152,512]{1,0:T(8,128)(2,1)S(1)} %get-tuple-element.54), channel_id=1, source_target_pairs={{0,8},{8,16},{16,24},{24,0},{1,9},{9,17},{17,25},{25,1},{2,10},{10... | collective-permute-start | bytes 3538952 | tf_op jit(solution)/shard_map/ppermute | solution.py:20
  33.1 11.8 %collective-permute-start.5 = (bf16[256,1024]{1,0:T(8,128)(2,1)S(1)}, bf16[256,1024]{1,0:T(8,128)(2,1)S(1)}, u32[]{:S(2)}, u32[]{:S(2)}) collective-permute-start(bf16[256,1024]{1,0:T(8,128)(2,1)S(1)} %collective-permute-done.4.refs_7_), channel_id=1, source_target_pairs={{0,1},{1,2},{2,3},{3,4},{4,5},{5,6},{6,7},{7,0},{8,9},{9,10},{10,1... | collective-permute-start | bytes 1572872 | tf_op jit(solution)/shard_map/ppermute | solution.py:20
  33.1 12.0 %collective-permute-start.8 = (bf16[256,1024]{1,0:T(8,128)(2,1)S(1)}, bf16[256,1024]{1,0:T(8,128)(2,1)S(1)}, u32[]{:S(2)}, u32[]{:S(2)}) collective-permute-start(bf16[256,1024]{1,0:T(8,128)(2,1)S(1)} %collective-permute-done.7.refs_8_), channel_id=1, source_target_pairs={{0,7},{1,0},{2,1},{3,2},{4,3},{5,4},{6,5},{7,6},{8,15},{9,8},{10,9... | collective-permute-start | bytes 1572872 | tf_op jit(solution)/shard_map/ppermute | solution.py:20
  44.9 7.4 %collective-permute-start.6 = (bf16[128,1024]{1,0:T(8,128)(2,1)S(1)}, bf16[128,1024]{1,0:T(8,128)(2,1)S(1)}, u32[]{:S(2)}, u32[]{:S(2)}) collective-permute-start(bf16[128,1024]{1,0:T(8,128)(2,1)S(1)} %slice.72), channel_id=1, source_target_pairs={{0,1},{1,2},{2,3},{3,4},{4,5},{5,6},{6,7},{7,0},{8,9},{9,10},{10,1... | collective-permute-start | bytes 786440 | tf_op jit(solution)/shard_map/ppermute | solution.py:20
  45.1 7.2 %collective-permute-start.9 = (bf16[128,1024]{1,0:T(8,128)(2,1)S(1)}, bf16[128,1024]{1,0:T(8,128)(2,1)S(1)}, u32[]{:S(2)}, u32[]{:S(2)}) collective-permute-start(bf16[128,1024]{1,0:T(8,128)(2,1)S(1)} %slice.73), channel_id=1, source_target_pairs={{0,7},{1,0},{2,1},{3,2},{4,3},{5,4},{6,5},{7,6},{8,15},{9,8},{10,9... | collective-permute-start | bytes 786440 | tf_op jit(solution)/shard_map/ppermute | solution.py:20
  54.0 5.6 %collective-permute-start.14 = (f16[64,1024]{1,0:T(8,128)(2,1)S(1)}, f16[64,1024]{1,0:T(8,128)(2,1)S(1)}, u32[]{:S(2)}, u32[]{:S(2)}) collective-permute-start(f16[64,1024]{1,0:T(8,128)(2,1)S(1)} %convert_element_type.37), channel_id=1, source_target_pairs={{0,16},{8,24},{16,0},{24,8},{1,17},{9,25},{17,1},{25,9},{2,18},{10... | collective-permute-start | bytes 393224 | tf_op jit(solution)/shard_map/ppermute | solution.py:20
  56.1 5.0 %collective-permute-start.13 = (f16[64,1024]{1,0:T(8,128)(2,1)S(1)}, f16[64,1024]{1,0:T(8,128)(2,1)S(1)}, u32[]{:S(2)}, u32[]{:S(2)}) collective-permute-start(f16[64,1024]{1,0:T(8,128)(2,1)S(1)} %convert_element_type.35), channel_id=1, source_target_pairs={{0,8},{8,16},{16,24},{24,0},{1,9},{9,17},{17,25},{25,1},{2,10},{10... | collective-permute-start | bytes 393224 | tf_op jit(solution)/shard_map/ppermute | solution.py:20
  61.3 7.0 %collective-permute-start.17 = (f16[64,1152]{1,0:T(8,128)(2,1)S(1)}, f16[64,1152]{1,0:T(8,128)(2,1)S(1)}, u32[]{:S(2)}, u32[]{:S(2)}) collective-permute-start(f16[64,1152]{1,0:T(8,128)(2,1)S(1)} %get-tuple-element.63), channel_id=1, source_target_pairs={{0,2},{1,3},{2,4},{3,5},{4,6},{5,7},{6,0},{7,1},{8,10},{9,11},{10,... | collective-permute-start | bytes 442376 | tf_op jit(solution)/shard_map/ppermute | solution.py:20
  61.6 8.9 %collective-permute-start.18 = (f16[64,1152]{1,0:T(8,128)(2,1)S(1)}, f16[64,1152]{1,0:T(8,128)(2,1)S(1)}, u32[]{:S(2)}, u32[]{:S(2)}) collective-permute-start(f16[64,1152]{1,0:T(8,128)(2,1)S(1)} %get-tuple-element.63), channel_id=1, source_target_pairs={{0,6},{1,7},{2,0},{3,1},{4,2},{5,3},{6,4},{7,5},{8,14},{9,15},{10,... | collective-permute-start | bytes 442376 | tf_op jit(solution)/shard_map/ppermute | solution.py:20
  65.0 5.7 %collective-permute-start.15 = (f16[64,1152]{1,0:T(8,128)(2,1)S(1)}, f16[64,1152]{1,0:T(8,128)(2,1)S(1)}, u32[]{:S(2)}, u32[]{:S(2)}) collective-permute-start(f16[64,1152]{1,0:T(8,128)(2,1)S(1)} %get-tuple-element.63), channel_id=1, source_target_pairs={{0,1},{1,2},{2,3},{3,4},{4,5},{5,6},{6,7},{7,0},{8,9},{9,10},{10,1... | collective-permute-start | bytes 442376 | tf_op jit(solution)/shard_map/ppermute | solution.py:20
  65.5 11.2 %collective-permute-start.20 = (bf16[512,512]{1,0:T(8,128)(2,1)S(1)}, bf16[512,512]{1,0:T(8,128)(2,1)S(1)}, u32[]{:S(2)}, u32[]{:S(2)}) collective-permute-start(bf16[512,512]{1,0:T(8,128)(2,1)S(1)} %slice.67), channel_id=1, source_target_pairs={{0,24},{8,0},{16,8},{24,16},{1,25},{9,1},{17,9},{25,17},{2,26},{10... | collective-permute-start | bytes 1572872 | tf_op jit(solution)/shard_map/ppermute | solution.py:20
  68.3 9.6 %collective-permute-start.19 = (bf16[512,512]{1,0:T(8,128)(2,1)S(1)}, bf16[512,512]{1,0:T(8,128)(2,1)S(1)}, u32[]{:S(2)}, u32[]{:S(2)}) collective-permute-start(bf16[512,512]{1,0:T(8,128)(2,1)S(1)} %slice.66), channel_id=1, source_target_pairs={{0,8},{8,16},{16,24},{24,0},{1,9},{9,17},{17,25},{25,1},{2,10},{10... | collective-permute-start | bytes 1572872 | tf_op jit(solution)/shard_map/ppermute | solution.py:20
  68.3 6.0 %collective-permute-start.16 = (f16[64,1152]{1,0:T(8,128)(2,1)S(1)}, f16[64,1152]{1,0:T(8,128)(2,1)S(1)}, u32[]{:S(2)}, u32[]{:S(2)}) collective-permute-start(f16[64,1152]{1,0:T(8,128)(2,1)S(1)} %get-tuple-element.63), channel_id=1, source_target_pairs={{0,7},{1,0},{2,1},{3,2},{4,3},{5,4},{6,5},{7,6},{8,15},{9,8},{10,9... | collective-permute-start | bytes 442376 | tf_op jit(solution)/shard_map/ppermute | solution.py:20
  70.5 11.2 %collective-permute-start.23 = (f16[32,1152]{1,0:T(8,128)(2,1)S(1)}, f16[32,1152]{1,0:T(8,128)(2,1)S(1)}, u32[]{:S(2)}, u32[]{:S(2)}) collective-permute-start(f16[32,1152]{1,0:T(8,128)(2,1)S(1)} %slice.76), channel_id=1, source_target_pairs={{0,2},{1,3},{2,4},{3,5},{4,6},{5,7},{6,0},{7,1},{8,10},{9,11},{10,... | collective-permute-start | bytes 221192 | tf_op jit(solution)/shard_map/ppermute | solution.py:20
  70.6 11.1 %collective-permute-start.24 = (f16[32,1152]{1,0:T(8,128)(2,1)S(1)}, f16[32,1152]{1,0:T(8,128)(2,1)S(1)}, u32[]{:S(2)}, u32[]{:S(2)}) collective-permute-start(f16[32,1152]{1,0:T(8,128)(2,1)S(1)} %slice.77), channel_id=1, source_target_pairs={{0,6},{1,7},{2,0},{3,1},{4,2},{5,3},{6,4},{7,5},{8,14},{9,15},{10,... | collective-permute-start | bytes 221192 | tf_op jit(solution)/shard_map/ppermute | solution.py:20
  74.3 7.4 %collective-permute-start.21 = (f16[64,1152]{1,0:T(8,128)(2,1)S(1)}, f16[64,1152]{1,0:T(8,128)(2,1)S(1)}, u32[]{:S(2)}, u32[]{:S(2)}) collective-permute-start(f16[64,1152]{1,0:T(8,128)(2,1)S(1)} %collective-permute-done.17), channel_id=1, source_target_pairs={{0,1},{1,2},{2,3},{3,4},{4,5},{5,6},{6,7},{7,0},{8,9},{9,10},{10,1... | collective-permute-start | bytes 442376 | tf_op jit(solution)/shard_map/ppermute | solution.py:20
  76.7 5.5 %collective-permute-start.22 = (f16[64,1152]{1,0:T(8,128)(2,1)S(1)}, f16[64,1152]{1,0:T(8,128)(2,1)S(1)}, u32[]{:S(2)}, u32[]{:S(2)}) collective-permute-start(f16[64,1152]{1,0:T(8,128)(2,1)S(1)} %collective-permute-done.18), channel_id=1, source_target_pairs={{0,7},{1,0},{2,1},{3,2},{4,3},{5,4},{6,5},{7,6},{8,15},{9,8},{10,9... | collective-permute-start | bytes 442376 | tf_op jit(solution)/shard_map/ppermute | solution.py:20
  (7 other events, 77.5 us)
